TPU v7x, 32 devices: a whole 2x2x4 slice. The times are simulated.
32 devices in a mesh: slab: 8 (over y, x, core), angle: 4 (over z).
Axes of the slice: x: 2, y: 2, z: 4, core: 2. Of those that a mesh axis runs over, the one named last changes fastest.
Arguments:
- projector: bfloat16 [4096, 128, 128], P(('slab', 'angle')), may hold values from 0 to 2, as said below
- block_vox: int32 [4096], P(('slab', 'angle')), may hold values from 0 to 63
- block_slot: int32 [4096], P(('slab', 'angle')), may hold values from 0 to 191, as said below
- send_ray: int32 [32, 192], P(('slab', 'angle')), may hold values from 0 to 31, as said below
- block_count: int32 [32], P(('slab', 'angle')), may hold values from 24 to 128, as said below
- prior: float32 [512, 128], P('slab'), may hold values from -6 to 6
- sinogram: float32 [1024, 128], P(('slab', 'angle')), may hold values from -12 to 12
Outputs:
- volume: float32 [512, 128], P('slab')
- residual: float32 [1024, 128], P(('slab', 'angle'))
Inputs may be any that keep to these rules, and one draw needn't show every extreme that they name: `block_slot`: entry k names a send slot o * 24 + j with j < 24, where o is the slab index that owns the rays of block k in the block's angle group. `send_ray`: within a row, the 24 entries of each owner's slots are distinct. Slots that no stored block names carry an arbitrary ray block. `block_count`: some device stores all 128 slots. `projector`: entries are nonnegative.
All inputs are finite; a program needn't handle non-finite values.
Results may differ from a plain program's by a relative error of at most 0.00076.
Values may be sent and summed in bfloat16 or wider, within the bound.
No kernel may reach another device: no remote copies, remote signals or barrier semaphores. Data moves between devices by JAX's collectives and lax.ppermute only.
A program may use at most 64 MiB of HBM per device.

v0:
```python
import jax
import jax.numpy as jnp
from jax import lax
from jax.sharding import PartitionSpec as P

ITERS = 2


def local(projector, block_vox, block_slot, send_ray, block_count, prior, sinogram):
    slabs = lax.axis_size("slab")
    slot_total = send_ray.shape[1]
    capacity = slot_total // slabs
    ray_dev = sinogram.shape[0]
    vox_dev = prior.shape[0]
    usable = (jnp.arange(projector.shape[0], dtype=jnp.int32) < block_count[0]).astype(jnp.float32)[
        :, None
    ]
    slot_rays = send_ray[0]
    owners = jnp.arange(slot_total, dtype=jnp.int32) // capacity
    block_rows = (owners * ray_dev + slot_rays)[block_slot]

    def to_owners(terms):
        spread = jax.ops.segment_sum(terms, block_rows, num_segments=slabs * ray_dev)
        return lax.psum_scatter(spread, "slab", scatter_dimension=0, tiled=True)

    def from_owners(values):
        gathered = lax.all_gather(values, "slab", axis=0, tiled=True)
        return gathered[block_rows]

    def over_angles(terms):
        return lax.psum(terms, "angle")

    row_terms = jnp.sum(projector, axis=2, dtype=jnp.float32) * usable
    col_terms = jax.ops.segment_sum(
        jnp.sum(projector, axis=1, dtype=jnp.float32) * usable, block_vox, num_segments=vox_dev
    )

    def forward_terms(current):
        inputs = current.astype(jnp.bfloat16)[block_vox]
        terms = jnp.einsum("kij,kj->ki", projector, inputs, preferred_element_type=jnp.float32)
        return terms * usable

    def backward_terms(weighted):
        picked = from_owners(weighted.astype(jnp.bfloat16))
        terms = jnp.einsum("kij,ki->kj", projector, picked, preferred_element_type=jnp.float32)
        return jax.ops.segment_sum(terms * usable, block_vox, num_segments=vox_dev)

    volume = prior
    residual = jnp.zeros(sinogram.shape, jnp.float32)
    for iteration in range(ITERS):
        if iteration == 0:
            row_weight = 1.0 / jnp.maximum(to_owners(row_terms), 1.0)
            col_weight = 1.0 / jnp.maximum(over_angles(col_terms), 1.0)
            residual = row_weight * (sinogram - to_owners(forward_terms(volume)))
            correction = over_angles(backward_terms(residual))
        else:
            residual = row_weight * (sinogram - to_owners(forward_terms(volume)))
            correction = over_angles(backward_terms(residual))
        volume = volume + col_weight * correction
    return (volume, residual)


def solution(mesh):
    return jax.shard_map(
        local,
        mesh=mesh,
        in_specs=(
            P(("slab", "angle"), None, None),
            P(("slab", "angle")),
            P(("slab", "angle")),
            P(("slab", "angle"), None),
            P(("slab", "angle")),
            P("slab", None),
            P(("slab", "angle"), None),
        ),
        out_specs=(P("slab", None), P(("slab", "angle"), None)),
        check_vma=False,
    )
```

profile of v0, /device:TPU:0, one launch (start us, length us, event | category | flops | bytes accessed | tf_op | source)
XLA Modules:
  0.0 224.8 jit_solution(1197387685587457171)
XLA Ops:
  7.9 0.7 compare_select_fusion.2
  8.5 0.7 compare_select_fusion.1
  9.2 0.7 fusion.34
  9.9 0.8 convert_element_type.25
  10.7 1.3 gather_fusion
  11.9 0.7 gather_fusion.1
  12.7 4.4 %fusion.6 = f32[128,1,128]{2,1,0:T(1,128)S(1)} fusion(bf16[128,128,128]{2,1,0:T(8,128)(2,1)} %param.7, bf16[128,128,1]{1,0,2:T(8,128)(2,1)S(1)} %bitcast.25), kind=kOutput, calls=%fused_computation.19 | convolution fusion | flops 4194304 | bytes 4292608 | tf_op jit(solution)/shard_map/kij,kj->ki/dot_general | solution.py:40
  17.1 1.7 scatter_custom_fusion.2
  18.9 3.4 %convert_reduce_fusion.1 = (f32[128,128]{1,0:T(8,128)S(1)}, f32[128,128]{1,0:T(8,128)S(1)}) fusion(bf16[128,128,128]{2,1,0:T(8,128)(2,1)} %param.7), kind=kLoop, calls=%fused_computation.12 | loop fusion | flops 6258688 | bytes 4325376 | tf_op jit(solution)/shard_map/reduce_sum | solution.py:35
  22.3 1.7 scatter_custom_fusion.1
  24.0 0.0 all-reduce.3.cloned.1.call-start
  24.1 1.8 scatter_custom_fusion
  25.9 29.2 %reduce-scatter.6.cloned.1.call-done = f32[32,128]{1,0:T(8,128)} async-done(((f32[256,128]{1,0:T(8,128)}), f32[32,128]{1,0:T(8,128)}) %reduce-scatter.6.cloned.1.call-update) | async-done | bytes 16400 | tf_op jit(solution)/shard_map/reduce_scatter | solution.py:24
  55.1 36.7 %reduce-scatter.4.cloned.1.call-done = f32[32,128]{1,0:T(8,128)} async-done(((f32[256,128]{1,0:T(8,128)}), f32[32,128]{1,0:T(8,128)}) %reduce-scatter.4.cloned.1.call-update) | async-done | bytes 16400 | tf_op jit(solution)/shard_map/reduce_scatter | solution.py:24
  91.8 0.7 multiply_convert_fusion
  92.5 9.2 %all_gather.6 = bf16[256,128]{1,0:T(8,128)(2,1)S(1)} all-gather(bf16[32,128]{1,0:T(8,128)(2,1)S(1)} %multiply_convert_fusion), channel_id=1, replica_groups=mesh['slab'=8,'angle'=4] {'slab'}, dimensions={0}, use_global_device_ids=true | all-gather | bytes 73728 | tf_op jit(solution)/shard_map/all_gather | solution.py:27
  101.7 0.7 gather_fusion.2
  102.4 3.4 %fusion.4 = f32[128,1,128]{2,1,0:T(1,128)S(1)} fusion(bf16[128,128,128]{2,1,0:T(8,128)(2,1)} %param.7, bf16[128,128,1]{1,0,2:T(8,128)(2,1)S(1)} %bitcast.26), kind=kOutput, calls=%fused_computation.17 | convolution fusion | flops 4194304 | bytes 4292608 | tf_op jit(solution)/shard_map/kij,ki->kj/dot_general | solution.py:45
  105.8 1.8 scatter_custom_fusion.3
  107.7 34.2 %all-reduce.3.cloned.1.call-done = (f32[64,128]{1,0:T(8,128)}, f32[64,128]{1,0:T(8,128)}) async-done(((f32[64,128]{1,0:T(8,128)}, f32[64,128]{1,0:T(8,128)}), (f32[64,128]{1,0:T(8,128)}, f32[64,128]{1,0:T(8,128)})) %all-reduce.3.cloned.1.call-update) | async-done | bytes 65552 | tf_op jit(solution)/shard_map/psum | solution.py:31
  141.8 0.8 fusion.32
  142.6 0.7 gather_fusion.3
  143.4 4.4 %fusion.2 = f32[128,1,128]{2,1,0:T(1,128)S(1)} fusion(bf16[128,128,128]{2,1,0:T(8,128)(2,1)} %param.7, bf16[128,128,1]{1,0,2:T(8,128)(2,1)S(1)} %bitcast.23), kind=kOutput, calls=%fused_computation.15 | convolution fusion | flops 4194304 | bytes 4292608 | tf_op jit(solution)/shard_map/kij,kj->ki/dot_general | solution.py:40
  147.8 1.7 scatter_custom_fusion.4
  149.5 33.2 %reduce-scatter.8.cloned.1.call-done = f32[32,128]{1,0:T(8,128)} async-done(((f32[256,128]{1,0:T(8,128)}), f32[32,128]{1,0:T(8,128)}) %reduce-scatter.8.cloned.1.call-update) | async-done | bytes 16400 | tf_op jit(solution)/shard_map/reduce_scatter | solution.py:24
  182.8 1.3 fusion.36
  184.1 9.2 %all_gather.7 = bf16[256,128]{1,0:T(8,128)(2,1)S(1)} all-gather(bf16[32,128]{1,0:T(8,128)(2,1)S(1)} %get-tuple-element.6), channel_id=1, replica_groups=mesh['slab'=8,'angle'=4] {'slab'}, dimensions={0}, use_global_device_ids=true | all-gather | bytes 73728 | tf_op jit(solution)/shard_map/all_gather | solution.py:27
  193.3 0.7 gather_fusion.4
  194.0 3.4 %fusion = f32[128,1,128]{2,1,0:T(1,128)S(1)} fusion(bf16[128,128,128]{2,1,0:T(8,128)(2,1)} %param.7, bf16[128,128,1]{1,0,2:T(8,128)(2,1)S(1)} %bitcast.24), kind=kOutput, calls=%fused_computation.13 | convolution fusion | flops 4194304 | bytes 4292608 | tf_op jit(solution)/shard_map/kij,ki->kj/dot_general | solution.py:45
  197.4 1.2 scatter_custom_fusion.5
  198.6 19.0 %psum.23 = f32[64,128]{1,0:T(8,128)S(1)} all-reduce(f32[64,128]{1,0:T(8,128)S(1)} %scatter_custom_fusion.5), channel_id=1, replica_groups=mesh['slab'=8,'angle'=4] {'angle'}, use_global_device_ids=true, to_apply=%region_13.14 | all-reduce | flops 8192 | bytes 65536 | tf_op jit(solution)/shard_map/psum | solution.py:31
  217.6 0.6 multiply_add_fusion
  (22 shorter events, 0.2 us)
Async XLA Ops:
  7.2 47.9 %reduce-scatter.6.cloned.1.call-start = ((), (), s32[]{:S(2)}) async-start(), calls=%async_computation.4 | async-start | bytes 147456 | tf_op jit(solution)/shard_map/reduce_scatter | solution.py:24
  12.6 79.1 %copy-start.3 = (f32[32,128]{1,0:T(8,128)S(1)}, f32[32,128]{1,0:T(8,128)}, u32[]{:S(2)}) copy-start(f32[32,128]{1,0:T(8,128)} %param.13) | copy-start | bytes 49156
  18.8 123.0 %copy-start = (f32[64,128]{1,0:T(8,128)S(1)}, f32[64,128]{1,0:T(8,128)}, u32[]{:S(2)}) copy-start(f32[64,128]{1,0:T(8,128)} %param.12) | copy-start | bytes 98308
  18.8 72.9 %reduce-scatter.4.cloned.1.call-start = ((), (), s32[]{:S(2)}) async-start(), calls=%async_computation.3 | async-start | bytes 147456 | tf_op jit(solution)/shard_map/reduce_scatter | solution.py:24
  24.0 117.8 %all-reduce.3.cloned.1.call-start = ((), (), s32[]{:S(2)}) async-start(), calls=%async_computation.6 | async-start | bytes 131072 | tf_op jit(solution)/shard_map/psum | solution.py:31
  102.4 80.4 %copy-start.4 = (f32[32,128]{1,0:T(8,128)S(1)}, f32[32,128]{1,0:T(8,128)}, u32[]{:S(2)}) copy-start(f32[32,128]{1,0:T(8,128)} %reduce-scatter.4.cloned.1.call-done) | copy-start | bytes 49156
  107.6 75.2 %reduce-scatter.8.cloned.1.call-start = ((), (), s32[]{:S(2)}) async-start(), calls=%async_computation.5 | async-start | bytes 147456 | tf_op jit(solution)/shard_map/reduce_scatter | solution.py:24
  143.3 74.2 %copy-start.1 = (f32[64,128]{1,0:T(8,128)S(1)}, f32[64,128]{1,0:T(8,128)}, u32[]{:S(2)}) copy-start(f32[64,128]{1,0:T(8,128)} %get-tuple-element.4) | copy-start | bytes 98308
  143.4 74.2 %copy-start.2 = (f32[64,128]{1,0:T(8,128)S(1)}, f32[64,128]{1,0:T(8,128)}, u32[]{:S(2)}) copy-start(f32[64,128]{1,0:T(8,128)} %get-tuple-element.5) | copy-start | bytes 98308
Sparse Core Ops, SparseCore 0:
  18.9 36.0 reduce-scatter.5
  58.4 33.3 reduce-scatter.3
  107.7 34.0 all-reduce.2
  149.7 33.0 reduce-scatter.7
where the time goes:
time: 225 us
  waiting for transfers between devices  133 us (59%)
  blocking collectives  37.3 us (17%)
  other arithmetic  19.6 us (9%)
  matrix products  15.6 us (7%)
  between operations  14.5 us (6%)
  local copies, waits for them, and re-layouts  4.13 us (2%)
    reduce_scatter x3, waiting for transfers between devices, to_owners(): return lax.psum_scatter(spread, 'slab', scatter_dimension=0, tiled=True)  99.1 us
    psum x1, waiting for transfers between devices, over_angles(): return lax.psum(terms, 'angle')  34.2 us
    psum x1, blocking collectives, over_angles(): return lax.psum(terms, 'angle')  19 us
    all_gather x2, blocking collectives, from_owners(): gathered = lax.all_gather(values, 'slab', axis=0, tiled=True)  18.4 us
    dot_general x2, matrix products, forward_terms(): jnp.einsum('kij,kj->ki', projector, inputs, preferred_element_type=jnp.fl...  8.88 us
    dot_general x2, matrix products, backward_terms(): jnp.einsum('kij,ki->kj', projector, picked, preferred_element_type=jnp.fl...  6.75 us
    scatter-add x3, other arithmetic, to_owners(): jax.ops.segment_sum(terms, block_rows, num_segments=slabs * ray_dev)  5.12 us
  transfers between devices with their start and end apart: 4, of which 4 were waited for; matrix products, arithmetic and copies ran while one was open for 3% of the time, Pallas kernels for 0%

commit v1 on v0

v1 whole, which is shorter than its diff:
```python
import jax
import jax.numpy as jnp
from jax import lax
from jax.experimental import pallas as pl
from jax.experimental.pallas import tpu as pltpu
from jax.sharding import PartitionSpec as P

ITERS = 2
F32 = jnp.float32
BF16 = jnp.bfloat16
BLK = 128
CHUNKS = 8


def whole(space=pltpu.VMEM):
    return pl.BlockSpec(memory_space=space)


def iota(shape, dim):
    return lax.broadcasted_iota(jnp.int32, shape, dim)


def split3(x):
    hi = x.astype(BF16)
    rest = x - hi.astype(F32)
    mid = rest.astype(BF16)
    low = (rest - mid.astype(F32)).astype(BF16)
    return hi, mid, low


def dot(a, b, dims=((1,), (0,))):
    return lax.dot_general(a, b, (dims, ((), ())), preferred_element_type=F32)


def one_hot_t(row, size):
    return jnp.where(iota((size, row.shape[1]), 0) == row, 1.0, 0.0)


def block_rows(slot_ref, ray_ref, count_ref, slabs, capacity, ray_dev):
    slot = slot_ref[...]
    slots = ray_ref.shape[1]
    picks = one_hot_t(slot, slots).astype(BF16)
    rays = jnp.broadcast_to(ray_ref[...], (16, slots)).astype(F32).astype(BF16)
    ray = dot(rays, picks)[0:1, :].astype(jnp.int32)
    owner = jnp.zeros_like(slot)
    for o in range(1, slabs):
        owner = owner + jnp.where(slot >= o * capacity, 1, 0)
    stored = iota(slot.shape, 1) < count_ref[0]
    return jnp.where(stored, owner * ray_dev + ray, -1)


def forward(proj, volume, vox, sums, before=None):
    blocks = proj.shape[0]
    half = blocks // 2
    picked = dot(volume.T.astype(BF16), one_hot_t(vox, volume.shape[0]).astype(BF16))
    lane = iota((BLK, blocks), 1)
    weights = jnp.concatenate([jnp.where(lane < half, picked, 0.0), jnp.where(lane >= half, picked, 0.0)], 0)
    if sums:
        ones = jnp.concatenate([jnp.where(lane < half, 1.0, 0.0), jnp.where(lane >= half, 1.0, 0.0)], 0)
        weights = jnp.concatenate([weights, ones], 1)
    weights = weights.astype(BF16)
    width = weights.shape[1]
    column = lax.rem(iota((BLK, width), 1), half)

    def step(p, acc):
        pair = jnp.concatenate([proj[p], proj[p + half]], 1)
        return jnp.where(column == p, dot(pair, weights), acc)

    acc = jnp.zeros((BLK, width), F32)
    per = half // CHUNKS
    for c in range(CHUNKS):
        if before is not None:
            before(c)
        for p in range(c * per, (c + 1) * per):
            acc = step(p, acc)
    return acc


def spread(rows, columns, total):
    spots = one_hot_t(rows, total).astype(BF16)
    out = None
    for term in split3(columns):
        part = dot(spots, term, ((1,), (1,)))
        out = part if out is None else out + part
    return out


def backward(proj, weighted, rows, vox, vox_dev, sums):
    blocks = proj.shape[0]
    spots = one_hot_t(rows, weighted.shape[0])
    picked = dot(spots.T.astype(BF16), weighted.astype(BF16)).astype(BF16)
    group = 16
    row = iota((group, BLK), 0)
    stored = jnp.where(rows >= 0, 1.0, 0.0)
    places = (one_hot_t(vox, vox_dev) * stored).astype(BF16)
    tops, lows = [], []
    for g in range(blocks // group):
        mine = picked[g * group:(g + 1) * group].astype(F32)
        left = [jnp.where(row == c, mine, 0.0) for c in range(group)]
        left = jnp.concatenate(left, 1)
        if sums:
            ones = jnp.concatenate([jnp.where(row == c, 1.0, 0.0) for c in range(group)], 1)
            left = jnp.concatenate([left, ones], 0)
        right = proj[g * group:(g + 1) * group].reshape(group * BLK, BLK)
        out = dot(left.astype(BF16), right)
        tops.append(out[:group])
        if sums:
            lows.append(out[group:])
    columns = jnp.concatenate(tops, 0)
    if sums:
        columns = jnp.concatenate([columns, jnp.concatenate(lows, 0)], 1)
    out = None
    for term in split3(columns):
        part = dot(places, term)
        out = part if out is None else out + part
    return out


def place_own(out_ref, sino_ref, ray_dev, start):
    me = lax.axis_index("slab")
    at = pl.ds(pl.multiple_of(start + me * ray_dev, 8), ray_dev)
    out_ref[at, :] = out_ref[at, :] + sino_ref[...]


def first_forward(slabs, capacity, ray_dev):
    def kernel(count, proj_hbm, vox, slot, ray, prior, sino, proj, rows_out, part, sems):
        blocks = proj_hbm.shape[0]
        half = blocks // 2
        per = half // CHUNKS
        copies = []
        for c in range(CHUNKS):
            for h in range(2):
                at = pl.ds(h * half + c * per, per)
                copy = pltpu.make_async_copy(proj_hbm.at[at], proj.at[at], sems.at[2 * c + h])
                copy.start()
                copies.append(copy)

        def before(c):
            copies[2 * c].wait()
            copies[2 * c + 1].wait()

        rows = block_rows(slot, ray, count, slabs, capacity, ray_dev)
        rows_out[...] = rows
        total = slabs * ray_dev
        columns = forward(proj, prior[...], vox[...], True, before)
        part[0:total, :] = -spread(rows, columns[:, :blocks], total)
        part[total:2 * total, :] = spread(rows, columns[:, blocks:], total)
        place_own(part, sino, ray_dev, 0)

    return kernel


def first_backward(ray_dev):
    def kernel(proj, rows, vox, own, other, weight, corr):
        total = own.shape[0] // 2
        sums = own[...] + other[...]
        weights = 1.0 / jnp.maximum(sums[total:], 1.0)
        weight[...] = weights
        both = backward(proj, weights * sums[:total], rows[...], vox[...], corr.shape[0] // 2, True)
        vox_dev = corr.shape[0] // 2
        corr[0:vox_dev, :] = both[:, :BLK]
        corr[vox_dev:2 * vox_dev, :] = both[:, BLK:]

    return kernel


def next_forward(ray_dev):
    def kernel(proj, rows, vox, volume, corr, sino, volume_out, weight_out, part):
        vox_dev = volume.shape[0]
        weights = 1.0 / jnp.maximum(corr[vox_dev:2 * vox_dev, :], 1.0)
        weight_out[...] = weights
        updated = volume[...] + weights * corr[0:vox_dev, :]
        volume_out[...] = updated
        columns = forward(proj, updated, vox[...], False)
        part[...] = -spread(rows[...], columns, part.shape[0])
        place_own(part, sino, ray_dev, 0)

    return kernel


def last_backward(ray_dev):
    def kernel(proj, rows, vox, own, other, weight, residual, corr):
        weighted = weight[...] * (own[...] + other[...])
        corr[...] = backward(proj, weighted, rows[...], vox[...], corr.shape[0], False)
        me = lax.axis_index("slab")
        residual[...] = weight[pl.ds(pl.multiple_of(me * ray_dev, 8), ray_dev), :] * (
            own[pl.ds(pl.multiple_of(me * ray_dev, 8), ray_dev), :]
            + other[pl.ds(pl.multiple_of(me * ray_dev, 8), ray_dev), :]
        )

    return kernel


def swap(x, axis, bit):
    size = lax.axis_size(axis)
    return lax.ppermute(x, axis, [(i, i ^ bit) for i in range(size)])


def over_slabs(x):
    slabs = lax.axis_size("slab")
    x, other = x, swap(x, "slab", 1)
    bits = [1 << b for b in range(1, slabs.bit_length() - 1)]
    while bits:
        x = x + other
        if len(bits) == 1:
            x, other, bits = x, swap(x, "slab", bits[0]), []
            continue
        first, second, bits = bits[0], bits[1], bits[2:]
        rows = x.shape[0] // 2
        core = lax.rem(lax.axis_index("slab"), 2)
        half = lax.dynamic_slice_in_dim(x, core * rows, rows)
        near = lax.ppermute(x, "slab", [(i, i ^ (second if i & 1 else first)) for i in range(slabs)])
        far = swap(half, "slab", first | second)
        got = lax.dynamic_update_slice_in_dim(
            near, lax.dynamic_slice_in_dim(near, core * rows, rows) + far, core * rows, 0
        )
        x, other = x + got, swap(got, "slab", 1)
    return x, other


def over_angles(x):
    slabs, angles = lax.axis_size("slab"), lax.axis_size("angle")
    bits = [1 << b for b in range(angles.bit_length() - 1)]
    core = lax.rem(lax.axis_index("slab"), 2)
    while bits:
        if len(bits) == 1:
            x, bits = x + swap(x, "angle", bits[0]), []
            continue
        first, second, bits = bits[0], bits[1], bits[2:]
        other = swap(x, "slab", 1)
        both = jnp.stack([jnp.where(core == 0, x, other), jnp.where(core == 0, other, x)])
        pairs = [
            (s * angles + g, s * angles + (g ^ (second if s & 1 else first)))
            for s in range(slabs)
            for g in range(angles)
        ]
        near = lax.ppermute(both, ("slab", "angle"), pairs)
        far = swap(x, "angle", first | second)
        mine = lax.dynamic_index_in_dim(near, core, 0, keepdims=False)
        theirs = swap(lax.dynamic_index_in_dim(near, 1 - core, 0, keepdims=False), "slab", 1)
        by_first = jnp.where(core == 0, mine, theirs)
        by_second = jnp.where(core == 0, theirs, mine)
        x = (x + by_first) + (by_second + far)
    return x


def local(projector, block_vox, block_slot, send_ray, block_count, prior, sinogram):
    slabs = lax.axis_size("slab")
    capacity = send_ray.shape[1] // slabs
    ray_dev = sinogram.shape[0]
    vox_dev = prior.shape[0]
    blocks = projector.shape[0]
    total = slabs * ray_dev
    params = pltpu.CompilerParams(vmem_limit_bytes=40 * 1024 * 1024)
    vmem = lambda rows, dtype=F32: pltpu.VMEM((rows, BLK), dtype)
    vox = block_vox.reshape(1, blocks)
    slot = block_slot.reshape(1, blocks)

    proj, rows, part = pl.pallas_call(
        first_forward(slabs, capacity, ray_dev),
        out_shape=(
            pltpu.VMEM(projector.shape, BF16),
            pltpu.VMEM((1, blocks), jnp.int32),
            vmem(2 * total),
        ),
        in_specs=[whole(pltpu.SMEM), whole(pl.ANY)] + [whole()] * 5,
        out_specs=(whole(), whole(), whole()),
        scratch_shapes=[pltpu.SemaphoreType.DMA((2 * CHUNKS,))],
        compiler_params=params,
        name="first_forward",
    )(block_count, projector, vox, slot, send_ray, prior, sinogram)
    own, other = over_slabs(part)

    row_weight, corr = pl.pallas_call(
        first_backward(ray_dev),
        out_shape=(vmem(total), vmem(2 * vox_dev)),
        in_specs=[whole()] * 5,
        out_specs=(whole(), whole()),
        compiler_params=params,
        name="first_backward",
    )(proj, rows, vox, own, other)
    corr = over_angles(corr)

    volume, col_weight, part = pl.pallas_call(
        next_forward(ray_dev),
        out_shape=(vmem(vox_dev), vmem(vox_dev), vmem(total)),
        in_specs=[whole()] * 6,
        out_specs=(whole(),) * 3,
        compiler_params=params,
        name="next_forward",
    )(proj, rows, vox, prior, corr, sinogram)
    own, other = over_slabs(part)

    residual, corr = pl.pallas_call(
        last_backward(ray_dev),
        out_shape=(jax.ShapeDtypeStruct((ray_dev, BLK), F32), vmem(vox_dev)),
        in_specs=[whole()] * 6,
        out_specs=(whole(), whole()),
        compiler_params=params,
        name="last_backward",
    )(proj, rows, vox, own, other, row_weight)
    corr = over_angles(corr)
    return volume + col_weight * corr, residual


def solution(mesh):
    return jax.shard_map(
        local,
        mesh=mesh,
        in_specs=(
            P(("slab", "angle"), None, None),
            P(("slab", "angle")),
            P(("slab", "angle")),
            P(("slab", "angle"), None),
            P(("slab", "angle")),
            P("slab", None),
            P(("slab", "angle"), None),
        ),
        out_specs=(P("slab", None), P(("slab", "angle"), None)),
        check_vma=False,
    )
```

time: 225 us -> 67.8 us (0.30)
  waiting for transfers between devices: 133 us -> 27.2 us
  blocking collectives: 37.3 us -> 0 us
  other arithmetic: 19.6 us -> 0.83 us
  starting transfers between devices: 0.16 us -> 16.1 us
  matrix products: 15.6 us -> 0 us
  between operations: 14.5 us -> 1.47 us
  local copies, waits for them, and re-layouts: 4.13 us -> 14.2 us
  Pallas kernels: 0 us -> 7.66 us
    reduce_scatter x3 -> x0, waiting for transfers between devices: 99.1 us -> none  [to_owners(): return lax.psum_scatter(spread, 'slab', scatter_dimension=0, tiled=True)]
    psum x1 -> x0, waiting for transfers between devices: 34.2 us -> none  [over_angles(): return lax.psum(terms, 'angle')]
    ppermute x0 -> x16, waiting for transfers between devices: none -> 27.2 us  [the longest x12 24 us: swap(): return lax.ppermute(x, axis, [(i, i ^ bit) for i in range(size)])]
    psum x1 -> x0, blocking collectives: 19 us -> none  [over_angles(): return lax.psum(terms, 'angle')]
    all_gather x2 -> x0, blocking collectives: 18.4 us -> none  [from_owners(): gathered = lax.all_gather(values, 'slab', axis=0, tiled=True)]
    ppermute x0 -> x16, starting transfers between devices: none -> 16.1 us  [the longest x12 8.51 us: swap(): return lax.ppermute(x, axis, [(i, i ^ bit) for i in range(size)])]
    dot_general x4 -> x0, matrix products: 15.6 us -> none  [the longest x2 8.88 us: forward_terms(): jnp.einsum('kij,kj->ki', projector, inputs, preferred_element_type=jnp.fl...]
    unnamed x10 -> x26, local copies, waits for them, and re-layouts: 0.02 us -> 14.2 us
  transfers between devices with their start and end apart: 4 -> 16, of which waited for: 4 -> 12; matrix products, arithmetic and copies ran while one was open for 3% -> 0% of each run, Pallas kernels for 0% -> 0%
where the time goes in v1:
time: 67.8 us; the launch traced here: 67.4 us
  waiting for transfers between devices  27.2 us (40%)
  starting transfers between devices  16.1 us (24%)
  local copies, waits for them, and re-layouts  14.2 us (21%)
  Pallas kernels  7.66 us (11%)
  between operations  1.47 us (2%)
  other arithmetic  0.83 us (1%)
    ppermute x12, waiting for transfers between devices, swap(): return lax.ppermute(x, axis, [(i, i ^ bit) for i in range(size)])  24 us
    unnamed x26, local copies, waits for them, and re-layouts  14.2 us
    ppermute x12, starting transfers between devices, swap(): return lax.ppermute(x, axis, [(i, i ^ bit) for i in range(size)])  8.51 us
    ppermute x2, starting transfers between devices, over_slabs(): lax.ppermute(x, 'slab', [(i, i ^ (second if i & 1 else first)) for i in r...  4.51 us
    pallas_call x1, Pallas kernels, local(): pl.pallas_call(first_forward(slabs, capacity, ray_dev), out_shape=(pltpu....  3.4 us
    ppermute x2, waiting for transfers between devices, over_angles(): near = lax.ppermute(both, ('slab', 'angle'), pairs)  3.16 us
    ppermute x2, starting transfers between devices, over_angles(): near = lax.ppermute(both, ('slab', 'angle'), pairs)  3.04 us
    pallas_call x1, Pallas kernels, local(): pl.pallas_call(next_forward(ray_dev), out_shape=(vmem(vox_dev), vmem(vox_...  1.7 us
  transfers between devices with their start and end apart: 16, of which 12 were waited for; matrix products, arithmetic and copies ran while one was open for 0% of the time, Pallas kernels for 0%

profile of v1, /device:TPU:0, one launch (start us, length us, event | category | flops | bytes accessed | tf_op | source)
XLA Modules:
  0.0 67.4 jit_solution(5387255884335832504)
XLA Ops:
  1.3 2.2 %copy-done.4 = bf16[128,128,128]{2,1,0:T(8,128)(2,1)S(1)} copy-done((bf16[128,128,128]{2,1,0:T(8,128)(2,1)S(1)}, bf16[128,128,128]{2,1,0:T(8,128)(2,1)}, u32[]{:S(2)}) %copy-start.4) | copy-done | bytes 4194328
  3.5 0.8 %copy-done.5 = f32[64,128]{1,0:T(8,128)S(1)} copy-done((f32[64,128]{1,0:T(8,128)S(1)}, f32[64,128]{1,0:T(8,128)}, u32[]{:S(2)}) %copy-start.5) | copy-done | bytes 32792
  4.2 0.7 %copy-done.7 = f32[32,128]{1,0:T(8,128)S(1)} copy-done((f32[32,128]{1,0:T(8,128)S(1)}, f32[32,128]{1,0:T(8,128)}, u32[]{:S(2)}) %copy-start.7) | copy-done | bytes 16408
  5.0 0.7 copy-done.9
  5.6 0.7 %copy-done.11 = s32[1,192]{1,0:T(1,128)S(1)} copy-done((s32[1,192]{1,0:T(1,128)S(1)}, s32[1,192]{1,0:T(1,128)}, u32[]{:S(2)}) %copy-start.11) | copy-done | bytes 792
  7.0 3.4 %first_forward.1 = (bf16[128,128,128]{2,1,0:T(8,128)(2,1)S(1)}, s32[1,128]{1,0:T(1,128)S(1)}, f32[512,128]{1,0:T(8,128)S(1)}) custom-call(s32[1]{0:T(128)S(6)} %copy.11.count, bf16[128,128,128]{2,1,0:T(8,128)(2,1)S(1)} %copy-done.4, s32[1,128]{1,0:T(1,128)S(1)} %bitcast.40, s32[1,128]{1,0:T(1,128)S(1)} %bitcast.44, s32[1,192]{1,0:T(1,128)S(1)} %copy-done.11, ...), custom_call_target="tpu_custom_call" | custom-call | tf_op jit(solution)/shard_map/first_forward/pallas_call | solution.py:259
  10.4 1.9 %copy-done = bf16[128,128,128]{2,1,0:T(8,128)(2,1)} copy-done((bf16[128,128,128]{2,1,0:T(8,128)(2,1)}, bf16[128,128,128]{2,1,0:T(8,128)(2,1)S(1)}, u32[]{:S(2)}) %copy-start) | copy-done | bytes 4194328
  12.8 1.2 %collective-permute-done = f32[512,128]{1,0:T(8,128)S(1)} collective-permute-done((f32[512,128]{1,0:T(8,128)S(1)}, f32[512,128]{1,0:T(8,128)S(1)}, u32[]{:S(2)}, u32[]{:S(2)}) %collective-permute-start) | collective-permute-done | bytes 262176 | tf_op jit(solution)/shard_map/ppermute | solution.py:196
  14.0 2.9 %collective-permute-start.1 = (f32[512,128]{1,0:T(8,128)S(1)}, f32[512,128]{1,0:T(8,128)S(1)}, u32[]{:S(2)}, u32[]{:S(2)}) collective-permute-start(f32[512,128]{1,0:T(8,128)S(1)} %add.60), channel_id=1, source_target_pairs={{0,8},{4,20},{8,0},{12,28},{16,24},{20,4},{24,16},{28,12},{1,9},{5... | collective-permute-start | bytes 786440 | tf_op jit(solution)/shard_map/ppermute | solution.py:212
  16.9 1.5 %collective-permute-start.2 = (f32[256,128]{1,0:T(8,128)S(1)}, f32[256,128]{1,0:T(8,128)S(1)}, u32[]{:S(2)}, u32[]{:S(2)}) collective-permute-start(f32[256,128]{1,0:T(8,128)S(1)} %constant_dynamic-slice_fusion.1), channel_id=1, source_target_pairs={{0,24},{4,28},{8,16},{12,20},{16,8},{20,12},{24,0},{28,4},{1,25},{... | collective-permute-start | bytes 393224 | tf_op jit(solution)/shard_map/ppermute | solution.py:196
  18.5 7.1 %collective-permute-done.2 = f32[256,128]{1,0:T(8,128)S(1)} collective-permute-done((f32[256,128]{1,0:T(8,128)S(1)}, f32[256,128]{1,0:T(8,128)S(1)}, u32[]{:S(2)}, u32[]{:S(2)}) %collective-permute-start.2) | collective-permute-done | bytes 131104 | tf_op jit(solution)/shard_map/ppermute | solution.py:196
  25.7 1.5 %collective-permute-done.3.other = f32[512,128]{1,0:T(8,128)S(1)} collective-permute-done((f32[512,128]{1,0:T(8,128)S(1)}, f32[512,128]{1,0:T(8,128)S(1)}, u32[]{:S(2)}, u32[]{:S(2)}) %collective-permute-start.3) | collective-permute-done | bytes 262176 | tf_op jit(solution)/shard_map/ppermute | solution.py:196
  27.2 2.2 %copy-done.1 = bf16[128,128,128]{2,1,0:T(8,128)(2,1)S(1)} copy-done((bf16[128,128,128]{2,1,0:T(8,128)(2,1)S(1)}, bf16[128,128,128]{2,1,0:T(8,128)(2,1)}, u32[]{:S(2)}) %copy-start.1) | copy-done | bytes 4194328
  29.4 1.0 %first_backward.1 = (f32[256,128]{1,0:T(8,128)S(1)}, f32[128,128]{1,0:T(8,128)S(1)}) custom-call(bf16[128,128,128]{2,1,0:T(8,128)(2,1)S(1)} %copy-done.1, s32[1,128]{1,0:T(1,128)S(1)} %get-tuple-element.13.rows, s32[1,128]{1,0:T(1,128)S(1)} %bitcast.41, f32[512,128]{1,0:T(8,128)S(1)} %add.63.own, f32[512,128]{1,0:T(8,128)S(1)} %collective-permute-done.3.other), custom_call_target="tpu_custom_call" | custom-call | tf_op jit(solution)/shard_map/first_backward/pallas_call | solution.py:274
  30.6 1.1 %collective-permute-done.4 = f32[128,128]{1,0:T(8,128)S(1)} collective-permute-done((f32[128,128]{1,0:T(8,128)S(1)}, f32[128,128]{1,0:T(8,128)S(1)}, u32[]{:S(2)}, u32[]{:S(2)}) %collective-permute-start.4) | collective-permute-done | bytes 65568 | tf_op jit(solution)/shard_map/ppermute | solution.py:196
  31.8 1.6 %collective-permute-start.5 = (f32[2,128,128]{2,1,0:T(8,128)S(1)}, f32[2,128,128]{2,1,0:T(8,128)S(1)}, u32[]{:S(2)}, u32[]{:S(2)}) collective-permute-start(f32[2,128,128]{2,1,0:T(8,128)S(1)} %pad_maximum_fusion), channel_id=1, source_target_pairs={{0,1},{1,0},{2,3},{3,2},{4,6},{5,7},{6,4},{7,5},{8,9},{9,8},{10,11... | collective-permute-start | bytes 393224 | tf_op jit(solution)/shard_map/ppermute | solution.py:237
  33.4 2.5 %collective-permute-start.7 = (f32[128,128]{1,0:T(8,128)S(1)}, f32[128,128]{1,0:T(8,128)S(1)}, u32[]{:S(2)}, u32[]{:S(2)}) collective-permute-start(f32[128,128]{1,0:T(8,128)S(1)} %get-tuple-element.15), channel_id=1, source_target_pairs={{0,3},{1,2},{2,1},{3,0},{4,7},{5,6},{6,5},{7,4},{8,11},{9,10},{10,... | collective-permute-start | bytes 196616 | tf_op jit(solution)/shard_map/ppermute | solution.py:196
  35.9 2.1 %collective-permute-done.5 = f32[2,128,128]{2,1,0:T(8,128)S(1)} collective-permute-done((f32[2,128,128]{2,1,0:T(8,128)S(1)}, f32[2,128,128]{2,1,0:T(8,128)S(1)}, u32[]{:S(2)}, u32[]{:S(2)}) %collective-permute-start.5) | collective-permute-done | bytes 131104 | tf_op jit(solution)/shard_map/ppermute | solution.py:237
  38.4 2.3 %collective-permute-done.7 = f32[128,128]{1,0:T(8,128)S(1)} collective-permute-done((f32[128,128]{1,0:T(8,128)S(1)}, f32[128,128]{1,0:T(8,128)S(1)}, u32[]{:S(2)}, u32[]{:S(2)}) %collective-permute-start.7) | collective-permute-done | bytes 65568 | tf_op jit(solution)/shard_map/ppermute | solution.py:196
  40.8 2.2 %copy-done.2 = bf16[128,128,128]{2,1,0:T(8,128)(2,1)S(1)} copy-done((bf16[128,128,128]{2,1,0:T(8,128)(2,1)S(1)}, bf16[128,128,128]{2,1,0:T(8,128)(2,1)}, u32[]{:S(2)}) %copy-start.2) | copy-done | bytes 4194328
  43.0 1.7 %next_forward.1 = (f32[64,128]{1,0:T(8,128)S(1)}, f32[64,128]{1,0:T(8,128)S(1)}, f32[256,128]{1,0:T(8,128)S(1)}) custom-call(bf16[128,128,128]{2,1,0:T(8,128)(2,1)S(1)} %copy-done.2, s32[1,128]{1,0:T(1,128)S(1)} %get-tuple-element.13.rows, s32[1,128]{1,0:T(1,128)S(1)} %bitcast.42, f32[64,128]{1,0:T(8,128)S(1)} %copy-done.6, f32[128,128]{1,0:T(8,128)S(1)} %fusion.1.corr, ...), custom_call_target="tpu_custom_call" | custom-call | tf_op jit(solution)/shard_map/next_forward/pallas_call | solution.py:284
  44.8 1.3 %collective-permute-done.8 = f32[256,128]{1,0:T(8,128)S(1)} collective-permute-done((f32[256,128]{1,0:T(8,128)S(1)}, f32[256,128]{1,0:T(8,128)S(1)}, u32[]{:S(2)}, u32[]{:S(2)}) %collective-permute-start.8) | collective-permute-done | bytes 131104 | tf_op jit(solution)/shard_map/ppermute | solution.py:196
  46.1 1.6 %collective-permute-start.9 = (f32[256,128]{1,0:T(8,128)S(1)}, f32[256,128]{1,0:T(8,128)S(1)}, u32[]{:S(2)}, u32[]{:S(2)}) collective-permute-start(f32[256,128]{1,0:T(8,128)S(1)} %add.69), channel_id=1, source_target_pairs={{0,8},{4,20},{8,0},{12,28},{16,24},{20,4},{24,16},{28,12},{1,9},{5... | collective-permute-start | bytes 393224 | tf_op jit(solution)/shard_map/ppermute | solution.py:212
  48.2 4.7 %collective-permute-done.10 = f32[128,128]{1,0:T(8,128)S(1)} collective-permute-done((f32[128,128]{1,0:T(8,128)S(1)}, f32[128,128]{1,0:T(8,128)S(1)}, u32[]{:S(2)}, u32[]{:S(2)}) %collective-permute-start.10) | collective-permute-done | bytes 65568 | tf_op jit(solution)/shard_map/ppermute | solution.py:196
  53.0 1.3 %collective-permute-done.11.other = f32[256,128]{1,0:T(8,128)S(1)} collective-permute-done((f32[256,128]{1,0:T(8,128)S(1)}, f32[256,128]{1,0:T(8,128)S(1)}, u32[]{:S(2)}, u32[]{:S(2)}) %collective-permute-start.11) | collective-permute-done | bytes 131104 | tf_op jit(solution)/shard_map/ppermute | solution.py:196
  54.3 2.2 %copy-done.3 = bf16[128,128,128]{2,1,0:T(8,128)(2,1)S(1)} copy-done((bf16[128,128,128]{2,1,0:T(8,128)(2,1)S(1)}, bf16[128,128,128]{2,1,0:T(8,128)(2,1)}, u32[]{:S(2)}) %copy-start.3) | copy-done | bytes 4194328
  56.5 1.5 %last_backward.1 = (f32[32,128]{1,0:T(8,128)}, f32[64,128]{1,0:T(8,128)S(1)}) custom-call(bf16[128,128,128]{2,1,0:T(8,128)(2,1)S(1)} %copy-done.3, s32[1,128]{1,0:T(1,128)S(1)} %get-tuple-element.13.rows, s32[1,128]{1,0:T(1,128)S(1)} %bitcast.43, f32[256,128]{1,0:T(8,128)S(1)} %add.72.own, f32[256,128]{1,0:T(8,128)S(1)} %collective-permute-done.11.other, ...), custom_call_target="tpu_custom_call" | custom-call | tf_op jit(solution)/shard_map/last_backward/pallas_call | solution.py:294
  58.2 1.1 %collective-permute-done.12 = f32[64,128]{1,0:T(8,128)S(1)} collective-permute-done((f32[64,128]{1,0:T(8,128)S(1)}, f32[64,128]{1,0:T(8,128)S(1)}, u32[]{:S(2)}, u32[]{:S(2)}) %collective-permute-start.12) | collective-permute-done | bytes 32800 | tf_op jit(solution)/shard_map/ppermute | solution.py:196
  59.3 1.4 %collective-permute-start.13 = (f32[2,64,128]{2,1,0:T(8,128)S(1)}, f32[2,64,128]{2,1,0:T(8,128)S(1)}, u32[]{:S(2)}, u32[]{:S(2)}) collective-permute-start(f32[2,64,128]{2,1,0:T(8,128)S(1)} %pad_maximum_fusion.1), channel_id=1, source_target_pairs={{0,1},{1,0},{2,3},{3,2},{4,6},{5,7},{6,4},{7,5},{8,9},{9,8},{10,11... | collective-permute-start | bytes 196616 | tf_op jit(solution)/shard_map/ppermute | solution.py:237
  60.7 2.6 %collective-permute-start.15 = (f32[64,128]{1,0:T(8,128)S(1)}, f32[64,128]{1,0:T(8,128)S(1)}, u32[]{:S(2)}, u32[]{:S(2)}) collective-permute-start(f32[64,128]{1,0:T(8,128)S(1)} %get-tuple-element.20), channel_id=1, source_target_pairs={{0,3},{1,2},{2,1},{3,0},{4,7},{5,6},{6,5},{7,4},{8,11},{9,10},{10,... | collective-permute-start | bytes 98312 | tf_op jit(solution)/shard_map/ppermute | solution.py:196
  63.3 1.0 %collective-permute-done.13 = f32[2,64,128]{2,1,0:T(8,128)S(1)} collective-permute-done((f32[2,64,128]{2,1,0:T(8,128)S(1)}, f32[2,64,128]{2,1,0:T(8,128)S(1)}, u32[]{:S(2)}, u32[]{:S(2)}) %collective-permute-start.13) | collective-permute-done | bytes 65568 | tf_op jit(solution)/shard_map/ppermute | solution.py:237
  64.3 2.4 %collective-permute-done.15 = f32[64,128]{1,0:T(8,128)S(1)} collective-permute-done((f32[64,128]{1,0:T(8,128)S(1)}, f32[64,128]{1,0:T(8,128)S(1)}, u32[]{:S(2)}, u32[]{:S(2)}) %collective-permute-start.15) | collective-permute-done | bytes 32800 | tf_op jit(solution)/shard_map/ppermute | solution.py:196
  (46 shorter events, 3.5 us)
Async XLA Ops:
  0.6 26.5 %copy-start.10 = (s32[128]{0:T(128)S(1)}, s32[128]{0:T(128)}, u32[]{:S(2)}) copy-start(s32[128]{0:T(128)} %param.8) | copy-start | bytes 1540
  1.3 2.2 %copy-start.4 = (bf16[128,128,128]{2,1,0:T(8,128)(2,1)S(1)}, bf16[128,128,128]{2,1,0:T(8,128)(2,1)}, u32[]{:S(2)}) copy-start(bf16[128,128,128]{2,1,0:T(8,128)(2,1)} %proj_hbm.1) | copy-start | bytes 12582916
  3.5 0.8 %copy-start.5 = (f32[64,128]{1,0:T(8,128)S(1)}, f32[64,128]{1,0:T(8,128)}, u32[]{:S(2)}) copy-start(f32[64,128]{1,0:T(8,128)} %volume.1) | copy-start | bytes 98308
  4.2 0.7 %copy-start.7 = (f32[32,128]{1,0:T(8,128)S(1)}, f32[32,128]{1,0:T(8,128)}, u32[]{:S(2)}) copy-start(f32[32,128]{1,0:T(8,128)} %sino.3) | copy-start | bytes 49156
  5.0 0.7 copy-start.9
  5.6 0.7 %copy-start.11 = (s32[1,192]{1,0:T(1,128)S(1)}, s32[1,192]{1,0:T(1,128)}, u32[]{:S(2)}) copy-start(s32[1,192]{1,0:T(1,128)} %ray.1) | copy-start | bytes 2308
  6.3 0.7 copy-start.12
  10.4 2.0 %copy-start = (bf16[128,128,128]{2,1,0:T(8,128)(2,1)}, bf16[128,128,128]{2,1,0:T(8,128)(2,1)S(1)}, u32[]{:S(2)}) copy-start(bf16[128,128,128]{2,1,0:T(8,128)(2,1)S(1)} %get-tuple-element.12.proj) | copy-start | bytes 12582916
  12.3 28.5 %copy-start.6 = (f32[64,128]{1,0:T(8,128)S(1)}, f32[64,128]{1,0:T(8,128)}, u32[]{:S(2)}) copy-start(f32[64,128]{1,0:T(8,128)} %volume.1) | copy-start | bytes 98308
  12.3 28.5 %copy-start.8 = (f32[32,128]{1,0:T(8,128)S(1)}, f32[32,128]{1,0:T(8,128)}, u32[]{:S(2)}) copy-start(f32[32,128]{1,0:T(8,128)} %sino.3) | copy-start | bytes 49156
  12.3 1.6 %collective-permute-start = (f32[512,128]{1,0:T(8,128)S(1)}, f32[512,128]{1,0:T(8,128)S(1)}, u32[]{:S(2)}, u32[]{:S(2)}) collective-permute-start(f32[512,128]{1,0:T(8,128)S(1)} %get-tuple-element.14), channel_id=1, source_target_pairs={{0,4},{4,0},{8,12},{12,8},{16,20},{20,16},{24,28},{28,24},{1,5},{5... | collective-permute-start | bytes 786440 | tf_op jit(solution)/shard_map/ppermute | solution.py:196
  14.0 11.6 %collective-permute-start.1 = (f32[512,128]{1,0:T(8,128)S(1)}, f32[512,128]{1,0:T(8,128)S(1)}, u32[]{:S(2)}, u32[]{:S(2)}) collective-permute-start(f32[512,128]{1,0:T(8,128)S(1)} %add.60), channel_id=1, source_target_pairs={{0,8},{4,20},{8,0},{12,28},{16,24},{20,4},{24,16},{28,12},{1,9},{5... | collective-permute-start | bytes 786440 | tf_op jit(solution)/shard_map/ppermute | solution.py:212
  16.9 8.6 %collective-permute-start.2 = (f32[256,128]{1,0:T(8,128)S(1)}, f32[256,128]{1,0:T(8,128)S(1)}, u32[]{:S(2)}, u32[]{:S(2)}) collective-permute-start(f32[256,128]{1,0:T(8,128)S(1)} %constant_dynamic-slice_fusion.1), channel_id=1, source_target_pairs={{0,24},{4,28},{8,16},{12,20},{16,8},{20,12},{24,0},{28,4},{1,25},{... | collective-permute-start | bytes 393224 | tf_op jit(solution)/shard_map/ppermute | solution.py:196
  25.6 1.6 %collective-permute-start.3 = (f32[512,128]{1,0:T(8,128)S(1)}, f32[512,128]{1,0:T(8,128)S(1)}, u32[]{:S(2)}, u32[]{:S(2)}) collective-permute-start(f32[512,128]{1,0:T(8,128)S(1)} %add_dynamic-update-slice_fusion), channel_id=1, source_target_pairs={{0,4},{4,0},{8,12},{12,8},{16,20},{20,16},{24,28},{28,24},{1,5},{5... | collective-permute-start | bytes 786440 | tf_op jit(solution)/shard_map/ppermute | solution.py:196
  27.2 2.2 %copy-start.1 = (bf16[128,128,128]{2,1,0:T(8,128)(2,1)S(1)}, bf16[128,128,128]{2,1,0:T(8,128)(2,1)}, u32[]{:S(2)}) copy-start(bf16[128,128,128]{2,1,0:T(8,128)(2,1)} %copy-done) | copy-start | bytes 12582916
  30.4 1.3 %collective-permute-start.4 = (f32[128,128]{1,0:T(8,128)S(1)}, f32[128,128]{1,0:T(8,128)S(1)}, u32[]{:S(2)}, u32[]{:S(2)}) collective-permute-start(f32[128,128]{1,0:T(8,128)S(1)} %get-tuple-element.15), channel_id=1, source_target_pairs={{0,4},{4,0},{8,12},{12,8},{16,20},{20,16},{24,28},{28,24},{1,5},{5... | collective-permute-start | bytes 196616 | tf_op jit(solution)/shard_map/ppermute | solution.py:196
  31.8 6.2 %collective-permute-start.5 = (f32[2,128,128]{2,1,0:T(8,128)S(1)}, f32[2,128,128]{2,1,0:T(8,128)S(1)}, u32[]{:S(2)}, u32[]{:S(2)}) collective-permute-start(f32[2,128,128]{2,1,0:T(8,128)S(1)} %pad_maximum_fusion), channel_id=1, source_target_pairs={{0,1},{1,0},{2,3},{3,2},{4,6},{5,7},{6,4},{7,5},{8,9},{9,8},{10,11... | collective-permute-start | bytes 393224 | tf_op jit(solution)/shard_map/ppermute | solution.py:237
  33.4 7.4 %collective-permute-start.7 = (f32[128,128]{1,0:T(8,128)S(1)}, f32[128,128]{1,0:T(8,128)S(1)}, u32[]{:S(2)}, u32[]{:S(2)}) collective-permute-start(f32[128,128]{1,0:T(8,128)S(1)} %get-tuple-element.15), channel_id=1, source_target_pairs={{0,3},{1,2},{2,1},{3,0},{4,7},{5,6},{6,5},{7,4},{8,11},{9,10},{10,... | collective-permute-start | bytes 196616 | tf_op jit(solution)/shard_map/ppermute | solution.py:196
  38.0 2.8 %collective-permute-start.6 = (f32[128,128]{1,0:T(8,128)S(1)}, f32[128,128]{1,0:T(8,128)S(1)}, u32[]{:S(2)}, u32[]{:S(2)}) collective-permute-start(f32[128,128]{1,0:T(8,128)S(1)} %dynamic-slice_bitcast_fusion), channel_id=1, source_target_pairs={{0,4},{4,0},{8,12},{12,8},{16,20},{20,16},{24,28},{28,24},{1,5},{5... | collective-permute-start | bytes 196616 | tf_op jit(solution)/shard_map/ppermute | solution.py:196
  40.8 2.2 %copy-start.2 = (bf16[128,128,128]{2,1,0:T(8,128)(2,1)S(1)}, bf16[128,128,128]{2,1,0:T(8,128)(2,1)}, u32[]{:S(2)}) copy-start(bf16[128,128,128]{2,1,0:T(8,128)(2,1)} %copy-done) | copy-start | bytes 12582916
  44.7 1.4 %collective-permute-start.8 = (f32[256,128]{1,0:T(8,128)S(1)}, f32[256,128]{1,0:T(8,128)S(1)}, u32[]{:S(2)}, u32[]{:S(2)}) collective-permute-start(f32[256,128]{1,0:T(8,128)S(1)} %get-tuple-element.18), channel_id=1, source_target_pairs={{0,4},{4,0},{8,12},{12,8},{16,20},{20,16},{24,28},{28,24},{1,5},{5... | collective-permute-start | bytes 393224 | tf_op jit(solution)/shard_map/ppermute | solution.py:196
  46.1 6.8 %collective-permute-start.9 = (f32[256,128]{1,0:T(8,128)S(1)}, f32[256,128]{1,0:T(8,128)S(1)}, u32[]{:S(2)}, u32[]{:S(2)}) collective-permute-start(f32[256,128]{1,0:T(8,128)S(1)} %add.69), channel_id=1, source_target_pairs={{0,8},{4,20},{8,0},{12,28},{16,24},{20,4},{24,16},{28,12},{1,9},{5... | collective-permute-start | bytes 393224 | tf_op jit(solution)/shard_map/ppermute | solution.py:212
  47.7 5.2 %collective-permute-start.10 = (f32[128,128]{1,0:T(8,128)S(1)}, f32[128,128]{1,0:T(8,128)S(1)}, u32[]{:S(2)}, u32[]{:S(2)}) collective-permute-start(f32[128,128]{1,0:T(8,128)S(1)} %constant_dynamic-slice_fusion), channel_id=1, source_target_pairs={{0,24},{4,28},{8,16},{12,20},{16,8},{20,12},{24,0},{28,4},{1,25},{... | collective-permute-start | bytes 196616 | tf_op jit(solution)/shard_map/ppermute | solution.py:196
  52.9 1.4 %collective-permute-start.11 = (f32[256,128]{1,0:T(8,128)S(1)}, f32[256,128]{1,0:T(8,128)S(1)}, u32[]{:S(2)}, u32[]{:S(2)}) collective-permute-start(f32[256,128]{1,0:T(8,128)S(1)} %add_dynamic-update-slice_fusion.1), channel_id=1, source_target_pairs={{0,4},{4,0},{8,12},{12,8},{16,20},{20,16},{24,28},{28,24},{1,5},{5... | collective-permute-start | bytes 393224 | tf_op jit(solution)/shard_map/ppermute | solution.py:196
  54.3 2.2 %copy-start.3 = (bf16[128,128,128]{2,1,0:T(8,128)(2,1)S(1)}, bf16[128,128,128]{2,1,0:T(8,128)(2,1)}, u32[]{:S(2)}) copy-start(bf16[128,128,128]{2,1,0:T(8,128)(2,1)} %copy-done) | copy-start | bytes 12582916
  58.0 1.2 %collective-permute-start.12 = (f32[64,128]{1,0:T(8,128)S(1)}, f32[64,128]{1,0:T(8,128)S(1)}, u32[]{:S(2)}, u32[]{:S(2)}) collective-permute-start(f32[64,128]{1,0:T(8,128)S(1)} %get-tuple-element.20), channel_id=1, source_target_pairs={{0,4},{4,0},{8,12},{12,8},{16,20},{20,16},{24,28},{28,24},{1,5},{5... | collective-permute-start | bytes 98312 | tf_op jit(solution)/shard_map/ppermute | solution.py:196
  59.3 5.0 %collective-permute-start.13 = (f32[2,64,128]{2,1,0:T(8,128)S(1)}, f32[2,64,128]{2,1,0:T(8,128)S(1)}, u32[]{:S(2)}, u32[]{:S(2)}) collective-permute-start(f32[2,64,128]{2,1,0:T(8,128)S(1)} %pad_maximum_fusion.1), channel_id=1, source_target_pairs={{0,1},{1,0},{2,3},{3,2},{4,6},{5,7},{6,4},{7,5},{8,9},{9,8},{10,11... | collective-permute-start | bytes 196616 | tf_op jit(solution)/shard_map/ppermute | solution.py:237
  60.7 6.1 %collective-permute-start.15 = (f32[64,128]{1,0:T(8,128)S(1)}, f32[64,128]{1,0:T(8,128)S(1)}, u32[]{:S(2)}, u32[]{:S(2)}) collective-permute-start(f32[64,128]{1,0:T(8,128)S(1)} %get-tuple-element.20), channel_id=1, source_target_pairs={{0,3},{1,2},{2,1},{3,0},{4,7},{5,6},{6,5},{7,4},{8,11},{9,10},{10,... | collective-permute-start | bytes 98312 | tf_op jit(solution)/shard_map/ppermute | solution.py:196
  64.3 2.4 %collective-permute-start.14 = (f32[64,128]{1,0:T(8,128)S(1)}, f32[64,128]{1,0:T(8,128)S(1)}, u32[]{:S(2)}, u32[]{:S(2)}) collective-permute-start(f32[64,128]{1,0:T(8,128)S(1)} %dynamic-slice_bitcast_fusion.1), channel_id=1, source_target_pairs={{0,4},{4,0},{8,12},{12,8},{16,20},{20,16},{24,28},{28,24},{1,5},{5... | collective-permute-start | bytes 98312 | tf_op jit(solution)/shard_map/ppermute | solution.py:196

commit v2 on v1

v2 whole, which is shorter than its diff:
```python
import jax
import jax.numpy as jnp
from jax import lax
from jax.experimental import pallas as pl
from jax.experimental.pallas import tpu as pltpu
from jax.sharding import PartitionSpec as P

ITERS = 2
F32 = jnp.float32
BF16 = jnp.bfloat16
BLK = 128
CHUNKS = 8


def whole(space=pltpu.VMEM):
    return pl.BlockSpec(memory_space=space)


def iota(shape, dim):
    return lax.broadcasted_iota(jnp.int32, shape, dim)


def split3(x):
    hi = x.astype(BF16)
    rest = x - hi.astype(F32)
    mid = rest.astype(BF16)
    low = (rest - mid.astype(F32)).astype(BF16)
    return hi, mid, low


def dot(a, b, dims=((1,), (0,))):
    return lax.dot_general(a, b, (dims, ((), ())), preferred_element_type=F32)


def one_hot_t(row, size):
    return jnp.where(iota((size, row.shape[1]), 0) == row, 1.0, 0.0)


def block_rows(slot, ray, count, slabs, capacity, ray_dev):
    slots = ray.shape[1]
    picks = one_hot_t(slot, slots).astype(BF16)
    rays = jnp.broadcast_to(ray, (16, slots)).astype(F32).astype(BF16)
    ray = dot(rays, picks)[0:1, :].astype(jnp.int32)
    owner = jnp.zeros_like(slot)
    for o in range(1, slabs):
        owner = owner + jnp.where(slot >= o * capacity, 1, 0)
    place = (owner & 1) * (slabs // 2) + (owner >> 1)
    stored = iota(slot.shape, 1) < count
    return jnp.where(stored, place * ray_dev + ray, -1)


def forward(proj, volume, vox, sums, before=None):
    blocks = proj.shape[0]
    half = blocks // 2
    picked = dot(volume.T.astype(BF16), one_hot_t(vox, volume.shape[0]).astype(BF16))
    lane = iota((BLK, blocks), 1)
    weights = jnp.concatenate([jnp.where(lane < half, picked, 0.0), jnp.where(lane >= half, picked, 0.0)], 0)
    if sums:
        ones = jnp.concatenate([jnp.where(lane < half, 1.0, 0.0), jnp.where(lane >= half, 1.0, 0.0)], 0)
        weights = jnp.concatenate([weights, ones], 1)
    weights = weights.astype(BF16)
    width = weights.shape[1]
    column = lax.rem(iota((BLK, width), 1), half)

    def step(p, acc):
        pair = jnp.concatenate([proj[p], proj[p + half]], 1)
        return jnp.where(column == p, dot(pair, weights), acc)

    acc = jnp.zeros((BLK, width), F32)
    per = half // CHUNKS
    for c in range(CHUNKS):
        if before is not None:
            before(c)
        for p in range(c * per, (c + 1) * per):
            acc = step(p, acc)
    return acc


def spread(rows, columns, total):
    spots = one_hot_t(rows, total).astype(BF16)
    out = None
    for term in split3(columns):
        part = dot(spots, term, ((1,), (1,)))
        out = part if out is None else out + part
    return out


def backward(proj, weighted, rows, vox, vox_dev, sums):
    blocks = proj.shape[0]
    spots = one_hot_t(rows, weighted.shape[0])
    picked = dot(spots.T.astype(BF16), weighted.astype(BF16)).astype(BF16)
    group = 16
    row = iota((group, BLK), 0)
    stored = jnp.where(rows >= 0, 1.0, 0.0)
    places = (one_hot_t(vox, vox_dev) * stored).astype(BF16)
    tops, lows = [], []
    for g in range(blocks // group):
        mine = picked[g * group:(g + 1) * group].astype(F32)
        left = [jnp.where(row == c, mine, 0.0) for c in range(group)]
        left = jnp.concatenate(left, 1)
        if sums:
            ones = jnp.concatenate([jnp.where(row == c, 1.0, 0.0) for c in range(group)], 1)
            left = jnp.concatenate([left, ones], 0)
        right = proj[g * group:(g + 1) * group].reshape(group * BLK, BLK)
        out = dot(left.astype(BF16), right)
        tops.append(out[:group])
        if sums:
            lows.append(out[group:])
    columns = jnp.concatenate(tops, 0)
    if sums:
        columns = jnp.concatenate([columns, jnp.concatenate(lows, 0)], 1)
    out = None
    for term in split3(columns):
        part = dot(places, term)
        out = part if out is None else out + part
    return out


def put_partial(sums, sino, mine, theirs, ray_dev):
    half = sums.shape[0] // 2
    slab = lax.axis_index("slab")
    core = lax.rem(slab, 2)
    top, low = sums[:half], sums[half:]
    mine[0:half, :] = -jnp.where(core == 0, top, low)
    theirs[0:half, :] = -jnp.where(core == 0, low, top)
    at = pl.ds(pl.multiple_of((slab >> 1) * ray_dev, 8), ray_dev)
    mine[at, :] = mine[at, :] + sino


def first_forward(slabs, capacity, ray_dev):
    def kernel(proj_hbm, vox_hbm, slot_hbm, ray_hbm, count_hbm, prior_hbm, sino_hbm,
               proj, vox, rows_out, prior, sino, mine, theirs, slot, ray, count, sems, small):
        blocks = proj_hbm.shape[0]
        half = blocks // 2
        per = half // CHUNKS
        smalls = [
            pltpu.make_async_copy(source, target, small.at[i])
            for i, (source, target) in enumerate([
                (vox_hbm, vox), (slot_hbm, slot), (ray_hbm, ray), (count_hbm, count),
                (prior_hbm, prior), (sino_hbm, sino),
            ])
        ]
        for copy in smalls:
            copy.start()
        copies = []
        for c in range(CHUNKS):
            for h in range(2):
                at = pl.ds(h * half + c * per, per)
                copy = pltpu.make_async_copy(proj_hbm.at[at], proj.at[at], sems.at[2 * c + h])
                copy.start()
                copies.append(copy)
        for copy in smalls:
            copy.wait()

        def before(c):
            copies[2 * c].wait()
            copies[2 * c + 1].wait()

        rows = block_rows(slot[...], ray[...], count[...], slabs, capacity, ray_dev)
        rows_out[...] = rows
        total = slabs * ray_dev
        columns = forward(proj, prior[...], vox[...], True, before)
        put_partial(spread(rows, columns[:, :blocks], total), sino[...], mine, theirs, ray_dev)
        sums = spread(rows, columns[:, blocks:], total)
        core = lax.rem(lax.axis_index("slab"), 2)
        top, low = sums[:total // 2], sums[total // 2:]
        mine[total // 2:total, :] = jnp.where(core == 0, top, low)
        theirs[total // 2:total, :] = jnp.where(core == 0, low, top)

    return kernel


def join_halves(mine, theirs):
    core = lax.rem(lax.axis_index("slab"), 2)
    mine, theirs = mine[...], theirs[...]
    return jnp.concatenate([jnp.where(core == 0, mine, theirs), jnp.where(core == 0, theirs, mine)], 0)


def first_backward(proj, rows, vox, mine, theirs, corr):
    vox_dev = corr.shape[0] // 2
    both = backward(proj, join_halves(mine, theirs), rows[...], vox[...], vox_dev, True)
    corr[0:vox_dev, :] = both[:, :BLK]
    corr[vox_dev:2 * vox_dev, :] = both[:, BLK:]


def next_forward(ray_dev):
    def kernel(proj, rows, vox, volume, corr, sino, volume_out, weight_out, mine, theirs):
        vox_dev = volume.shape[0]
        weights = 1.0 / jnp.maximum(corr[vox_dev:2 * vox_dev, :], 1.0)
        weight_out[...] = weights
        updated = volume[...] + weights * corr[0:vox_dev, :]
        volume_out[...] = updated
        columns = forward(proj, updated, vox[...], False)
        put_partial(spread(rows[...], columns, 2 * mine.shape[0]), sino[...], mine, theirs, ray_dev)

    return kernel


def last_backward(proj, rows, vox, mine, theirs, corr):
    corr[...] = backward(proj, join_halves(mine, theirs), rows[...], vox[...], corr.shape[0], False)


def swap(x, axis, bit):
    size = lax.axis_size(axis)
    return lax.ppermute(x, axis, [(i, i ^ bit) for i in range(size)])


def over_slabs(mine, theirs):
    slabs = lax.axis_size("slab")
    x = mine + swap(theirs, "slab", 1)
    bits = [1 << b for b in range(1, slabs.bit_length() - 1)]
    while bits:
        if len(bits) == 1:
            x, bits = x + swap(x, "slab", bits[0]), []
            continue
        first, second, bits = bits[0], bits[1], bits[2:]
        x = (x + swap(x, "slab", first)) + (swap(x, "slab", second) + swap(x, "slab", first | second))
    return x


def over_angles(x):
    slabs, angles = lax.axis_size("slab"), lax.axis_size("angle")
    bits = [1 << b for b in range(angles.bit_length() - 1)]
    for bit in bits:
        x = x + swap(x, "angle", bit)
    return x


def local(projector, block_vox, block_slot, send_ray, block_count, prior, sinogram):
    slabs = lax.axis_size("slab")
    capacity = send_ray.shape[1] // slabs
    ray_dev = sinogram.shape[0]
    vox_dev = prior.shape[0]
    blocks = projector.shape[0]
    half = slabs * ray_dev // 2
    params = pltpu.CompilerParams(vmem_limit_bytes=8 * 1024 * 1024)
    vmem = lambda rows, dtype=F32: pltpu.VMEM((rows, BLK), dtype)
    line = pltpu.VMEM((1, blocks), jnp.int32)
    arguments = (
        projector, block_vox.reshape(1, blocks), block_slot.reshape(1, blocks), send_ray,
        block_count.reshape(1, 1), prior, sinogram,
    )

    proj, vox, rows, volume, sino, mine, theirs = pl.pallas_call(
        first_forward(slabs, capacity, ray_dev),
        out_shape=(
            pltpu.VMEM(projector.shape, BF16), line, line, vmem(vox_dev), vmem(ray_dev),
            vmem(2 * half), vmem(2 * half),
        ),
        in_specs=[whole(pl.ANY)] * 7,
        out_specs=(whole(),) * 7,
        scratch_shapes=[
            line,
            pltpu.VMEM(send_ray.shape, jnp.int32),
            pltpu.VMEM((1, 1), jnp.int32),
            pltpu.SemaphoreType.DMA((2 * CHUNKS,)),
            pltpu.SemaphoreType.DMA((6,)),
        ],
        compiler_params=params,
        name="first_forward",
    )(*[x if x.size == 1 else pltpu.with_memory_space_constraint(x, pltpu.HBM) for x in arguments])
    sums = over_slabs(mine, theirs)
    row_weight = 1.0 / jnp.maximum(sums[half:], 1.0)
    weighted = (row_weight * sums[:half]).astype(BF16)

    corr = pl.pallas_call(
        first_backward,
        out_shape=vmem(2 * vox_dev),
        in_specs=[whole()] * 5,
        out_specs=whole(),
        compiler_params=params,
        name="first_backward",
    )(proj, rows, vox, weighted, swap(weighted, "slab", 1))
    corr = over_angles(corr)

    volume, col_weight, mine, theirs = pl.pallas_call(
        next_forward(ray_dev),
        out_shape=(vmem(vox_dev), vmem(vox_dev), vmem(half), vmem(half)),
        in_specs=[whole()] * 6,
        out_specs=(whole(),) * 4,
        compiler_params=params,
        name="next_forward",
    )(proj, rows, vox, volume, corr, sino)
    residual = row_weight * over_slabs(mine, theirs)
    weighted = residual.astype(BF16)
    start = lax.div(lax.axis_index("slab"), 2) * ray_dev
    residual = lax.dynamic_slice_in_dim(residual, start, ray_dev)

    corr = pl.pallas_call(
        last_backward,
        out_shape=vmem(vox_dev),
        in_specs=[whole()] * 5,
        out_specs=whole(),
        compiler_params=params,
        name="last_backward",
    )(proj, rows, vox, weighted, swap(weighted, "slab", 1))
    corr = over_angles(corr)
    return volume + col_weight * corr, residual


def solution(mesh):
    return jax.shard_map(
        local,
        mesh=mesh,
        in_specs=(
            P(("slab", "angle"), None, None),
            P(("slab", "angle")),
            P(("slab", "angle")),
            P(("slab", "angle"), None),
            P(("slab", "angle")),
            P("slab", None),
            P(("slab", "angle"), None),
        ),
        out_specs=(P("slab", None), P(("slab", "angle"), None)),
        check_vma=False,
    )
```

time: 67.8 us -> 53.1 us (0.78)
  local copies, waits for them, and re-layouts: 14.2 us -> 0.61 us
  waiting for transfers between devices: 27.2 us -> 24 us
  starting transfers between devices: 16.1 us -> 17.4 us
  Pallas kernels: 7.66 us -> 8.88 us
    unnamed x26 -> x0, local copies, waits for them, and re-layouts: 14.2 us -> none
    ppermute x12 -> x14, starting transfers between devices: 8.51 us -> 17.4 us  [swap(): return lax.ppermute(x, axis, [(i, i ^ bit) for i in range(size)])]
    ppermute x4 -> x0, starting transfers between devices: 7.55 us -> none  [the longest x2 4.51 us: over_slabs(): lax.ppermute(x, 'slab', [(i, i ^ (second if i & 1 else first)) for i in r...]
    ppermute x4 -> x0, waiting for transfers between devices: 3.16 us -> none  [the longest x2 3.16 us: over_angles(): near = lax.ppermute(both, ('slab', 'angle'), pairs)]
    pallas_call x1, Pallas kernels: 3.4 us -> 5.12 us  [local(): pl.pallas_call(first_forward(slabs, capacity, ray_dev), out_shape=(pltpu....]
    ppermute x12 -> x14, waiting for transfers between devices: 24 us -> 24 us  [swap(): return lax.ppermute(x, axis, [(i, i ^ bit) for i in range(size)])]
  transfers between devices with their start and end apart: 16 -> 14, of which waited for: 12 -> 13; matrix products, arithmetic and copies ran while one was open for 0% -> 1% of each run, Pallas kernels for 0% -> 0%
where the time goes in v2:
time: 53.1 us; the launch traced here: 53 us
  waiting for transfers between devices  24 us (45%)
  starting transfers between devices  17.4 us (33%)
  Pallas kernels  8.88 us (17%)
  between operations  1.36 us (3%)
  other arithmetic  0.76 us (1%)
  local copies, waits for them, and re-layouts  0.61 us (1%)
    ppermute x14, waiting for transfers between devices, swap(): return lax.ppermute(x, axis, [(i, i ^ bit) for i in range(size)])  24 us
    ppermute x14, starting transfers between devices, swap(): return lax.ppermute(x, axis, [(i, i ^ bit) for i in range(size)])  17.4 us
    pallas_call x1, Pallas kernels, local(): pl.pallas_call(first_forward(slabs, capacity, ray_dev), out_shape=(pltpu....  5.12 us
    pallas_call x1, Pallas kernels, local(): pl.pallas_call(next_forward(ray_dev), out_shape=(vmem(vox_dev), vmem(vox_...  1.71 us
  transfers between devices with their start and end apart: 14, of which 13 were waited for; matrix products, arithmetic and copies ran while one was open for 1% of the time, Pallas kernels for 0%

profile of v2, /device:TPU:0, one launch (start us, length us, event | category | flops | bytes accessed | tf_op | source)
XLA Modules:
  0.0 53.0 jit_solution(7245834390548968502)
XLA Ops:
  1.3 5.1 %first_forward.1 = (bf16[128,128,128]{2,1,0:T(8,128)(2,1)S(1)}, s32[1,128]{1,0:T(1,128)S(1)}, s32[1,128]{1,0:T(1,128)S(1)}, f32[64,128]{1,0:T(8,128)S(1)}, f32[3...) custom-call(bf16[128,128,128]{2,1,0:T(8,128)(2,1)} %proj_hbm.1, s32[1,128]{1,0:T(1,128)} %bitcast.4, ...), custom_call_target="tpu_custom_call" | custom-call | tf_op jit(solution)/shard_map/first_forward/pallas_call | solution.py:244
  6.4 0.5 collective-permute-start
  6.9 1.0 %collective-permute-done = f32[256,128]{1,0:T(8,128)S(1)} collective-permute-done((f32[256,128]{1,0:T(8,128)S(1)}, f32[256,128]{1,0:T(8,128)S(1)}, u32[]{:S(2)}, u32[]{:S(2)}) %collective-permute-start) | collective-permute-done | bytes 131104 | tf_op jit(solution)/shard_map/ppermute | solution.py:205
  7.9 2.9 %collective-permute-start.1 = (f32[256,128]{1,0:T(8,128)S(1)}, f32[256,128]{1,0:T(8,128)S(1)}, u32[]{:S(2)}, u32[]{:S(2)}) collective-permute-start(f32[256,128]{1,0:T(8,128)S(1)} %add.42), channel_id=1, source_target_pairs={{0,8},{4,12},{8,0},{12,4},{16,24},{20,28},{24,16},{28,20},{1,9},{5... | collective-permute-start | bytes 393224 | tf_op jit(solution)/shard_map/ppermute | solution.py:205
  10.9 1.5 %collective-permute-start.2 = (f32[256,128]{1,0:T(8,128)S(1)}, f32[256,128]{1,0:T(8,128)S(1)}, u32[]{:S(2)}, u32[]{:S(2)}) collective-permute-start(f32[256,128]{1,0:T(8,128)S(1)} %add.42), channel_id=1, source_target_pairs={{0,16},{4,20},{8,24},{12,28},{16,0},{20,4},{24,8},{28,12},{1,17},{... | collective-permute-start | bytes 393224 | tf_op jit(solution)/shard_map/ppermute | solution.py:205
  12.4 2.4 %collective-permute-done.1 = f32[256,128]{1,0:T(8,128)S(1)} collective-permute-done((f32[256,128]{1,0:T(8,128)S(1)}, f32[256,128]{1,0:T(8,128)S(1)}, u32[]{:S(2)}, u32[]{:S(2)}) %collective-permute-start.1) | collective-permute-done | bytes 131104 | tf_op jit(solution)/shard_map/ppermute | solution.py:205
  14.8 4.2 %collective-permute-done.2 = f32[256,128]{1,0:T(8,128)S(1)} collective-permute-done((f32[256,128]{1,0:T(8,128)S(1)}, f32[256,128]{1,0:T(8,128)S(1)}, u32[]{:S(2)}, u32[]{:S(2)}) %collective-permute-start.2) | collective-permute-done | bytes 131104 | tf_op jit(solution)/shard_map/ppermute | solution.py:205
  19.0 0.1 collective-permute-start.4
  19.1 1.2 %collective-permute-done.4.theirs = bf16[128,128]{1,0:T(8,128)(2,1)S(1)} collective-permute-done((bf16[128,128]{1,0:T(8,128)(2,1)S(1)}, bf16[128,128]{1,0:T(8,128)(2,1)S(1)}, u32[]{:S(2)}, u32[]{:S(2)}) %collective-permute-start.4) | collective-permute-done | bytes 32800 | tf_op jit(solution)/shard_map/ppermute | solution.py:205
  20.3 1.0 %first_backward.1 = f32[128,128]{1,0:T(8,128)S(1)} custom-call(bf16[128,128,128]{2,1,0:T(8,128)(2,1)S(1)} %get-tuple-element.13.proj, s32[1,128]{1,0:T(1,128)S(1)} %get-tuple-element.14.rows, s32[1,128]{1,0:T(1,128)S(1)} %get-tuple-element.15.vox, bf16[128,128]{1,0:T(8,128)(2,1)S(1)} %fusion.mine, bf16[128,128]{1,0:T(8,128)(2,1)S(1)} %collective-permute-done.4.theirs), custom_call_target="tpu_custom_call" | custom-call | tf_op jit(solution)/shard_map/first_backward/pallas_call | solution.py:266
  21.3 1.6 %collective-permute-start.5 = (f32[128,128]{1,0:T(8,128)S(1)}, f32[128,128]{1,0:T(8,128)S(1)}, u32[]{:S(2)}, u32[]{:S(2)}) collective-permute-start(f32[128,128]{1,0:T(8,128)S(1)} %first_backward.1), channel_id=1, source_target_pairs={{0,1},{1,0},{2,3},{3,2},{4,5},{5,4},{6,7},{7,6},{8,9},{9,8},{10,11... | collective-permute-start | bytes 196616 | tf_op jit(solution)/shard_map/ppermute | solution.py:205
  23.0 2.7 %collective-permute-done.5 = f32[128,128]{1,0:T(8,128)S(1)} collective-permute-done((f32[128,128]{1,0:T(8,128)S(1)}, f32[128,128]{1,0:T(8,128)S(1)}, u32[]{:S(2)}, u32[]{:S(2)}) %collective-permute-start.5) | collective-permute-done | bytes 65568 | tf_op jit(solution)/shard_map/ppermute | solution.py:205
  25.7 2.6 %collective-permute-start.6 = (f32[128,128]{1,0:T(8,128)S(1)}, f32[128,128]{1,0:T(8,128)S(1)}, u32[]{:S(2)}, u32[]{:S(2)}) collective-permute-start(f32[128,128]{1,0:T(8,128)S(1)} %add.46), channel_id=1, source_target_pairs={{0,2},{1,3},{2,0},{3,1},{4,6},{5,7},{6,4},{7,5},{8,10},{9,11},{10,... | collective-permute-start | bytes 196616 | tf_op jit(solution)/shard_map/ppermute | solution.py:205
  28.3 2.6 %collective-permute-done.6 = f32[128,128]{1,0:T(8,128)S(1)} collective-permute-done((f32[128,128]{1,0:T(8,128)S(1)}, f32[128,128]{1,0:T(8,128)S(1)}, u32[]{:S(2)}, u32[]{:S(2)}) %collective-permute-start.6) | collective-permute-done | bytes 65568 | tf_op jit(solution)/shard_map/ppermute | solution.py:205
  30.9 1.7 %next_forward.1 = (f32[64,128]{1,0:T(8,128)S(1)}, f32[64,128]{1,0:T(8,128)S(1)}, f32[128,128]{1,0:T(8,128)S(1)}, f32[128,128]{1,0:T(8,128)S(1)}) custom-call(bf16[128,128,128]{2,1,0:T(8,128)(2,1)S(1)} %get-tuple-element.13.proj, s32[1,128]{1,0:T(1,128)S(1)} %get-tuple-element.14.rows, s32[1,128]{1,0:T(1,128)S(1)} %get-tuple-element.15.vox, ...), custom_call_target="tpu_custom_call" | custom-call | tf_op jit(solution)/shard_map/next_forward/pallas_call | solution.py:276
  32.6 0.1 collective-permute-start.7
  32.7 1.2 %collective-permute-done.7 = f32[128,128]{1,0:T(8,128)S(1)} collective-permute-done((f32[128,128]{1,0:T(8,128)S(1)}, f32[128,128]{1,0:T(8,128)S(1)}, u32[]{:S(2)}, u32[]{:S(2)}) %collective-permute-start.7) | collective-permute-done | bytes 65568 | tf_op jit(solution)/shard_map/ppermute | solution.py:205
  34.0 1.5 %collective-permute-start.10 = (f32[128,128]{1,0:T(8,128)S(1)}, f32[128,128]{1,0:T(8,128)S(1)}, u32[]{:S(2)}, u32[]{:S(2)}) collective-permute-start(f32[128,128]{1,0:T(8,128)S(1)} %add.48), channel_id=1, source_target_pairs={{0,24},{4,28},{8,16},{12,20},{16,8},{20,12},{24,0},{28,4},{1,25},{... | collective-permute-start | bytes 196616 | tf_op jit(solution)/shard_map/ppermute | solution.py:205
  35.5 1.5 %collective-permute-start.8 = (f32[128,128]{1,0:T(8,128)S(1)}, f32[128,128]{1,0:T(8,128)S(1)}, u32[]{:S(2)}, u32[]{:S(2)}) collective-permute-start(f32[128,128]{1,0:T(8,128)S(1)} %add.48), channel_id=1, source_target_pairs={{0,8},{4,12},{8,0},{12,4},{16,24},{20,28},{24,16},{28,20},{1,9},{5... | collective-permute-start | bytes 196616 | tf_op jit(solution)/shard_map/ppermute | solution.py:205
  37.0 0.5 collective-permute-start.9
  37.5 2.2 %collective-permute-done.10 = f32[128,128]{1,0:T(8,128)S(1)} collective-permute-done((f32[128,128]{1,0:T(8,128)S(1)}, f32[128,128]{1,0:T(8,128)S(1)}, u32[]{:S(2)}, u32[]{:S(2)}) %collective-permute-start.10) | collective-permute-done | bytes 65568 | tf_op jit(solution)/shard_map/ppermute | solution.py:205
  39.8 0.8 %collective-permute-done.8 = f32[128,128]{1,0:T(8,128)S(1)} collective-permute-done((f32[128,128]{1,0:T(8,128)S(1)}, f32[128,128]{1,0:T(8,128)S(1)}, u32[]{:S(2)}, u32[]{:S(2)}) %collective-permute-start.8) | collective-permute-done | bytes 65568 | tf_op jit(solution)/shard_map/ppermute | solution.py:205
  40.5 0.7 %collective-permute-done.9 = f32[128,128]{1,0:T(8,128)S(1)} collective-permute-done((f32[128,128]{1,0:T(8,128)S(1)}, f32[128,128]{1,0:T(8,128)S(1)}, u32[]{:S(2)}, u32[]{:S(2)}) %collective-permute-start.9) | collective-permute-done | bytes 65568 | tf_op jit(solution)/shard_map/ppermute | solution.py:205
  41.3 0.1 collective-permute-start.11
  41.4 1.2 %collective-permute-done.11.theirs = bf16[128,128]{1,0:T(8,128)(2,1)S(1)} collective-permute-done((bf16[128,128]{1,0:T(8,128)(2,1)S(1)}, bf16[128,128]{1,0:T(8,128)(2,1)S(1)}, u32[]{:S(2)}, u32[]{:S(2)}) %collective-permute-start.11) | collective-permute-done | bytes 32800 | tf_op jit(solution)/shard_map/ppermute | solution.py:205
  42.6 1.0 %last_backward.1 = f32[64,128]{1,0:T(8,128)S(1)} custom-call(bf16[128,128,128]{2,1,0:T(8,128)(2,1)S(1)} %get-tuple-element.13.proj, s32[1,128]{1,0:T(1,128)S(1)} %get-tuple-element.14.rows, s32[1,128]{1,0:T(1,128)S(1)} %get-tuple-element.15.vox, bf16[128,128]{1,0:T(8,128)(2,1)S(1)} %get-tuple-element.24.mine, bf16[128,128]{1,0:T(8,128)(2,1)S(1)} %collective-permute-done.11.theirs), custom_call_target="tpu_custom_call" | custom-call | tf_op jit(solution)/shard_map/last_backward/pallas_call | solution.py:289
  43.6 1.6 %collective-permute-start.12 = (f32[64,128]{1,0:T(8,128)S(1)}, f32[64,128]{1,0:T(8,128)S(1)}, u32[]{:S(2)}, u32[]{:S(2)}) collective-permute-start(f32[64,128]{1,0:T(8,128)S(1)} %last_backward.1), channel_id=1, source_target_pairs={{0,1},{1,0},{2,3},{3,2},{4,5},{5,4},{6,7},{7,6},{8,9},{9,8},{10,11... | collective-permute-start | bytes 98312 | tf_op jit(solution)/shard_map/ppermute | solution.py:205
  45.2 2.3 %collective-permute-done.12 = f32[64,128]{1,0:T(8,128)S(1)} collective-permute-done((f32[64,128]{1,0:T(8,128)S(1)}, f32[64,128]{1,0:T(8,128)S(1)}, u32[]{:S(2)}, u32[]{:S(2)}) %collective-permute-start.12) | collective-permute-done | bytes 32800 | tf_op jit(solution)/shard_map/ppermute | solution.py:205
  47.5 2.7 %collective-permute-start.13 = (f32[64,128]{1,0:T(8,128)S(1)}, f32[64,128]{1,0:T(8,128)S(1)}, u32[]{:S(2)}, u32[]{:S(2)}) collective-permute-start(f32[64,128]{1,0:T(8,128)S(1)} %add.52), channel_id=1, source_target_pairs={{0,2},{1,3},{2,0},{3,1},{4,6},{5,7},{6,4},{7,5},{8,10},{9,11},{10,... | collective-permute-start | bytes 98312 | tf_op jit(solution)/shard_map/ppermute | solution.py:205
  50.2 0.6 %constant_dynamic-slice_fusion = f32[32,128]{1,0:T(8,128)} fusion(f32[128,128]{1,0:T(8,128)S(1)} %get-tuple-element.25, s32[]{:T(128)S(6)} %select_n.3), kind=kLoop, calls=%fused_computation.7 | loop fusion | bytes 32772 | tf_op jit(solution)/shard_map/dynamic_slice | solution.py:287
  50.9 1.5 %collective-permute-done.13 = f32[64,128]{1,0:T(8,128)S(1)} collective-permute-done((f32[64,128]{1,0:T(8,128)S(1)}, f32[64,128]{1,0:T(8,128)S(1)}, u32[]{:S(2)}, u32[]{:S(2)}) %collective-permute-start.13) | collective-permute-done | bytes 32800 | tf_op jit(solution)/shard_map/ppermute | solution.py:205
  52.3 0.6 %multiply_add_fusion = f32[64,128]{1,0:T(8,128)} fusion(f32[64,128]{1,0:T(8,128)S(1)} %get-tuple-element.20, f32[64,128]{1,0:T(8,128)S(1)} %get-tuple-element.21, f32[64,128]{1,0:T(8,128)S(1)} %add.52, f32[64,128]{1,0:T(8,128)S(1)} %collective-permute-done.13), kind=kLoop, calls=%fused_computation.6 | loop fusion | flops 24576 | bytes 163840 | tf_op jit(solution)/shard_map/add | solution.py:298
  (10 shorter events, 0.2 us)
Async XLA Ops:
  6.4 1.5 %collective-permute-start = (f32[256,128]{1,0:T(8,128)S(1)}, f32[256,128]{1,0:T(8,128)S(1)}, u32[]{:S(2)}, u32[]{:S(2)}) collective-permute-start(f32[256,128]{1,0:T(8,128)S(1)} %get-tuple-element.18), channel_id=1, source_target_pairs={{0,4},{4,0},{8,12},{12,8},{16,20},{20,16},{24,28},{28,24},{1,5},{5... | collective-permute-start | bytes 393224 | tf_op jit(solution)/shard_map/ppermute | solution.py:205
  7.9 6.8 %collective-permute-start.1 = (f32[256,128]{1,0:T(8,128)S(1)}, f32[256,128]{1,0:T(8,128)S(1)}, u32[]{:S(2)}, u32[]{:S(2)}) collective-permute-start(f32[256,128]{1,0:T(8,128)S(1)} %add.42), channel_id=1, source_target_pairs={{0,8},{4,12},{8,0},{12,4},{16,24},{20,28},{24,16},{28,20},{1,9},{5... | collective-permute-start | bytes 393224 | tf_op jit(solution)/shard_map/ppermute | solution.py:205
  10.9 8.1 %collective-permute-start.2 = (f32[256,128]{1,0:T(8,128)S(1)}, f32[256,128]{1,0:T(8,128)S(1)}, u32[]{:S(2)}, u32[]{:S(2)}) collective-permute-start(f32[256,128]{1,0:T(8,128)S(1)} %add.42), channel_id=1, source_target_pairs={{0,16},{4,20},{8,24},{12,28},{16,0},{20,4},{24,8},{28,12},{1,17},{... | collective-permute-start | bytes 393224 | tf_op jit(solution)/shard_map/ppermute | solution.py:205
  12.4 6.6 %collective-permute-start.3 = (f32[256,128]{1,0:T(8,128)S(1)}, f32[256,128]{1,0:T(8,128)S(1)}, u32[]{:S(2)}, u32[]{:S(2)}) collective-permute-start(f32[256,128]{1,0:T(8,128)S(1)} %add.42), channel_id=1, source_target_pairs={{0,24},{4,28},{8,16},{12,20},{16,8},{20,12},{24,0},{28,4},{1,25},{... | collective-permute-start | bytes 393224 | tf_op jit(solution)/shard_map/ppermute | solution.py:205
  19.0 1.3 %collective-permute-start.4 = (bf16[128,128]{1,0:T(8,128)(2,1)S(1)}, bf16[128,128]{1,0:T(8,128)(2,1)S(1)}, u32[]{:S(2)}, u32[]{:S(2)}) collective-permute-start(bf16[128,128]{1,0:T(8,128)(2,1)S(1)} %fusion.mine), channel_id=1, source_target_pairs={{0,4},{4,0},{8,12},{12,8},{16,20},{20,16},{24,28},{28,24},{1,5},{5... | collective-permute-start | bytes 98312 | tf_op jit(solution)/shard_map/ppermute | solution.py:205
  21.3 4.3 %collective-permute-start.5 = (f32[128,128]{1,0:T(8,128)S(1)}, f32[128,128]{1,0:T(8,128)S(1)}, u32[]{:S(2)}, u32[]{:S(2)}) collective-permute-start(f32[128,128]{1,0:T(8,128)S(1)} %first_backward.1), channel_id=1, source_target_pairs={{0,1},{1,0},{2,3},{3,2},{4,5},{5,4},{6,7},{7,6},{8,9},{9,8},{10,11... | collective-permute-start | bytes 196616 | tf_op jit(solution)/shard_map/ppermute | solution.py:205
  25.7 5.2 %collective-permute-start.6 = (f32[128,128]{1,0:T(8,128)S(1)}, f32[128,128]{1,0:T(8,128)S(1)}, u32[]{:S(2)}, u32[]{:S(2)}) collective-permute-start(f32[128,128]{1,0:T(8,128)S(1)} %add.46), channel_id=1, source_target_pairs={{0,2},{1,3},{2,0},{3,1},{4,6},{5,7},{6,4},{7,5},{8,10},{9,11},{10,... | collective-permute-start | bytes 196616 | tf_op jit(solution)/shard_map/ppermute | solution.py:205
  32.6 1.3 %collective-permute-start.7 = (f32[128,128]{1,0:T(8,128)S(1)}, f32[128,128]{1,0:T(8,128)S(1)}, u32[]{:S(2)}, u32[]{:S(2)}) collective-permute-start(f32[128,128]{1,0:T(8,128)S(1)} %get-tuple-element.23), channel_id=1, source_target_pairs={{0,4},{4,0},{8,12},{12,8},{16,20},{20,16},{24,28},{28,24},{1,5},{5... | collective-permute-start | bytes 196616 | tf_op jit(solution)/shard_map/ppermute | solution.py:205
  34.0 5.8 %collective-permute-start.10 = (f32[128,128]{1,0:T(8,128)S(1)}, f32[128,128]{1,0:T(8,128)S(1)}, u32[]{:S(2)}, u32[]{:S(2)}) collective-permute-start(f32[128,128]{1,0:T(8,128)S(1)} %add.48), channel_id=1, source_target_pairs={{0,24},{4,28},{8,16},{12,20},{16,8},{20,12},{24,0},{28,4},{1,25},{... | collective-permute-start | bytes 196616 | tf_op jit(solution)/shard_map/ppermute | solution.py:205
  35.5 5.0 %collective-permute-start.8 = (f32[128,128]{1,0:T(8,128)S(1)}, f32[128,128]{1,0:T(8,128)S(1)}, u32[]{:S(2)}, u32[]{:S(2)}) collective-permute-start(f32[128,128]{1,0:T(8,128)S(1)} %add.48), channel_id=1, source_target_pairs={{0,8},{4,12},{8,0},{12,4},{16,24},{20,28},{24,16},{28,20},{1,9},{5... | collective-permute-start | bytes 196616 | tf_op jit(solution)/shard_map/ppermute | solution.py:205
  37.0 4.3 %collective-permute-start.9 = (f32[128,128]{1,0:T(8,128)S(1)}, f32[128,128]{1,0:T(8,128)S(1)}, u32[]{:S(2)}, u32[]{:S(2)}) collective-permute-start(f32[128,128]{1,0:T(8,128)S(1)} %add.48), channel_id=1, source_target_pairs={{0,16},{4,20},{8,24},{12,28},{16,0},{20,4},{24,8},{28,12},{1,17},{... | collective-permute-start | bytes 196616 | tf_op jit(solution)/shard_map/ppermute | solution.py:205
  41.3 1.3 %collective-permute-start.11 = (bf16[128,128]{1,0:T(8,128)(2,1)S(1)}, bf16[128,128]{1,0:T(8,128)(2,1)S(1)}, u32[]{:S(2)}, u32[]{:S(2)}) collective-permute-start(bf16[128,128]{1,0:T(8,128)(2,1)S(1)} %get-tuple-element.24.mine), channel_id=1, source_target_pairs={{0,4},{4,0},{8,12},{12,8},{16,20},{20,16},{24,28},{28,24},{1,5},{5... | collective-permute-start | bytes 98312 | tf_op jit(solution)/shard_map/ppermute | solution.py:205
  43.6 3.9 %collective-permute-start.12 = (f32[64,128]{1,0:T(8,128)S(1)}, f32[64,128]{1,0:T(8,128)S(1)}, u32[]{:S(2)}, u32[]{:S(2)}) collective-permute-start(f32[64,128]{1,0:T(8,128)S(1)} %last_backward.1), channel_id=1, source_target_pairs={{0,1},{1,0},{2,3},{3,2},{4,5},{5,4},{6,7},{7,6},{8,9},{9,8},{10,11... | collective-permute-start | bytes 98312 | tf_op jit(solution)/shard_map/ppermute | solution.py:205
  47.5 4.8 %collective-permute-start.13 = (f32[64,128]{1,0:T(8,128)S(1)}, f32[64,128]{1,0:T(8,128)S(1)}, u32[]{:S(2)}, u32[]{:S(2)}) collective-permute-start(f32[64,128]{1,0:T(8,128)S(1)} %add.52), channel_id=1, source_target_pairs={{0,2},{1,3},{2,0},{3,1},{4,6},{5,7},{6,4},{7,5},{8,10},{9,11},{10,... | collective-permute-start | bytes 98312 | tf_op jit(solution)/shard_map/ppermute | solution.py:205

commit v3 on v2

--- a/solution.py
+++ b/solution.py
@@ -9,7 +9,7 @@
 F32 = jnp.float32
 BF16 = jnp.bfloat16
 BLK = 128
-CHUNKS = 8
+CHUNKS = 2
 
 
 def whole(space=pltpu.VMEM):
@@ -76,28 +76,14 @@
     return acc
 
 
-def spread(rows, columns, total):
-    spots = one_hot_t(rows, total).astype(BF16)
-    out = None
-    for term in split3(columns):
-        part = dot(spots, term, ((1,), (1,)))
-        out = part if out is None else out + part
-    return out
-
-
-def backward(proj, weighted, rows, vox, vox_dev, sums):
+def products(proj, vectors, sums):
     blocks = proj.shape[0]
-    spots = one_hot_t(rows, weighted.shape[0])
-    picked = dot(spots.T.astype(BF16), weighted.astype(BF16)).astype(BF16)
     group = 16
     row = iota((group, BLK), 0)
-    stored = jnp.where(rows >= 0, 1.0, 0.0)
-    places = (one_hot_t(vox, vox_dev) * stored).astype(BF16)
     tops, lows = [], []
     for g in range(blocks // group):
-        mine = picked[g * group:(g + 1) * group].astype(F32)
-        left = [jnp.where(row == c, mine, 0.0) for c in range(group)]
-        left = jnp.concatenate(left, 1)
+        mine = vectors[g * group:(g + 1) * group]
+        left = jnp.concatenate([jnp.where(row == c, mine, 0.0) for c in range(group)], 1)
         if sums:
             ones = jnp.concatenate([jnp.where(row == c, 1.0, 0.0) for c in range(group)], 1)
             left = jnp.concatenate([left, ones], 0)
@@ -107,13 +93,29 @@
         if sums:
             lows.append(out[group:])
     columns = jnp.concatenate(tops, 0)
-    if sums:
-        columns = jnp.concatenate([columns, jnp.concatenate(lows, 0)], 1)
-    out = None
-    for term in split3(columns):
-        part = dot(places, term)
-        out = part if out is None else out + part
-    return out
+    return jnp.concatenate([columns, jnp.concatenate(lows, 0)], 1) if sums else columns
+
+
+def collect(places, columns):
+    return dot(jnp.concatenate([places] * 3, 1), jnp.concatenate(split3(columns), 0))
+
+
+def backward(proj, weighted, rows, vox, vox_dev, sums):
+    spots = one_hot_t(rows, weighted.shape[0])
+    picked = dot(spots.T.astype(BF16), weighted.astype(BF16))
+    stored = jnp.where(rows >= 0, 1.0, 0.0)
+    places = (one_hot_t(vox, vox_dev) * stored).astype(BF16)
+    return collect(places, products(proj, picked, sums))
+
+
+def forward_turned(turned, volume, rows, vox, total):
+    picked = dot(one_hot_t(vox, volume.shape[0]).T.astype(BF16), volume.astype(BF16))
+    return collect(one_hot_t(rows, total).astype(BF16), products(turned, picked, False))
+
+
+def turn_blocks(proj, turned):
+    for k in range(proj.shape[0]):
+        turned[k] = proj[k].T
 
 
 def put_partial(sums, sino, mine, theirs, ray_dev):
@@ -160,8 +162,10 @@
         rows_out[...] = rows
         total = slabs * ray_dev
         columns = forward(proj, prior[...], vox[...], True, before)
-        put_partial(spread(rows, columns[:, :blocks], total), sino[...], mine, theirs, ray_dev)
-        sums = spread(rows, columns[:, blocks:], total)
+        columns = jnp.concatenate([columns[:, :blocks].T, columns[:, blocks:].T], 1)
+        both = collect(one_hot_t(rows, total).astype(BF16), columns)
+        put_partial(both[:, :BLK], sino[...], mine, theirs, ray_dev)
+        sums = both[:, BLK:]
         core = lax.rem(lax.axis_index("slab"), 2)
         top, low = sums[:total // 2], sums[total // 2:]
         mine[total // 2:total, :] = jnp.where(core == 0, top, low)
@@ -190,8 +194,8 @@
         weight_out[...] = weights
         updated = volume[...] + weights * corr[0:vox_dev, :]
         volume_out[...] = updated
-        columns = forward(proj, updated, vox[...], False)
-        put_partial(spread(rows[...], columns, 2 * mine.shape[0]), sino[...], mine, theirs, ray_dev)
+        sums = forward_turned(proj, updated, rows[...], vox[...], 2 * mine.shape[0])
+        put_partial(sums, sino[...], mine, theirs, ray_dev)
 
     return kernel
 
@@ -218,11 +222,15 @@
     return x
 
 
-def over_angles(x):
-    slabs, angles = lax.axis_size("slab"), lax.axis_size("angle")
+def over_angles(x, direct):
+    angles = lax.axis_size("angle")
     bits = [1 << b for b in range(angles.bit_length() - 1)]
-    for bit in bits:
-        x = x + swap(x, "angle", bit)
+    while bits:
+        if len(bits) == 1 or not direct:
+            x, bits = x + swap(x, "angle", bits[0]), bits[1:]
+            continue
+        first, second, bits = bits[0], bits[1], bits[2:]
+        x = (x + swap(x, "angle", first)) + (swap(x, "angle", second) + swap(x, "angle", first | second))
     return x
 
 
@@ -259,6 +267,15 @@
         compiler_params=params,
         name="first_forward",
     )(*[x if x.size == 1 else pltpu.with_memory_space_constraint(x, pltpu.HBM) for x in arguments])
+    turned = pl.pallas_call(
+        turn_blocks,
+        out_shape=pltpu.VMEM(projector.shape, BF16),
+        in_specs=[whole()],
+        out_specs=whole(),
+        compiler_params=params,
+        cost_estimate=pl.CostEstimate(flops=0, bytes_accessed=2 * projector.size * 2, transcendentals=0),
+        name="turn_blocks",
+    )(proj)
     sums = over_slabs(mine, theirs)
     row_weight = 1.0 / jnp.maximum(sums[half:], 1.0)
     weighted = (row_weight * sums[:half]).astype(BF16)
@@ -271,7 +288,7 @@
         compiler_params=params,
         name="first_backward",
     )(proj, rows, vox, weighted, swap(weighted, "slab", 1))
-    corr = over_angles(corr)
+    corr = over_angles(corr, False)
 
     volume, col_weight, mine, theirs = pl.pallas_call(
         next_forward(ray_dev),
@@ -280,7 +297,7 @@
         out_specs=(whole(),) * 4,
         compiler_params=params,
         name="next_forward",
-    )(proj, rows, vox, volume, corr, sino)
+    )(turned, rows, vox, volume, corr, sino)
     residual = row_weight * over_slabs(mine, theirs)
     weighted = residual.astype(BF16)
     start = lax.div(lax.axis_index("slab"), 2) * ray_dev
@@ -294,7 +311,7 @@
         compiler_params=params,
         name="last_backward",
     )(proj, rows, vox, weighted, swap(weighted, "slab", 1))
-    corr = over_angles(corr)
+    corr = over_angles(corr, False)
     return volume + col_weight * corr, residual
 
 

time: 53.1 us -> 51.2 us (0.964)
  waiting for transfers between devices: 24 us -> 22.9 us
  Pallas kernels: 8.88 us -> 7.98 us
    pallas_call x1, Pallas kernels: 5.12 us -> 3.77 us  [local(): pl.pallas_call(first_forward(slabs, capacity, ray_dev), out_shape=(pltpu....]
    pallas_call x0 -> x1, Pallas kernels: none -> 1.13 us  [local(): pl.pallas_call(turn_blocks, out_shape=pltpu.VMEM(projector.shape, BF16),...]
    ppermute x14, waiting for transfers between devices: 24 us -> 22.9 us  [swap(): return lax.ppermute(x, axis, [(i, i ^ bit) for i in range(size)])]
    pallas_call x1, Pallas kernels: 1.71 us -> 1.06 us  [local(): pl.pallas_call(next_forward(ray_dev), out_shape=(vmem(vox_dev), vmem(vox_...]
  transfers between devices with their start and end apart: 14 -> 14, of which waited for: 13 -> 13; matrix products, arithmetic and copies ran while one was open for 1% -> 1% of each run, Pallas kernels for 0% -> 2%
where the time goes in v3:
time: 51.2 us; the launch traced here: 51 us
  waiting for transfers between devices  22.9 us (45%)
  starting transfers between devices  17.4 us (34%)
  Pallas kernels  7.98 us (16%)
  between operations  1.37 us (3%)
  other arithmetic  0.76 us (1%)
  local copies, waits for them, and re-layouts  0.61 us (1%)
    ppermute x14, waiting for transfers between devices, swap(): return lax.ppermute(x, axis, [(i, i ^ bit) for i in range(size)])  22.9 us
    ppermute x14, starting transfers between devices, swap(): return lax.ppermute(x, axis, [(i, i ^ bit) for i in range(size)])  17.4 us
    pallas_call x1, Pallas kernels, local(): pl.pallas_call(first_forward(slabs, capacity, ray_dev), out_shape=(pltpu....  3.77 us
    pallas_call x1, Pallas kernels, local(): pl.pallas_call(turn_blocks, out_shape=pltpu.VMEM(projector.shape, BF16),...  1.13 us
    pallas_call x1, Pallas kernels, local(): pl.pallas_call(next_forward(ray_dev), out_shape=(vmem(vox_dev), vmem(vox_...  1.06 us
    pallas_call x1, Pallas kernels, local(): pl.pallas_call(first_backward, out_shape=vmem(2 * vox_dev), in_specs=[who...  1.03 us
  transfers between devices with their start and end apart: 14, of which 13 were waited for; matrix products, arithmetic and copies ran while one was open for 1% of the time, Pallas kernels for 2%

profile of v3, /device:TPU:0, one launch (start us, length us, event | category | flops | bytes accessed | tf_op | source)
XLA Modules:
  0.0 51.0 jit_solution(8320174208017541789)
XLA Ops:
  1.3 3.8 %first_forward.1 = (bf16[128,128,128]{2,1,0:T(8,128)(2,1)S(1)}, s32[1,128]{1,0:T(1,128)S(1)}, s32[1,128]{1,0:T(1,128)S(1)}, f32[64,128]{1,0:T(8,128)S(1)}, f32[3...) custom-call(bf16[128,128,128]{2,1,0:T(8,128)(2,1)} %proj_hbm.1, s32[1,128]{1,0:T(1,128)} %bitcast.4, ...), custom_call_target="tpu_custom_call" | custom-call | tf_op jit(solution)/shard_map/first_forward/pallas_call | solution.py:252
  5.1 0.5 %collective-permute-start = (f32[256,128]{1,0:T(8,128)S(1)}, f32[256,128]{1,0:T(8,128)S(1)}, u32[]{:S(2)}, u32[]{:S(2)}) collective-permute-start(f32[256,128]{1,0:T(8,128)S(1)} %get-tuple-element.18), channel_id=1, source_target_pairs={{0,4},{4,0},{8,12},{12,8},{16,20},{20,16},{24,28},{28,24},{1,5},{5... | collective-permute-start | bytes 393224 | tf_op jit(solution)/shard_map/ppermute | solution.py:209
  5.6 1.0 %collective-permute-done = f32[256,128]{1,0:T(8,128)S(1)} collective-permute-done((f32[256,128]{1,0:T(8,128)S(1)}, f32[256,128]{1,0:T(8,128)S(1)}, u32[]{:S(2)}, u32[]{:S(2)}) %collective-permute-start) | collective-permute-done | bytes 131104 | tf_op jit(solution)/shard_map/ppermute | solution.py:209
  6.6 2.9 %collective-permute-start.1 = (f32[256,128]{1,0:T(8,128)S(1)}, f32[256,128]{1,0:T(8,128)S(1)}, u32[]{:S(2)}, u32[]{:S(2)}) collective-permute-start(f32[256,128]{1,0:T(8,128)S(1)} %add.42), channel_id=1, source_target_pairs={{0,8},{4,12},{8,0},{12,4},{16,24},{20,28},{24,16},{28,20},{1,9},{5... | collective-permute-start | bytes 393224 | tf_op jit(solution)/shard_map/ppermute | solution.py:209
  9.5 1.5 %collective-permute-start.2 = (f32[256,128]{1,0:T(8,128)S(1)}, f32[256,128]{1,0:T(8,128)S(1)}, u32[]{:S(2)}, u32[]{:S(2)}) collective-permute-start(f32[256,128]{1,0:T(8,128)S(1)} %add.42), channel_id=1, source_target_pairs={{0,16},{4,20},{8,24},{12,28},{16,0},{20,4},{24,8},{28,12},{1,17},{... | collective-permute-start | bytes 393224 | tf_op jit(solution)/shard_map/ppermute | solution.py:209
  11.0 2.4 %collective-permute-done.1 = f32[256,128]{1,0:T(8,128)S(1)} collective-permute-done((f32[256,128]{1,0:T(8,128)S(1)}, f32[256,128]{1,0:T(8,128)S(1)}, u32[]{:S(2)}, u32[]{:S(2)}) %collective-permute-start.1) | collective-permute-done | bytes 131104 | tf_op jit(solution)/shard_map/ppermute | solution.py:209
  13.4 4.2 %collective-permute-done.2 = f32[256,128]{1,0:T(8,128)S(1)} collective-permute-done((f32[256,128]{1,0:T(8,128)S(1)}, f32[256,128]{1,0:T(8,128)S(1)}, u32[]{:S(2)}, u32[]{:S(2)}) %collective-permute-start.2) | collective-permute-done | bytes 131104 | tf_op jit(solution)/shard_map/ppermute | solution.py:209
  17.6 0.1 collective-permute-start.4
  17.7 1.2 %collective-permute-done.4.theirs = bf16[128,128]{1,0:T(8,128)(2,1)S(1)} collective-permute-done((bf16[128,128]{1,0:T(8,128)(2,1)S(1)}, bf16[128,128]{1,0:T(8,128)(2,1)S(1)}, u32[]{:S(2)}, u32[]{:S(2)}) %collective-permute-start.4) | collective-permute-done | bytes 32800 | tf_op jit(solution)/shard_map/ppermute | solution.py:209
  18.9 1.0 %first_backward.1 = f32[128,128]{1,0:T(8,128)S(1)} custom-call(bf16[128,128,128]{2,1,0:T(8,128)(2,1)S(1)} %get-tuple-element.13.proj, s32[1,128]{1,0:T(1,128)S(1)} %get-tuple-element.14.rows, s32[1,128]{1,0:T(1,128)S(1)} %get-tuple-element.15.vox, bf16[128,128]{1,0:T(8,128)(2,1)S(1)} %fusion.mine, bf16[128,128]{1,0:T(8,128)(2,1)S(1)} %collective-permute-done.4.theirs), custom_call_target="tpu_custom_call" | custom-call | tf_op jit(solution)/shard_map/first_backward/pallas_call | solution.py:283
  20.0 1.6 %collective-permute-start.5 = (f32[128,128]{1,0:T(8,128)S(1)}, f32[128,128]{1,0:T(8,128)S(1)}, u32[]{:S(2)}, u32[]{:S(2)}) collective-permute-start(f32[128,128]{1,0:T(8,128)S(1)} %first_backward.1), channel_id=1, source_target_pairs={{0,1},{1,0},{2,3},{3,2},{4,5},{5,4},{6,7},{7,6},{8,9},{9,8},{10,11... | collective-permute-start | bytes 196616 | tf_op jit(solution)/shard_map/ppermute | solution.py:209
  21.6 2.7 %collective-permute-done.5 = f32[128,128]{1,0:T(8,128)S(1)} collective-permute-done((f32[128,128]{1,0:T(8,128)S(1)}, f32[128,128]{1,0:T(8,128)S(1)}, u32[]{:S(2)}, u32[]{:S(2)}) %collective-permute-start.5) | collective-permute-done | bytes 65568 | tf_op jit(solution)/shard_map/ppermute | solution.py:209
  24.3 2.7 %collective-permute-start.6 = (f32[128,128]{1,0:T(8,128)S(1)}, f32[128,128]{1,0:T(8,128)S(1)}, u32[]{:S(2)}, u32[]{:S(2)}) collective-permute-start(f32[128,128]{1,0:T(8,128)S(1)} %add.46), channel_id=1, source_target_pairs={{0,2},{1,3},{2,0},{3,1},{4,6},{5,7},{6,4},{7,5},{8,10},{9,11},{10,... | collective-permute-start | bytes 196616 | tf_op jit(solution)/shard_map/ppermute | solution.py:209
  27.0 1.1 %turn_blocks.1.proj = bf16[128,128,128]{2,1,0:T(8,128)(2,1)S(1)} custom-call(bf16[128,128,128]{2,1,0:T(8,128)(2,1)S(1)} %get-tuple-element.13.proj), custom_call_target="tpu_custom_call" | custom-call | bytes 8388608 | tf_op jit(solution)/shard_map/turn_blocks/pallas_call | solution.py:270
  28.1 1.4 %collective-permute-done.6 = f32[128,128]{1,0:T(8,128)S(1)} collective-permute-done((f32[128,128]{1,0:T(8,128)S(1)}, f32[128,128]{1,0:T(8,128)S(1)}, u32[]{:S(2)}, u32[]{:S(2)}) %collective-permute-start.6) | collective-permute-done | bytes 65568 | tf_op jit(solution)/shard_map/ppermute | solution.py:209
  29.5 1.1 %next_forward.1 = (f32[64,128]{1,0:T(8,128)S(1)}, f32[64,128]{1,0:T(8,128)S(1)}, f32[128,128]{1,0:T(8,128)S(1)}, f32[128,128]{1,0:T(8,128)S(1)}) custom-call(bf16[128,128,128]{2,1,0:T(8,128)(2,1)S(1)} %turn_blocks.1.proj, s32[1,128]{1,0:T(1,128)S(1)} %get-tuple-element.14.rows, s32[1,128]{1,0:T(1,128)S(1)} %get-tuple-element.15.vox, ...), custom_call_target="tpu_custom_call" | custom-call | tf_op jit(solution)/shard_map/next_forward/pallas_call | solution.py:293
  30.6 0.1 collective-permute-start.7
  30.7 1.2 %collective-permute-done.7 = f32[128,128]{1,0:T(8,128)S(1)} collective-permute-done((f32[128,128]{1,0:T(8,128)S(1)}, f32[128,128]{1,0:T(8,128)S(1)}, u32[]{:S(2)}, u32[]{:S(2)}) %collective-permute-start.7) | collective-permute-done | bytes 65568 | tf_op jit(solution)/shard_map/ppermute | solution.py:209
  31.9 1.5 %collective-permute-start.10 = (f32[128,128]{1,0:T(8,128)S(1)}, f32[128,128]{1,0:T(8,128)S(1)}, u32[]{:S(2)}, u32[]{:S(2)}) collective-permute-start(f32[128,128]{1,0:T(8,128)S(1)} %add.48), channel_id=1, source_target_pairs={{0,24},{4,28},{8,16},{12,20},{16,8},{20,12},{24,0},{28,4},{1,25},{... | collective-permute-start | bytes 196616 | tf_op jit(solution)/shard_map/ppermute | solution.py:209
  33.5 1.5 %collective-permute-start.8 = (f32[128,128]{1,0:T(8,128)S(1)}, f32[128,128]{1,0:T(8,128)S(1)}, u32[]{:S(2)}, u32[]{:S(2)}) collective-permute-start(f32[128,128]{1,0:T(8,128)S(1)} %add.48), channel_id=1, source_target_pairs={{0,8},{4,12},{8,0},{12,4},{16,24},{20,28},{24,16},{28,20},{1,9},{5... | collective-permute-start | bytes 196616 | tf_op jit(solution)/shard_map/ppermute | solution.py:209
  35.0 0.5 collective-permute-start.9
  35.5 2.2 %collective-permute-done.10 = f32[128,128]{1,0:T(8,128)S(1)} collective-permute-done((f32[128,128]{1,0:T(8,128)S(1)}, f32[128,128]{1,0:T(8,128)S(1)}, u32[]{:S(2)}, u32[]{:S(2)}) %collective-permute-start.10) | collective-permute-done | bytes 65568 | tf_op jit(solution)/shard_map/ppermute | solution.py:209
  37.7 0.8 %collective-permute-done.8 = f32[128,128]{1,0:T(8,128)S(1)} collective-permute-done((f32[128,128]{1,0:T(8,128)S(1)}, f32[128,128]{1,0:T(8,128)S(1)}, u32[]{:S(2)}, u32[]{:S(2)}) %collective-permute-start.8) | collective-permute-done | bytes 65568 | tf_op jit(solution)/shard_map/ppermute | solution.py:209
  38.5 0.7 %collective-permute-done.9 = f32[128,128]{1,0:T(8,128)S(1)} collective-permute-done((f32[128,128]{1,0:T(8,128)S(1)}, f32[128,128]{1,0:T(8,128)S(1)}, u32[]{:S(2)}, u32[]{:S(2)}) %collective-permute-start.9) | collective-permute-done | bytes 65568 | tf_op jit(solution)/shard_map/ppermute | solution.py:209
  39.4 1.2 %collective-permute-done.11.theirs = bf16[128,128]{1,0:T(8,128)(2,1)S(1)} collective-permute-done((bf16[128,128]{1,0:T(8,128)(2,1)S(1)}, bf16[128,128]{1,0:T(8,128)(2,1)S(1)}, u32[]{:S(2)}, u32[]{:S(2)}) %collective-permute-start.11) | collective-permute-done | bytes 32800 | tf_op jit(solution)/shard_map/ppermute | solution.py:209
  40.6 1.0 %last_backward.1 = f32[64,128]{1,0:T(8,128)S(1)} custom-call(bf16[128,128,128]{2,1,0:T(8,128)(2,1)S(1)} %get-tuple-element.13.proj, s32[1,128]{1,0:T(1,128)S(1)} %get-tuple-element.14.rows, s32[1,128]{1,0:T(1,128)S(1)} %get-tuple-element.15.vox, bf16[128,128]{1,0:T(8,128)(2,1)S(1)} %get-tuple-element.24.mine, bf16[128,128]{1,0:T(8,128)(2,1)S(1)} %collective-permute-done.11.theirs), custom_call_target="tpu_custom_call" | custom-call | tf_op jit(solution)/shard_map/last_backward/pallas_call | solution.py:306
  41.6 1.6 %collective-permute-start.12 = (f32[64,128]{1,0:T(8,128)S(1)}, f32[64,128]{1,0:T(8,128)S(1)}, u32[]{:S(2)}, u32[]{:S(2)}) collective-permute-start(f32[64,128]{1,0:T(8,128)S(1)} %last_backward.1), channel_id=1, source_target_pairs={{0,1},{1,0},{2,3},{3,2},{4,5},{5,4},{6,7},{7,6},{8,9},{9,8},{10,11... | collective-permute-start | bytes 98312 | tf_op jit(solution)/shard_map/ppermute | solution.py:209
  43.2 2.3 %collective-permute-done.12 = f32[64,128]{1,0:T(8,128)S(1)} collective-permute-done((f32[64,128]{1,0:T(8,128)S(1)}, f32[64,128]{1,0:T(8,128)S(1)}, u32[]{:S(2)}, u32[]{:S(2)}) %collective-permute-start.12) | collective-permute-done | bytes 32800 | tf_op jit(solution)/shard_map/ppermute | solution.py:209
  45.6 2.7 %collective-permute-start.13 = (f32[64,128]{1,0:T(8,128)S(1)}, f32[64,128]{1,0:T(8,128)S(1)}, u32[]{:S(2)}, u32[]{:S(2)}) collective-permute-start(f32[64,128]{1,0:T(8,128)S(1)} %add.52), channel_id=1, source_target_pairs={{0,2},{1,3},{2,0},{3,1},{4,6},{5,7},{6,4},{7,5},{8,10},{9,11},{10,... | collective-permute-start | bytes 98312 | tf_op jit(solution)/shard_map/ppermute | solution.py:209
  48.3 0.6 %constant_dynamic-slice_fusion = f32[32,128]{1,0:T(8,128)} fusion(f32[128,128]{1,0:T(8,128)S(1)} %get-tuple-element.25, s32[]{:T(128)S(6)} %select_n.3), kind=kLoop, calls=%fused_computation.7 | loop fusion | bytes 32772 | tf_op jit(solution)/shard_map/dynamic_slice | solution.py:304
  48.9 1.5 %collective-permute-done.13 = f32[64,128]{1,0:T(8,128)S(1)} collective-permute-done((f32[64,128]{1,0:T(8,128)S(1)}, f32[64,128]{1,0:T(8,128)S(1)}, u32[]{:S(2)}, u32[]{:S(2)}) %collective-permute-start.13) | collective-permute-done | bytes 32800 | tf_op jit(solution)/shard_map/ppermute | solution.py:209
  50.4 0.6 %multiply_add_fusion = f32[64,128]{1,0:T(8,128)} fusion(f32[64,128]{1,0:T(8,128)S(1)} %get-tuple-element.20, f32[64,128]{1,0:T(8,128)S(1)} %get-tuple-element.21, f32[64,128]{1,0:T(8,128)S(1)} %add.52, f32[64,128]{1,0:T(8,128)S(1)} %collective-permute-done.13), kind=kLoop, calls=%fused_computation.6 | loop fusion | flops 24576 | bytes 163840 | tf_op jit(solution)/shard_map/add | solution.py:315
  (11 shorter events, 0.2 us)
Async XLA Ops:
  5.1 1.5 %collective-permute-start = (f32[256,128]{1,0:T(8,128)S(1)}, f32[256,128]{1,0:T(8,128)S(1)}, u32[]{:S(2)}, u32[]{:S(2)}) collective-permute-start(f32[256,128]{1,0:T(8,128)S(1)} %get-tuple-element.18), channel_id=1, source_target_pairs={{0,4},{4,0},{8,12},{12,8},{16,20},{20,16},{24,28},{28,24},{1,5},{5... | collective-permute-start | bytes 393224 | tf_op jit(solution)/shard_map/ppermute | solution.py:209
  6.6 6.8 %collective-permute-start.1 = (f32[256,128]{1,0:T(8,128)S(1)}, f32[256,128]{1,0:T(8,128)S(1)}, u32[]{:S(2)}, u32[]{:S(2)}) collective-permute-start(f32[256,128]{1,0:T(8,128)S(1)} %add.42), channel_id=1, source_target_pairs={{0,8},{4,12},{8,0},{12,4},{16,24},{20,28},{24,16},{28,20},{1,9},{5... | collective-permute-start | bytes 393224 | tf_op jit(solution)/shard_map/ppermute | solution.py:209
  9.5 8.1 %collective-permute-start.2 = (f32[256,128]{1,0:T(8,128)S(1)}, f32[256,128]{1,0:T(8,128)S(1)}, u32[]{:S(2)}, u32[]{:S(2)}) collective-permute-start(f32[256,128]{1,0:T(8,128)S(1)} %add.42), channel_id=1, source_target_pairs={{0,16},{4,20},{8,24},{12,28},{16,0},{20,4},{24,8},{28,12},{1,17},{... | collective-permute-start | bytes 393224 | tf_op jit(solution)/shard_map/ppermute | solution.py:209
  11.0 6.6 %collective-permute-start.3 = (f32[256,128]{1,0:T(8,128)S(1)}, f32[256,128]{1,0:T(8,128)S(1)}, u32[]{:S(2)}, u32[]{:S(2)}) collective-permute-start(f32[256,128]{1,0:T(8,128)S(1)} %add.42), channel_id=1, source_target_pairs={{0,24},{4,28},{8,16},{12,20},{16,8},{20,12},{24,0},{28,4},{1,25},{... | collective-permute-start | bytes 393224 | tf_op jit(solution)/shard_map/ppermute | solution.py:209
  17.6 1.3 %collective-permute-start.4 = (bf16[128,128]{1,0:T(8,128)(2,1)S(1)}, bf16[128,128]{1,0:T(8,128)(2,1)S(1)}, u32[]{:S(2)}, u32[]{:S(2)}) collective-permute-start(bf16[128,128]{1,0:T(8,128)(2,1)S(1)} %fusion.mine), channel_id=1, source_target_pairs={{0,4},{4,0},{8,12},{12,8},{16,20},{20,16},{24,28},{28,24},{1,5},{5... | collective-permute-start | bytes 98312 | tf_op jit(solution)/shard_map/ppermute | solution.py:209
  20.0 4.3 %collective-permute-start.5 = (f32[128,128]{1,0:T(8,128)S(1)}, f32[128,128]{1,0:T(8,128)S(1)}, u32[]{:S(2)}, u32[]{:S(2)}) collective-permute-start(f32[128,128]{1,0:T(8,128)S(1)} %first_backward.1), channel_id=1, source_target_pairs={{0,1},{1,0},{2,3},{3,2},{4,5},{5,4},{6,7},{7,6},{8,9},{9,8},{10,11... | collective-permute-start | bytes 196616 | tf_op jit(solution)/shard_map/ppermute | solution.py:209
  24.3 5.2 %collective-permute-start.6 = (f32[128,128]{1,0:T(8,128)S(1)}, f32[128,128]{1,0:T(8,128)S(1)}, u32[]{:S(2)}, u32[]{:S(2)}) collective-permute-start(f32[128,128]{1,0:T(8,128)S(1)} %add.46), channel_id=1, source_target_pairs={{0,2},{1,3},{2,0},{3,1},{4,6},{5,7},{6,4},{7,5},{8,10},{9,11},{10,... | collective-permute-start | bytes 196616 | tf_op jit(solution)/shard_map/ppermute | solution.py:209
  30.6 1.3 %collective-permute-start.7 = (f32[128,128]{1,0:T(8,128)S(1)}, f32[128,128]{1,0:T(8,128)S(1)}, u32[]{:S(2)}, u32[]{:S(2)}) collective-permute-start(f32[128,128]{1,0:T(8,128)S(1)} %get-tuple-element.23), channel_id=1, source_target_pairs={{0,4},{4,0},{8,12},{12,8},{16,20},{20,16},{24,28},{28,24},{1,5},{5... | collective-permute-start | bytes 196616 | tf_op jit(solution)/shard_map/ppermute | solution.py:209
  31.9 5.8 %collective-permute-start.10 = (f32[128,128]{1,0:T(8,128)S(1)}, f32[128,128]{1,0:T(8,128)S(1)}, u32[]{:S(2)}, u32[]{:S(2)}) collective-permute-start(f32[128,128]{1,0:T(8,128)S(1)} %add.48), channel_id=1, source_target_pairs={{0,24},{4,28},{8,16},{12,20},{16,8},{20,12},{24,0},{28,4},{1,25},{... | collective-permute-start | bytes 196616 | tf_op jit(solution)/shard_map/ppermute | solution.py:209
  33.5 5.0 %collective-permute-start.8 = (f32[128,128]{1,0:T(8,128)S(1)}, f32[128,128]{1,0:T(8,128)S(1)}, u32[]{:S(2)}, u32[]{:S(2)}) collective-permute-start(f32[128,128]{1,0:T(8,128)S(1)} %add.48), channel_id=1, source_target_pairs={{0,8},{4,12},{8,0},{12,4},{16,24},{20,28},{24,16},{28,20},{1,9},{5... | collective-permute-start | bytes 196616 | tf_op jit(solution)/shard_map/ppermute | solution.py:209
  35.0 4.3 %collective-permute-start.9 = (f32[128,128]{1,0:T(8,128)S(1)}, f32[128,128]{1,0:T(8,128)S(1)}, u32[]{:S(2)}, u32[]{:S(2)}) collective-permute-start(f32[128,128]{1,0:T(8,128)S(1)} %add.48), channel_id=1, source_target_pairs={{0,16},{4,20},{8,24},{12,28},{16,0},{20,4},{24,8},{28,12},{1,17},{... | collective-permute-start | bytes 196616 | tf_op jit(solution)/shard_map/ppermute | solution.py:209
  39.3 1.3 %collective-permute-start.11 = (bf16[128,128]{1,0:T(8,128)(2,1)S(1)}, bf16[128,128]{1,0:T(8,128)(2,1)S(1)}, u32[]{:S(2)}, u32[]{:S(2)}) collective-permute-start(bf16[128,128]{1,0:T(8,128)(2,1)S(1)} %get-tuple-element.24.mine), channel_id=1, source_target_pairs={{0,4},{4,0},{8,12},{12,8},{16,20},{20,16},{24,28},{28,24},{1,5},{5... | collective-permute-start | bytes 98312 | tf_op jit(solution)/shard_map/ppermute | solution.py:209
  41.6 4.0 %collective-permute-start.12 = (f32[64,128]{1,0:T(8,128)S(1)}, f32[64,128]{1,0:T(8,128)S(1)}, u32[]{:S(2)}, u32[]{:S(2)}) collective-permute-start(f32[64,128]{1,0:T(8,128)S(1)} %last_backward.1), channel_id=1, source_target_pairs={{0,1},{1,0},{2,3},{3,2},{4,5},{5,4},{6,7},{7,6},{8,9},{9,8},{10,11... | collective-permute-start | bytes 98312 | tf_op jit(solution)/shard_map/ppermute | solution.py:209
  45.6 4.8 %collective-permute-start.13 = (f32[64,128]{1,0:T(8,128)S(1)}, f32[64,128]{1,0:T(8,128)S(1)}, u32[]{:S(2)}, u32[]{:S(2)}) collective-permute-start(f32[64,128]{1,0:T(8,128)S(1)} %add.52), channel_id=1, source_target_pairs={{0,2},{1,3},{2,0},{3,1},{4,6},{5,7},{6,4},{7,5},{8,10},{9,11},{10,... | collective-permute-start | bytes 98312 | tf_op jit(solution)/shard_map/ppermute | solution.py:209

commit v4 on v3

--- a/solution.py
+++ b/solution.py
@@ -49,30 +49,22 @@
     return jnp.where(stored, place * ray_dev + ray, -1)
 
 
-def forward(proj, volume, vox, sums, before=None):
+def forward(proj, volume, vox, before):
     blocks = proj.shape[0]
-    half = blocks // 2
+    part = blocks // (2 * CHUNKS)
     picked = dot(volume.T.astype(BF16), one_hot_t(vox, volume.shape[0]).astype(BF16))
-    lane = iota((BLK, blocks), 1)
-    weights = jnp.concatenate([jnp.where(lane < half, picked, 0.0), jnp.where(lane >= half, picked, 0.0)], 0)
-    if sums:
-        ones = jnp.concatenate([jnp.where(lane < half, 1.0, 0.0), jnp.where(lane >= half, 1.0, 0.0)], 0)
-        weights = jnp.concatenate([weights, ones], 1)
-    weights = weights.astype(BF16)
-    width = weights.shape[1]
-    column = lax.rem(iota((BLK, width), 1), half)
-
-    def step(p, acc):
-        pair = jnp.concatenate([proj[p], proj[p + half]], 1)
-        return jnp.where(column == p, dot(pair, weights), acc)
-
-    acc = jnp.zeros((BLK, width), F32)
-    per = half // CHUNKS
+    first = lax.rem(iota((BLK, blocks), 1), 2 * part) < part
+    halves = [jnp.where(side, jnp.concatenate([picked, jnp.ones_like(picked)], 1), 0.0)
+              for side in (jnp.concatenate([first] * 2, 1), ~jnp.concatenate([first] * 2, 1))]
+    weights = jnp.concatenate(halves, 0).astype(BF16)
+    lane = lax.rem(iota((BLK, 2 * blocks), 1), blocks)
+    column = lane - jnp.where(lax.rem(lane, 2 * part) < part, 0, part)
+    acc = jnp.zeros((BLK, 2 * blocks), F32)
     for c in range(CHUNKS):
-        if before is not None:
-            before(c)
-        for p in range(c * per, (c + 1) * per):
-            acc = step(p, acc)
+        before(c)
+        for k in range(2 * part * c, 2 * part * c + part):
+            pair = jnp.concatenate([proj[k], proj[k + part]], 1)
+            acc = jnp.where(column == k, dot(pair, weights), acc)
     return acc
 
 
@@ -100,17 +92,21 @@
     return dot(jnp.concatenate([places] * 3, 1), jnp.concatenate(split3(columns), 0))
 
 
-def backward(proj, weighted, rows, vox, vox_dev, sums):
-    spots = one_hot_t(rows, weighted.shape[0])
-    picked = dot(spots.T.astype(BF16), weighted.astype(BF16))
-    stored = jnp.where(rows >= 0, 1.0, 0.0)
-    places = (one_hot_t(vox, vox_dev) * stored).astype(BF16)
-    return collect(places, products(proj, picked, sums))
-
-
-def forward_turned(turned, volume, rows, vox, total):
-    picked = dot(one_hot_t(vox, volume.shape[0]).T.astype(BF16), volume.astype(BF16))
-    return collect(one_hot_t(rows, total).astype(BF16), products(turned, picked, False))
+def backward(proj, weighted, picks, places, sums):
+    return collect(places, products(proj, dot(picks, weighted), sums))
+
+
+def forward_turned(turned, volume, picks, places):
+    return collect(places, products(turned, dot(picks, volume.astype(BF16)), False))
+
+
+def name_places(rows, vox, from_rays, to_rays, from_vox, to_vox):
+    spots = one_hot_t(rows[...], to_rays.shape[0])
+    from_rays[...] = spots.T.astype(BF16)
+    to_rays[...] = spots.astype(BF16)
+    spots = one_hot_t(vox[...], to_vox.shape[0])
+    from_vox[...] = spots.T.astype(BF16)
+    to_vox[...] = (spots * jnp.where(rows[...] >= 0, 1.0, 0.0)).astype(BF16)
 
 
 def turn_blocks(proj, turned):
@@ -142,26 +138,26 @@
                 (prior_hbm, prior), (sino_hbm, sino),
             ])
         ]
-        for copy in smalls:
+        copies = []
+        size = blocks // CHUNKS
+        for c in range(CHUNKS):
+            at = pl.ds(c * size, size)
+            copy = pltpu.make_async_copy(proj_hbm.at[at], proj.at[at], sems.at[c])
             copy.start()
-        copies = []
-        for c in range(CHUNKS):
-            for h in range(2):
-                at = pl.ds(h * half + c * per, per)
-                copy = pltpu.make_async_copy(proj_hbm.at[at], proj.at[at], sems.at[2 * c + h])
-                copy.start()
-                copies.append(copy)
+            copies.append(copy)
+            if not c:
+                for copy in smalls:
+                    copy.start()
         for copy in smalls:
             copy.wait()
 
         def before(c):
-            copies[2 * c].wait()
-            copies[2 * c + 1].wait()
+            copies[c].wait()
 
         rows = block_rows(slot[...], ray[...], count[...], slabs, capacity, ray_dev)
         rows_out[...] = rows
         total = slabs * ray_dev
-        columns = forward(proj, prior[...], vox[...], True, before)
+        columns = forward(proj, prior[...], vox[...], before)
         columns = jnp.concatenate([columns[:, :blocks].T, columns[:, blocks:].T], 1)
         both = collect(one_hot_t(rows, total).astype(BF16), columns)
         put_partial(both[:, :BLK], sino[...], mine, theirs, ray_dev)
@@ -180,28 +176,28 @@
     return jnp.concatenate([jnp.where(core == 0, mine, theirs), jnp.where(core == 0, theirs, mine)], 0)
 
 
-def first_backward(proj, rows, vox, mine, theirs, corr):
+def first_backward(proj, picks, places, mine, theirs, corr):
     vox_dev = corr.shape[0] // 2
-    both = backward(proj, join_halves(mine, theirs), rows[...], vox[...], vox_dev, True)
+    both = backward(proj, join_halves(mine, theirs), picks[...], places[...], True)
     corr[0:vox_dev, :] = both[:, :BLK]
     corr[vox_dev:2 * vox_dev, :] = both[:, BLK:]
 
 
 def next_forward(ray_dev):
-    def kernel(proj, rows, vox, volume, corr, sino, volume_out, weight_out, mine, theirs):
+    def kernel(proj, picks, places, volume, corr, sino, volume_out, weight_out, mine, theirs):
         vox_dev = volume.shape[0]
         weights = 1.0 / jnp.maximum(corr[vox_dev:2 * vox_dev, :], 1.0)
         weight_out[...] = weights
         updated = volume[...] + weights * corr[0:vox_dev, :]
         volume_out[...] = updated
-        sums = forward_turned(proj, updated, rows[...], vox[...], 2 * mine.shape[0])
+        sums = forward_turned(proj, updated, picks[...], places[...])
         put_partial(sums, sino[...], mine, theirs, ray_dev)
 
     return kernel
 
 
-def last_backward(proj, rows, vox, mine, theirs, corr):
-    corr[...] = backward(proj, join_halves(mine, theirs), rows[...], vox[...], corr.shape[0], False)
+def last_backward(proj, picks, places, mine, theirs, corr):
+    corr[...] = backward(proj, join_halves(mine, theirs), picks[...], places[...], False)
 
 
 def swap(x, axis, bit):
@@ -267,6 +263,18 @@
         compiler_params=params,
         name="first_forward",
     )(*[x if x.size == 1 else pltpu.with_memory_space_constraint(x, pltpu.HBM) for x in arguments])
+    from_rays, to_rays, from_vox, to_vox = pl.pallas_call(
+        name_places,
+        out_shape=(
+            pltpu.VMEM((blocks, 2 * half), BF16), pltpu.VMEM((2 * half, blocks), BF16),
+            pltpu.VMEM((blocks, vox_dev), BF16), pltpu.VMEM((vox_dev, blocks), BF16),
+        ),
+        in_specs=[whole()] * 2,
+        out_specs=(whole(),) * 4,
+        compiler_params=params,
+        cost_estimate=pl.CostEstimate(flops=0, bytes_accessed=1 << 20, transcendentals=0),
+        name="name_places",
+    )(rows, vox)
     turned = pl.pallas_call(
         turn_blocks,
         out_shape=pltpu.VMEM(projector.shape, BF16),
@@ -287,7 +295,7 @@
         out_specs=whole(),
         compiler_params=params,
         name="first_backward",
-    )(proj, rows, vox, weighted, swap(weighted, "slab", 1))
+    )(proj, from_rays, to_vox, weighted, swap(weighted, "slab", 1))
     corr = over_angles(corr, False)
 
     volume, col_weight, mine, theirs = pl.pallas_call(
@@ -297,7 +305,7 @@
         out_specs=(whole(),) * 4,
         compiler_params=params,
         name="next_forward",
-    )(turned, rows, vox, volume, corr, sino)
+    )(turned, from_vox, to_rays, volume, corr, sino)
     residual = row_weight * over_slabs(mine, theirs)
     weighted = residual.astype(BF16)
     start = lax.div(lax.axis_index("slab"), 2) * ray_dev
@@ -310,7 +318,7 @@
         out_specs=whole(),
         compiler_params=params,
         name="last_backward",
-    )(proj, rows, vox, weighted, swap(weighted, "slab", 1))
+    )(proj, from_rays, to_vox, weighted, swap(weighted, "slab", 1))
     corr = over_angles(corr, False)
     return volume + col_weight * corr, residual
 

time: 51.2 us -> 50.7 us (level)
  no operation moved by 1% of the time
where the time goes in v4:
time: 50.7 us; the launch traced here: 50.6 us
  waiting for transfers between devices  22.8 us (45%)
  starting transfers between devices  17.4 us (34%)
  Pallas kernels  7.66 us (15%)
  between operations  1.39 us (3%)
  other arithmetic  0.75 us (1%)
  local copies, waits for them, and re-layouts  0.61 us (1%)
    ppermute x14, waiting for transfers between devices, swap(): return lax.ppermute(x, axis, [(i, i ^ bit) for i in range(size)])  22.8 us
    ppermute x14, starting transfers between devices, swap(): return lax.ppermute(x, axis, [(i, i ^ bit) for i in range(size)])  17.4 us
    pallas_call x1, Pallas kernels, local(): pl.pallas_call(first_forward(slabs, capacity, ray_dev), out_shape=(pltpu....  3.48 us
    pallas_call x1, Pallas kernels, local(): pl.pallas_call(turn_blocks, out_shape=pltpu.VMEM(projector.shape, BF16),...  1.13 us
  transfers between devices with their start and end apart: 14, of which 13 were waited for; matrix products, arithmetic and copies ran while one was open for 1% of the time, Pallas kernels for 2%

profile of v4, /device:TPU:0, one launch (start us, length us, event | category | flops | bytes accessed | tf_op | source)
XLA Modules:
  0.0 50.6 jit_solution(17334341218979288954)
XLA Ops:
  1.3 3.5 %first_forward.1 = (bf16[128,128,128]{2,1,0:T(8,128)(2,1)S(1)}, s32[1,128]{1,0:T(1,128)S(1)}, s32[1,128]{1,0:T(1,128)S(1)}, f32[64,128]{1,0:T(8,128)S(1)}, f32[3...) custom-call(bf16[128,128,128]{2,1,0:T(8,128)(2,1)} %proj_hbm.1, s32[1,128]{1,0:T(1,128)} %bitcast.4, ...), custom_call_target="tpu_custom_call" | custom-call | tf_op jit(solution)/shard_map/first_forward/pallas_call | solution.py:248
  4.8 0.5 %collective-permute-start = (f32[256,128]{1,0:T(8,128)S(1)}, f32[256,128]{1,0:T(8,128)S(1)}, u32[]{:S(2)}, u32[]{:S(2)}) collective-permute-start(f32[256,128]{1,0:T(8,128)S(1)} %get-tuple-element.26), channel_id=1, source_target_pairs={{0,4},{4,0},{8,12},{12,8},{16,20},{20,16},{24,28},{28,24},{1,5},{5... | collective-permute-start | bytes 393224 | tf_op jit(solution)/shard_map/ppermute | solution.py:205
  5.3 1.0 %collective-permute-done = f32[256,128]{1,0:T(8,128)S(1)} collective-permute-done((f32[256,128]{1,0:T(8,128)S(1)}, f32[256,128]{1,0:T(8,128)S(1)}, u32[]{:S(2)}, u32[]{:S(2)}) %collective-permute-start) | collective-permute-done | bytes 131104 | tf_op jit(solution)/shard_map/ppermute | solution.py:205
  6.3 2.9 %collective-permute-start.1 = (f32[256,128]{1,0:T(8,128)S(1)}, f32[256,128]{1,0:T(8,128)S(1)}, u32[]{:S(2)}, u32[]{:S(2)}) collective-permute-start(f32[256,128]{1,0:T(8,128)S(1)} %add.42), channel_id=1, source_target_pairs={{0,8},{4,12},{8,0},{12,4},{16,24},{20,28},{24,16},{28,20},{1,9},{5... | collective-permute-start | bytes 393224 | tf_op jit(solution)/shard_map/ppermute | solution.py:205
  9.2 1.5 %collective-permute-start.2 = (f32[256,128]{1,0:T(8,128)S(1)}, f32[256,128]{1,0:T(8,128)S(1)}, u32[]{:S(2)}, u32[]{:S(2)}) collective-permute-start(f32[256,128]{1,0:T(8,128)S(1)} %add.42), channel_id=1, source_target_pairs={{0,16},{4,20},{8,24},{12,28},{16,0},{20,4},{24,8},{28,12},{1,17},{... | collective-permute-start | bytes 393224 | tf_op jit(solution)/shard_map/ppermute | solution.py:205
  10.7 2.4 %collective-permute-done.1 = f32[256,128]{1,0:T(8,128)S(1)} collective-permute-done((f32[256,128]{1,0:T(8,128)S(1)}, f32[256,128]{1,0:T(8,128)S(1)}, u32[]{:S(2)}, u32[]{:S(2)}) %collective-permute-start.1) | collective-permute-done | bytes 131104 | tf_op jit(solution)/shard_map/ppermute | solution.py:205
  13.1 4.2 %collective-permute-done.2 = f32[256,128]{1,0:T(8,128)S(1)} collective-permute-done((f32[256,128]{1,0:T(8,128)S(1)}, f32[256,128]{1,0:T(8,128)S(1)}, u32[]{:S(2)}, u32[]{:S(2)}) %collective-permute-start.2) | collective-permute-done | bytes 131104 | tf_op jit(solution)/shard_map/ppermute | solution.py:205
  17.4 0.1 name_places.1
  17.5 1.1 %collective-permute-done.4.theirs = bf16[128,128]{1,0:T(8,128)(2,1)S(1)} collective-permute-done((bf16[128,128]{1,0:T(8,128)(2,1)S(1)}, bf16[128,128]{1,0:T(8,128)(2,1)S(1)}, u32[]{:S(2)}, u32[]{:S(2)}) %collective-permute-start.4) | collective-permute-done | bytes 32800 | tf_op jit(solution)/shard_map/ppermute | solution.py:205
  18.6 1.0 %first_backward.1 = f32[128,128]{1,0:T(8,128)S(1)} custom-call(bf16[128,128,128]{2,1,0:T(8,128)(2,1)S(1)} %get-tuple-element.17.proj, bf16[128,256]{1,0:T(8,128)(2,1)S(1)} %get-tuple-element.23.picks, bf16[64,128]{1,0:T(8,128)(2,1)S(1)} %get-tuple-element.24.places, bf16[128,128]{1,0:T(8,128)(2,1)S(1)} %fusion.mine, ...), custom_call_target="tpu_custom_call" | custom-call | tf_op jit(solution)/shard_map/first_backward/pallas_call | solution.py:291
  19.6 1.6 %collective-permute-start.5 = (f32[128,128]{1,0:T(8,128)S(1)}, f32[128,128]{1,0:T(8,128)S(1)}, u32[]{:S(2)}, u32[]{:S(2)}) collective-permute-start(f32[128,128]{1,0:T(8,128)S(1)} %first_backward.1), channel_id=1, source_target_pairs={{0,1},{1,0},{2,3},{3,2},{4,5},{5,4},{6,7},{7,6},{8,9},{9,8},{10,11... | collective-permute-start | bytes 196616 | tf_op jit(solution)/shard_map/ppermute | solution.py:205
  21.3 2.7 %collective-permute-done.5 = f32[128,128]{1,0:T(8,128)S(1)} collective-permute-done((f32[128,128]{1,0:T(8,128)S(1)}, f32[128,128]{1,0:T(8,128)S(1)}, u32[]{:S(2)}, u32[]{:S(2)}) %collective-permute-start.5) | collective-permute-done | bytes 65568 | tf_op jit(solution)/shard_map/ppermute | solution.py:205
  24.0 2.6 %collective-permute-start.6 = (f32[128,128]{1,0:T(8,128)S(1)}, f32[128,128]{1,0:T(8,128)S(1)}, u32[]{:S(2)}, u32[]{:S(2)}) collective-permute-start(f32[128,128]{1,0:T(8,128)S(1)} %add.46), channel_id=1, source_target_pairs={{0,2},{1,3},{2,0},{3,1},{4,6},{5,7},{6,4},{7,5},{8,10},{9,11},{10,... | collective-permute-start | bytes 196616 | tf_op jit(solution)/shard_map/ppermute | solution.py:205
  26.6 1.1 %turn_blocks.1.proj = bf16[128,128,128]{2,1,0:T(8,128)(2,1)S(1)} custom-call(bf16[128,128,128]{2,1,0:T(8,128)(2,1)S(1)} %get-tuple-element.17.proj), custom_call_target="tpu_custom_call" | custom-call | bytes 8388608 | tf_op jit(solution)/shard_map/turn_blocks/pallas_call | solution.py:278
  27.7 1.4 %collective-permute-done.6 = f32[128,128]{1,0:T(8,128)S(1)} collective-permute-done((f32[128,128]{1,0:T(8,128)S(1)}, f32[128,128]{1,0:T(8,128)S(1)}, u32[]{:S(2)}, u32[]{:S(2)}) %collective-permute-start.6) | collective-permute-done | bytes 65568 | tf_op jit(solution)/shard_map/ppermute | solution.py:205
  29.2 1.0 %next_forward.1 = (f32[64,128]{1,0:T(8,128)S(1)}, f32[64,128]{1,0:T(8,128)S(1)}, f32[128,128]{1,0:T(8,128)S(1)}, f32[128,128]{1,0:T(8,128)S(1)}) custom-call(bf16[128,128,128]{2,1,0:T(8,128)(2,1)S(1)} %turn_blocks.1.proj, bf16[128,64]{1,0:T(8,128)(2,1)S(1)} %get-tuple-element.20.picks, bf16[256,128]{1,0:T(8,128)(2,1)S(1)} %get-tuple-element.21.places, ...), custom_call_target="tpu_custom_call" | custom-call | tf_op jit(solution)/shard_map/next_forward/pallas_call | solution.py:301
  30.3 1.2 %collective-permute-done.7 = f32[128,128]{1,0:T(8,128)S(1)} collective-permute-done((f32[128,128]{1,0:T(8,128)S(1)}, f32[128,128]{1,0:T(8,128)S(1)}, u32[]{:S(2)}, u32[]{:S(2)}) %collective-permute-start.7) | collective-permute-done | bytes 65568 | tf_op jit(solution)/shard_map/ppermute | solution.py:205
  31.6 1.6 %collective-permute-start.10 = (f32[128,128]{1,0:T(8,128)S(1)}, f32[128,128]{1,0:T(8,128)S(1)}, u32[]{:S(2)}, u32[]{:S(2)}) collective-permute-start(f32[128,128]{1,0:T(8,128)S(1)} %add.48), channel_id=1, source_target_pairs={{0,24},{4,28},{8,16},{12,20},{16,8},{20,12},{24,0},{28,4},{1,25},{... | collective-permute-start | bytes 196616 | tf_op jit(solution)/shard_map/ppermute | solution.py:205
  33.1 1.5 %collective-permute-start.8 = (f32[128,128]{1,0:T(8,128)S(1)}, f32[128,128]{1,0:T(8,128)S(1)}, u32[]{:S(2)}, u32[]{:S(2)}) collective-permute-start(f32[128,128]{1,0:T(8,128)S(1)} %add.48), channel_id=1, source_target_pairs={{0,8},{4,12},{8,0},{12,4},{16,24},{20,28},{24,16},{28,20},{1,9},{5... | collective-permute-start | bytes 196616 | tf_op jit(solution)/shard_map/ppermute | solution.py:205
  34.6 0.5 collective-permute-start.9
  35.1 2.2 %collective-permute-done.10 = f32[128,128]{1,0:T(8,128)S(1)} collective-permute-done((f32[128,128]{1,0:T(8,128)S(1)}, f32[128,128]{1,0:T(8,128)S(1)}, u32[]{:S(2)}, u32[]{:S(2)}) %collective-permute-start.10) | collective-permute-done | bytes 65568 | tf_op jit(solution)/shard_map/ppermute | solution.py:205
  37.3 0.8 %collective-permute-done.8 = f32[128,128]{1,0:T(8,128)S(1)} collective-permute-done((f32[128,128]{1,0:T(8,128)S(1)}, f32[128,128]{1,0:T(8,128)S(1)}, u32[]{:S(2)}, u32[]{:S(2)}) %collective-permute-start.8) | collective-permute-done | bytes 65568 | tf_op jit(solution)/shard_map/ppermute | solution.py:205
  38.1 0.7 %collective-permute-done.9 = f32[128,128]{1,0:T(8,128)S(1)} collective-permute-done((f32[128,128]{1,0:T(8,128)S(1)}, f32[128,128]{1,0:T(8,128)S(1)}, u32[]{:S(2)}, u32[]{:S(2)}) %collective-permute-start.9) | collective-permute-done | bytes 65568 | tf_op jit(solution)/shard_map/ppermute | solution.py:205
  38.9 0.1 collective-permute-start.11
  39.0 1.2 %collective-permute-done.11.theirs = bf16[128,128]{1,0:T(8,128)(2,1)S(1)} collective-permute-done((bf16[128,128]{1,0:T(8,128)(2,1)S(1)}, bf16[128,128]{1,0:T(8,128)(2,1)S(1)}, u32[]{:S(2)}, u32[]{:S(2)}) %collective-permute-start.11) | collective-permute-done | bytes 32800 | tf_op jit(solution)/shard_map/ppermute | solution.py:205
  40.2 0.9 %last_backward.1 = f32[64,128]{1,0:T(8,128)S(1)} custom-call(bf16[128,128,128]{2,1,0:T(8,128)(2,1)S(1)} %get-tuple-element.17.proj, bf16[128,256]{1,0:T(8,128)(2,1)S(1)} %get-tuple-element.23.picks, bf16[64,128]{1,0:T(8,128)(2,1)S(1)} %get-tuple-element.24.places, bf16[128,128]{1,0:T(8,128)(2,1)S(1)} %get-tuple-element.32.mine, ...), custom_call_target="tpu_custom_call" | custom-call | tf_op jit(solution)/shard_map/last_backward/pallas_call | solution.py:314
  41.1 1.6 %collective-permute-start.12 = (f32[64,128]{1,0:T(8,128)S(1)}, f32[64,128]{1,0:T(8,128)S(1)}, u32[]{:S(2)}, u32[]{:S(2)}) collective-permute-start(f32[64,128]{1,0:T(8,128)S(1)} %last_backward.1), channel_id=1, source_target_pairs={{0,1},{1,0},{2,3},{3,2},{4,5},{5,4},{6,7},{7,6},{8,9},{9,8},{10,11... | collective-permute-start | bytes 98312 | tf_op jit(solution)/shard_map/ppermute | solution.py:205
  42.8 2.3 %collective-permute-done.12 = f32[64,128]{1,0:T(8,128)S(1)} collective-permute-done((f32[64,128]{1,0:T(8,128)S(1)}, f32[64,128]{1,0:T(8,128)S(1)}, u32[]{:S(2)}, u32[]{:S(2)}) %collective-permute-start.12) | collective-permute-done | bytes 32800 | tf_op jit(solution)/shard_map/ppermute | solution.py:205
  45.1 2.7 %collective-permute-start.13 = (f32[64,128]{1,0:T(8,128)S(1)}, f32[64,128]{1,0:T(8,128)S(1)}, u32[]{:S(2)}, u32[]{:S(2)}) collective-permute-start(f32[64,128]{1,0:T(8,128)S(1)} %add.52), channel_id=1, source_target_pairs={{0,2},{1,3},{2,0},{3,1},{4,6},{5,7},{6,4},{7,5},{8,10},{9,11},{10,... | collective-permute-start | bytes 98312 | tf_op jit(solution)/shard_map/ppermute | solution.py:205
  47.8 0.6 %constant_dynamic-slice_fusion = f32[32,128]{1,0:T(8,128)} fusion(f32[128,128]{1,0:T(8,128)S(1)} %get-tuple-element.33, s32[]{:T(128)S(6)} %select_n.3), kind=kLoop, calls=%fused_computation.7 | loop fusion | bytes 32772 | tf_op jit(solution)/shard_map/dynamic_slice | solution.py:312
  48.5 1.5 %collective-permute-done.13 = f32[64,128]{1,0:T(8,128)S(1)} collective-permute-done((f32[64,128]{1,0:T(8,128)S(1)}, f32[64,128]{1,0:T(8,128)S(1)}, u32[]{:S(2)}, u32[]{:S(2)}) %collective-permute-start.13) | collective-permute-done | bytes 32800 | tf_op jit(solution)/shard_map/ppermute | solution.py:205
  49.9 0.6 %multiply_add_fusion = f32[64,128]{1,0:T(8,128)} fusion(f32[64,128]{1,0:T(8,128)S(1)} %get-tuple-element.28, f32[64,128]{1,0:T(8,128)S(1)} %get-tuple-element.29, f32[64,128]{1,0:T(8,128)S(1)} %add.52, f32[64,128]{1,0:T(8,128)S(1)} %collective-permute-done.13), kind=kLoop, calls=%fused_computation.6 | loop fusion | flops 24576 | bytes 163840 | tf_op jit(solution)/shard_map/add | solution.py:323
  (12 shorter events, 0.3 us)
Async XLA Ops:
  4.8 1.5 %collective-permute-start = (f32[256,128]{1,0:T(8,128)S(1)}, f32[256,128]{1,0:T(8,128)S(1)}, u32[]{:S(2)}, u32[]{:S(2)}) collective-permute-start(f32[256,128]{1,0:T(8,128)S(1)} %get-tuple-element.26), channel_id=1, source_target_pairs={{0,4},{4,0},{8,12},{12,8},{16,20},{20,16},{24,28},{28,24},{1,5},{5... | collective-permute-start | bytes 393224 | tf_op jit(solution)/shard_map/ppermute | solution.py:205
  6.3 6.8 %collective-permute-start.1 = (f32[256,128]{1,0:T(8,128)S(1)}, f32[256,128]{1,0:T(8,128)S(1)}, u32[]{:S(2)}, u32[]{:S(2)}) collective-permute-start(f32[256,128]{1,0:T(8,128)S(1)} %add.42), channel_id=1, source_target_pairs={{0,8},{4,12},{8,0},{12,4},{16,24},{20,28},{24,16},{28,20},{1,9},{5... | collective-permute-start | bytes 393224 | tf_op jit(solution)/shard_map/ppermute | solution.py:205
  9.2 8.1 %collective-permute-start.2 = (f32[256,128]{1,0:T(8,128)S(1)}, f32[256,128]{1,0:T(8,128)S(1)}, u32[]{:S(2)}, u32[]{:S(2)}) collective-permute-start(f32[256,128]{1,0:T(8,128)S(1)} %add.42), channel_id=1, source_target_pairs={{0,16},{4,20},{8,24},{12,28},{16,0},{20,4},{24,8},{28,12},{1,17},{... | collective-permute-start | bytes 393224 | tf_op jit(solution)/shard_map/ppermute | solution.py:205
  10.7 6.5 %collective-permute-start.3 = (f32[256,128]{1,0:T(8,128)S(1)}, f32[256,128]{1,0:T(8,128)S(1)}, u32[]{:S(2)}, u32[]{:S(2)}) collective-permute-start(f32[256,128]{1,0:T(8,128)S(1)} %add.42), channel_id=1, source_target_pairs={{0,24},{4,28},{8,16},{12,20},{16,8},{20,12},{24,0},{28,4},{1,25},{... | collective-permute-start | bytes 393224 | tf_op jit(solution)/shard_map/ppermute | solution.py:205
  17.3 1.3 %collective-permute-start.4 = (bf16[128,128]{1,0:T(8,128)(2,1)S(1)}, bf16[128,128]{1,0:T(8,128)(2,1)S(1)}, u32[]{:S(2)}, u32[]{:S(2)}) collective-permute-start(bf16[128,128]{1,0:T(8,128)(2,1)S(1)} %fusion.mine), channel_id=1, source_target_pairs={{0,4},{4,0},{8,12},{12,8},{16,20},{20,16},{24,28},{28,24},{1,5},{5... | collective-permute-start | bytes 98312 | tf_op jit(solution)/shard_map/ppermute | solution.py:205
  19.6 4.3 %collective-permute-start.5 = (f32[128,128]{1,0:T(8,128)S(1)}, f32[128,128]{1,0:T(8,128)S(1)}, u32[]{:S(2)}, u32[]{:S(2)}) collective-permute-start(f32[128,128]{1,0:T(8,128)S(1)} %first_backward.1), channel_id=1, source_target_pairs={{0,1},{1,0},{2,3},{3,2},{4,5},{5,4},{6,7},{7,6},{8,9},{9,8},{10,11... | collective-permute-start | bytes 196616 | tf_op jit(solution)/shard_map/ppermute | solution.py:205
  24.0 5.2 %collective-permute-start.6 = (f32[128,128]{1,0:T(8,128)S(1)}, f32[128,128]{1,0:T(8,128)S(1)}, u32[]{:S(2)}, u32[]{:S(2)}) collective-permute-start(f32[128,128]{1,0:T(8,128)S(1)} %add.46), channel_id=1, source_target_pairs={{0,2},{1,3},{2,0},{3,1},{4,6},{5,7},{6,4},{7,5},{8,10},{9,11},{10,... | collective-permute-start | bytes 196616 | tf_op jit(solution)/shard_map/ppermute | solution.py:205
  30.2 1.3 %collective-permute-start.7 = (f32[128,128]{1,0:T(8,128)S(1)}, f32[128,128]{1,0:T(8,128)S(1)}, u32[]{:S(2)}, u32[]{:S(2)}) collective-permute-start(f32[128,128]{1,0:T(8,128)S(1)} %get-tuple-element.31), channel_id=1, source_target_pairs={{0,4},{4,0},{8,12},{12,8},{16,20},{20,16},{24,28},{28,24},{1,5},{5... | collective-permute-start | bytes 196616 | tf_op jit(solution)/shard_map/ppermute | solution.py:205
  31.6 5.8 %collective-permute-start.10 = (f32[128,128]{1,0:T(8,128)S(1)}, f32[128,128]{1,0:T(8,128)S(1)}, u32[]{:S(2)}, u32[]{:S(2)}) collective-permute-start(f32[128,128]{1,0:T(8,128)S(1)} %add.48), channel_id=1, source_target_pairs={{0,24},{4,28},{8,16},{12,20},{16,8},{20,12},{24,0},{28,4},{1,25},{... | collective-permute-start | bytes 196616 | tf_op jit(solution)/shard_map/ppermute | solution.py:205
  33.1 5.0 %collective-permute-start.8 = (f32[128,128]{1,0:T(8,128)S(1)}, f32[128,128]{1,0:T(8,128)S(1)}, u32[]{:S(2)}, u32[]{:S(2)}) collective-permute-start(f32[128,128]{1,0:T(8,128)S(1)} %add.48), channel_id=1, source_target_pairs={{0,8},{4,12},{8,0},{12,4},{16,24},{20,28},{24,16},{28,20},{1,9},{5... | collective-permute-start | bytes 196616 | tf_op jit(solution)/shard_map/ppermute | solution.py:205
  34.6 4.3 %collective-permute-start.9 = (f32[128,128]{1,0:T(8,128)S(1)}, f32[128,128]{1,0:T(8,128)S(1)}, u32[]{:S(2)}, u32[]{:S(2)}) collective-permute-start(f32[128,128]{1,0:T(8,128)S(1)} %add.48), channel_id=1, source_target_pairs={{0,16},{4,20},{8,24},{12,28},{16,0},{20,4},{24,8},{28,12},{1,17},{... | collective-permute-start | bytes 196616 | tf_op jit(solution)/shard_map/ppermute | solution.py:205
  38.9 1.3 %collective-permute-start.11 = (bf16[128,128]{1,0:T(8,128)(2,1)S(1)}, bf16[128,128]{1,0:T(8,128)(2,1)S(1)}, u32[]{:S(2)}, u32[]{:S(2)}) collective-permute-start(bf16[128,128]{1,0:T(8,128)(2,1)S(1)} %get-tuple-element.32.mine), channel_id=1, source_target_pairs={{0,4},{4,0},{8,12},{12,8},{16,20},{20,16},{24,28},{28,24},{1,5},{5... | collective-permute-start | bytes 98312 | tf_op jit(solution)/shard_map/ppermute | solution.py:205
  41.1 4.0 %collective-permute-start.12 = (f32[64,128]{1,0:T(8,128)S(1)}, f32[64,128]{1,0:T(8,128)S(1)}, u32[]{:S(2)}, u32[]{:S(2)}) collective-permute-start(f32[64,128]{1,0:T(8,128)S(1)} %last_backward.1), channel_id=1, source_target_pairs={{0,1},{1,0},{2,3},{3,2},{4,5},{5,4},{6,7},{7,6},{8,9},{9,8},{10,11... | collective-permute-start | bytes 98312 | tf_op jit(solution)/shard_map/ppermute | solution.py:205
  45.1 4.8 %collective-permute-start.13 = (f32[64,128]{1,0:T(8,128)S(1)}, f32[64,128]{1,0:T(8,128)S(1)}, u32[]{:S(2)}, u32[]{:S(2)}) collective-permute-start(f32[64,128]{1,0:T(8,128)S(1)} %add.52), channel_id=1, source_target_pairs={{0,2},{1,3},{2,0},{3,1},{4,6},{5,7},{6,4},{7,5},{8,10},{9,11},{10,... | collective-permute-start | bytes 98312 | tf_op jit(solution)/shard_map/ppermute | solution.py:205

commit v5 on v4

--- a/solution.py
+++ b/solution.py
@@ -49,37 +49,23 @@
     return jnp.where(stored, place * ray_dev + ray, -1)
 
 
-def forward(proj, volume, vox, before):
-    blocks = proj.shape[0]
-    part = blocks // (2 * CHUNKS)
-    picked = dot(volume.T.astype(BF16), one_hot_t(vox, volume.shape[0]).astype(BF16))
-    first = lax.rem(iota((BLK, blocks), 1), 2 * part) < part
-    halves = [jnp.where(side, jnp.concatenate([picked, jnp.ones_like(picked)], 1), 0.0)
-              for side in (jnp.concatenate([first] * 2, 1), ~jnp.concatenate([first] * 2, 1))]
-    weights = jnp.concatenate(halves, 0).astype(BF16)
-    lane = lax.rem(iota((BLK, 2 * blocks), 1), blocks)
-    column = lane - jnp.where(lax.rem(lane, 2 * part) < part, 0, part)
-    acc = jnp.zeros((BLK, 2 * blocks), F32)
-    for c in range(CHUNKS):
-        before(c)
-        for k in range(2 * part * c, 2 * part * c + part):
-            pair = jnp.concatenate([proj[k], proj[k + part]], 1)
-            acc = jnp.where(column == k, dot(pair, weights), acc)
-    return acc
-
-
-def products(proj, vectors, sums):
+def products(proj, vectors, sums=False, before=None, turn=False):
     blocks = proj.shape[0]
     group = 16
     row = iota((group, BLK), 0)
     tops, lows = [], []
     for g in range(blocks // group):
+        if before is not None:
+            before(g * group)
         mine = vectors[g * group:(g + 1) * group]
         left = jnp.concatenate([jnp.where(row == c, mine, 0.0) for c in range(group)], 1)
         if sums:
             ones = jnp.concatenate([jnp.where(row == c, 1.0, 0.0) for c in range(group)], 1)
             left = jnp.concatenate([left, ones], 0)
-        right = proj[g * group:(g + 1) * group].reshape(group * BLK, BLK)
+        if turn:
+            right = jnp.concatenate([proj[k].T for k in range(g * group, (g + 1) * group)], 0)
+        else:
+            right = proj[g * group:(g + 1) * group].reshape(group * BLK, BLK)
         out = dot(left.astype(BF16), right)
         tops.append(out[:group])
         if sums:
@@ -92,21 +78,23 @@
     return dot(jnp.concatenate([places] * 3, 1), jnp.concatenate(split3(columns), 0))
 
 
-def backward(proj, weighted, picks, places, sums):
-    return collect(places, products(proj, dot(picks, weighted), sums))
+def backward(proj, weighted, picks, places):
+    return collect(places, products(proj, dot(picks, weighted)))
 
 
 def forward_turned(turned, volume, picks, places):
-    return collect(places, products(turned, dot(picks, volume.astype(BF16)), False))
-
-
-def name_places(rows, vox, from_rays, to_rays, from_vox, to_vox):
+    return collect(places, products(turned, dot(picks, volume.astype(BF16))))
+
+
+def name_places(proj, rows, vox, from_rays, to_rays, from_vox, to_vox, columns):
     spots = one_hot_t(rows[...], to_rays.shape[0])
     from_rays[...] = spots.T.astype(BF16)
     to_rays[...] = spots.astype(BF16)
     spots = one_hot_t(vox[...], to_vox.shape[0])
     from_vox[...] = spots.T.astype(BF16)
-    to_vox[...] = (spots * jnp.where(rows[...] >= 0, 1.0, 0.0)).astype(BF16)
+    places = (spots * jnp.where(rows[...] >= 0, 1.0, 0.0)).astype(BF16)
+    to_vox[...] = places
+    columns[...] = collect(places, products(proj, jnp.ones((proj.shape[0], BLK), F32)))
 
 
 def turn_blocks(proj, turned):
@@ -151,14 +139,15 @@
         for copy in smalls:
             copy.wait()
 
-        def before(c):
-            copies[c].wait()
+        def before(k):
+            if k % size == 0:
+                copies[k // size].wait()
 
         rows = block_rows(slot[...], ray[...], count[...], slabs, capacity, ray_dev)
         rows_out[...] = rows
         total = slabs * ray_dev
-        columns = forward(proj, prior[...], vox[...], before)
-        columns = jnp.concatenate([columns[:, :blocks].T, columns[:, blocks:].T], 1)
+        picks = one_hot_t(vox[...], prior.shape[0]).T.astype(BF16)
+        columns = products(proj, dot(picks, prior[...].astype(BF16)), True, before, True)
         both = collect(one_hot_t(rows, total).astype(BF16), columns)
         put_partial(both[:, :BLK], sino[...], mine, theirs, ray_dev)
         sums = both[:, BLK:]
@@ -176,19 +165,11 @@
     return jnp.concatenate([jnp.where(core == 0, mine, theirs), jnp.where(core == 0, theirs, mine)], 0)
 
 
-def first_backward(proj, picks, places, mine, theirs, corr):
-    vox_dev = corr.shape[0] // 2
-    both = backward(proj, join_halves(mine, theirs), picks[...], places[...], True)
-    corr[0:vox_dev, :] = both[:, :BLK]
-    corr[vox_dev:2 * vox_dev, :] = both[:, BLK:]
-
-
 def next_forward(ray_dev):
-    def kernel(proj, picks, places, volume, corr, sino, volume_out, weight_out, mine, theirs):
-        vox_dev = volume.shape[0]
-        weights = 1.0 / jnp.maximum(corr[vox_dev:2 * vox_dev, :], 1.0)
+    def kernel(proj, picks, places, volume, corr, col_total, sino, volume_out, weight_out, mine, theirs):
+        weights = 1.0 / jnp.maximum(col_total[...], 1.0)
         weight_out[...] = weights
-        updated = volume[...] + weights * corr[0:vox_dev, :]
+        updated = volume[...] + weights * corr[...]
         volume_out[...] = updated
         sums = forward_turned(proj, updated, picks[...], places[...])
         put_partial(sums, sino[...], mine, theirs, ray_dev)
@@ -196,8 +177,8 @@
     return kernel
 
 
-def last_backward(proj, picks, places, mine, theirs, corr):
-    corr[...] = backward(proj, join_halves(mine, theirs), picks[...], places[...], False)
+def to_voxels(proj, picks, places, mine, theirs, corr):
+    corr[...] = backward(proj, join_halves(mine, theirs), picks[...], places[...])
 
 
 def swap(x, axis, bit):
@@ -205,7 +186,7 @@
     return lax.ppermute(x, axis, [(i, i ^ bit) for i in range(size)])
 
 
-def over_slabs(mine, theirs):
+def over_slabs(mine, theirs, beside=None):
     slabs = lax.axis_size("slab")
     x = mine + swap(theirs, "slab", 1)
     bits = [1 << b for b in range(1, slabs.bit_length() - 1)]
@@ -214,19 +195,19 @@
             x, bits = x + swap(x, "slab", bits[0]), []
             continue
         first, second, bits = bits[0], bits[1], bits[2:]
-        x = (x + swap(x, "slab", first)) + (swap(x, "slab", second) + swap(x, "slab", first | second))
-    return x
-
-
-def over_angles(x, direct):
+        near = swap(x, "slab", first)
+        other = swap(x, "slab", second) , swap(x, "slab", first | second)
+        if beside is not None and not bits:
+            near, beside = lax.optimization_barrier((near, beside))
+            beside = beside + swap(beside, "angle", 1)
+        x = (x + near) + (other[0] + other[1])
+    return x if beside is None else (x, beside)
+
+
+def over_angles(x, done=0):
     angles = lax.axis_size("angle")
-    bits = [1 << b for b in range(angles.bit_length() - 1)]
-    while bits:
-        if len(bits) == 1 or not direct:
-            x, bits = x + swap(x, "angle", bits[0]), bits[1:]
-            continue
-        first, second, bits = bits[0], bits[1], bits[2:]
-        x = (x + swap(x, "angle", first)) + (swap(x, "angle", second) + swap(x, "angle", first | second))
+    for b in range(done, angles.bit_length() - 1):
+        x = x + swap(x, "angle", 1 << b)
     return x
 
 
@@ -263,18 +244,18 @@
         compiler_params=params,
         name="first_forward",
     )(*[x if x.size == 1 else pltpu.with_memory_space_constraint(x, pltpu.HBM) for x in arguments])
-    from_rays, to_rays, from_vox, to_vox = pl.pallas_call(
+    from_rays, to_rays, from_vox, to_vox, col_total = pl.pallas_call(
         name_places,
         out_shape=(
             pltpu.VMEM((blocks, 2 * half), BF16), pltpu.VMEM((2 * half, blocks), BF16),
-            pltpu.VMEM((blocks, vox_dev), BF16), pltpu.VMEM((vox_dev, blocks), BF16),
+            pltpu.VMEM((blocks, vox_dev), BF16), pltpu.VMEM((vox_dev, blocks), BF16), vmem(vox_dev),
         ),
-        in_specs=[whole()] * 2,
-        out_specs=(whole(),) * 4,
+        in_specs=[whole()] * 3,
+        out_specs=(whole(),) * 5,
         compiler_params=params,
         cost_estimate=pl.CostEstimate(flops=0, bytes_accessed=1 << 20, transcendentals=0),
         name="name_places",
-    )(rows, vox)
+    )(proj, rows, vox)
     turned = pl.pallas_call(
         turn_blocks,
         out_shape=pltpu.VMEM(projector.shape, BF16),
@@ -284,42 +265,43 @@
         cost_estimate=pl.CostEstimate(flops=0, bytes_accessed=2 * projector.size * 2, transcendentals=0),
         name="turn_blocks",
     )(proj)
-    sums = over_slabs(mine, theirs)
+    sums, col_total = over_slabs(mine, theirs, col_total)
+    col_total = over_angles(col_total, 1)
     row_weight = 1.0 / jnp.maximum(sums[half:], 1.0)
     weighted = (row_weight * sums[:half]).astype(BF16)
 
     corr = pl.pallas_call(
-        first_backward,
-        out_shape=vmem(2 * vox_dev),
+        to_voxels,
+        out_shape=vmem(vox_dev),
         in_specs=[whole()] * 5,
         out_specs=whole(),
         compiler_params=params,
         name="first_backward",
     )(proj, from_rays, to_vox, weighted, swap(weighted, "slab", 1))
-    corr = over_angles(corr, False)
+    corr = over_angles(corr)
 
     volume, col_weight, mine, theirs = pl.pallas_call(
         next_forward(ray_dev),
         out_shape=(vmem(vox_dev), vmem(vox_dev), vmem(half), vmem(half)),
-        in_specs=[whole()] * 6,
+        in_specs=[whole()] * 7,
         out_specs=(whole(),) * 4,
         compiler_params=params,
         name="next_forward",
-    )(turned, from_vox, to_rays, volume, corr, sino)
+    )(turned, from_vox, to_rays, volume, corr, col_total, sino)
     residual = row_weight * over_slabs(mine, theirs)
     weighted = residual.astype(BF16)
     start = lax.div(lax.axis_index("slab"), 2) * ray_dev
     residual = lax.dynamic_slice_in_dim(residual, start, ray_dev)
 
     corr = pl.pallas_call(
-        last_backward,
+        to_voxels,
         out_shape=vmem(vox_dev),
         in_specs=[whole()] * 5,
         out_specs=whole(),
         compiler_params=params,
         name="last_backward",
     )(proj, from_rays, to_vox, weighted, swap(weighted, "slab", 1))
-    corr = over_angles(corr, False)
+    corr = over_angles(corr)
     return volume + col_weight * corr, residual
 
 

time: 50.7 us -> 50.3 us (level)
  waiting for transfers between devices: 22.8 us -> 18.2 us
  starting transfers between devices: 17.4 us -> 20.9 us
  Pallas kernels: 7.66 us -> 8.22 us
    ppermute x14 -> x16, waiting for transfers between devices: 22.8 us -> 18.2 us  [swap(): return lax.ppermute(x, axis, [(i, i ^ bit) for i in range(size)])]
    ppermute x14 -> x16, starting transfers between devices: 17.4 us -> 20.9 us  [swap(): return lax.ppermute(x, axis, [(i, i ^ bit) for i in range(size)])]
    pallas_call x1, Pallas kernels: 0.1 us -> 0.8 us  [local(): pl.pallas_call(name_places, out_shape=(pltpu.VMEM((blocks, 2 * half), BF1...]
  transfers between devices with their start and end apart: 14 -> 16, of which waited for: 13 -> 12; matrix products, arithmetic and copies ran while one was open for 1% -> 1% of each run, Pallas kernels for 2% -> 6%
where the time goes in v5:
time: 50.3 us; the launch traced here: 50.1 us
  starting transfers between devices  20.9 us (42%)
  waiting for transfers between devices  18.2 us (36%)
  Pallas kernels  8.22 us (16%)
  between operations  1.4 us (3%)
  other arithmetic  0.75 us (1%)
  local copies, waits for them, and re-layouts  0.61 us (1%)
    ppermute x16, starting transfers between devices, swap(): return lax.ppermute(x, axis, [(i, i ^ bit) for i in range(size)])  20.9 us
    ppermute x16, waiting for transfers between devices, swap(): return lax.ppermute(x, axis, [(i, i ^ bit) for i in range(size)])  18.2 us
    pallas_call x1, Pallas kernels, local(): pl.pallas_call(first_forward(slabs, capacity, ray_dev), out_shape=(pltpu....  3.4 us
    pallas_call x2, Pallas kernels, local(): pl.pallas_call(to_voxels, out_shape=vmem(vox_dev), in_specs=[whole()] * 5...  1.89 us
    pallas_call x1, Pallas kernels, local(): pl.pallas_call(turn_blocks, out_shape=pltpu.VMEM(projector.shape, BF16),...  1.13 us
  transfers between devices with their start and end apart: 16, of which 12 were waited for; matrix products, arithmetic and copies ran while one was open for 1% of the time, Pallas kernels for 6%

profile of v5, /device:TPU:0, one launch (start us, length us, event | category | flops | bytes accessed | tf_op | source)
XLA Modules:
  0.0 50.1 jit_solution(16341197629764574790)
XLA Ops:
  1.3 3.4 %first_forward.1 = (bf16[128,128,128]{2,1,0:T(8,128)(2,1)S(1)}, s32[1,128]{1,0:T(1,128)S(1)}, s32[1,128]{1,0:T(1,128)S(1)}, f32[64,128]{1,0:T(8,128)S(1)}, f32[3...) custom-call(bf16[128,128,128]{2,1,0:T(8,128)(2,1)} %proj_hbm.1, s32[1,128]{1,0:T(1,128)} %bitcast.4, ...), custom_call_target="tpu_custom_call" | custom-call | tf_op jit(solution)/shard_map/first_forward/pallas_call | solution.py:229
  4.7 0.5 %collective-permute-start = (f32[256,128]{1,0:T(8,128)S(1)}, f32[256,128]{1,0:T(8,128)S(1)}, u32[]{:S(2)}, u32[]{:S(2)}) collective-permute-start(f32[256,128]{1,0:T(8,128)S(1)} %get-tuple-element.29), channel_id=1, source_target_pairs={{0,4},{4,0},{8,12},{12,8},{16,20},{20,16},{24,28},{28,24},{1,5},{5... | collective-permute-start | bytes 393224 | tf_op jit(solution)/shard_map/ppermute | solution.py:186
  5.2 1.0 %collective-permute-done = f32[256,128]{1,0:T(8,128)S(1)} collective-permute-done((f32[256,128]{1,0:T(8,128)S(1)}, f32[256,128]{1,0:T(8,128)S(1)}, u32[]{:S(2)}, u32[]{:S(2)}) %collective-permute-start) | collective-permute-done | bytes 131104 | tf_op jit(solution)/shard_map/ppermute | solution.py:186
  6.2 2.9 %collective-permute-start.1 = (f32[256,128]{1,0:T(8,128)S(1)}, f32[256,128]{1,0:T(8,128)S(1)}, u32[]{:S(2)}, u32[]{:S(2)}) collective-permute-start(f32[256,128]{1,0:T(8,128)S(1)} %add.48), channel_id=1, source_target_pairs={{0,8},{4,12},{8,0},{12,4},{16,24},{20,28},{24,16},{28,20},{1,9},{5... | collective-permute-start | bytes 393224 | tf_op jit(solution)/shard_map/ppermute | solution.py:186
  9.1 1.5 %collective-permute-start.2 = (f32[256,128]{1,0:T(8,128)S(1)}, f32[256,128]{1,0:T(8,128)S(1)}, u32[]{:S(2)}, u32[]{:S(2)}) collective-permute-start(f32[256,128]{1,0:T(8,128)S(1)} %add.48), channel_id=1, source_target_pairs={{0,16},{4,20},{8,24},{12,28},{16,0},{20,4},{24,8},{28,12},{1,17},{... | collective-permute-start | bytes 393224 | tf_op jit(solution)/shard_map/ppermute | solution.py:186
  10.7 0.8 %name_places.1 = (bf16[128,256]{1,0:T(8,128)(2,1)S(1)}, bf16[256,128]{1,0:T(8,128)(2,1)S(1)}, bf16[128,64]{1,0:T(8,128)(2,1)S(1)}, bf16[64,128]{1,0:T(8,128)(2,1)S(1)}, f32[64,128]{1,0:T(8,128)S(1)}) custom-call(bf16[128,128,128]{2,1,0:T(8,128)(2,1)S(1)} %get-tuple-element.20.proj, s32[1,128]{1,0:T(1,128)S(1)} %get-tuple-element.21.rows, ...), custom_call_target="tpu_custom_call" | custom-call | bytes 1048576 | tf_op jit(solution)/shard_map/name_places/pallas_call | solution.py:247
  11.5 1.6 %collective-permute-done.1 = f32[256,128]{1,0:T(8,128)S(1)} collective-permute-done((f32[256,128]{1,0:T(8,128)S(1)}, f32[256,128]{1,0:T(8,128)S(1)}, u32[]{:S(2)}, u32[]{:S(2)}) %collective-permute-start.1) | collective-permute-done | bytes 131104 | tf_op jit(solution)/shard_map/ppermute | solution.py:186
  13.0 4.2 %collective-permute-done.2 = f32[256,128]{1,0:T(8,128)S(1)} collective-permute-done((f32[256,128]{1,0:T(8,128)S(1)}, f32[256,128]{1,0:T(8,128)S(1)}, u32[]{:S(2)}, u32[]{:S(2)}) %collective-permute-start.2) | collective-permute-done | bytes 131104 | tf_op jit(solution)/shard_map/ppermute | solution.py:186
  17.3 1.6 %collective-permute-start.7 = (f32[64,128]{1,0:T(8,128)S(1)}, f32[64,128]{1,0:T(8,128)S(1)}, u32[]{:S(2)}, u32[]{:S(2)}) collective-permute-start(f32[64,128]{1,0:T(8,128)S(1)} %get-tuple-element.32), channel_id=1, source_target_pairs={{0,1},{1,0},{2,3},{3,2},{4,5},{5,4},{6,7},{7,6},{8,9},{9,8},{10,11... | collective-permute-start | bytes 98312 | tf_op jit(solution)/shard_map/ppermute | solution.py:186
  19.0 0.9 %first_backward.1 = f32[64,128]{1,0:T(8,128)S(1)} custom-call(bf16[128,128,128]{2,1,0:T(8,128)(2,1)S(1)} %get-tuple-element.20.proj, bf16[128,256]{1,0:T(8,128)(2,1)S(1)} %get-tuple-element.26.picks, bf16[64,128]{1,0:T(8,128)(2,1)S(1)} %get-tuple-element.27.places, bf16[128,128]{1,0:T(8,128)(2,1)S(1)} %fusion.mine, ...), custom_call_target="tpu_custom_call" | custom-call | tf_op jit(solution)/shard_map/first_backward/pallas_call | solution.py:273
  19.9 1.2 %collective-permute-start.5 = (f32[64,128]{1,0:T(8,128)S(1)}, f32[64,128]{1,0:T(8,128)S(1)}, u32[]{:S(2)}, u32[]{:S(2)}) collective-permute-start(f32[64,128]{1,0:T(8,128)S(1)} %first_backward.1), channel_id=1, source_target_pairs={{0,1},{1,0},{2,3},{3,2},{4,5},{5,4},{6,7},{7,6},{8,9},{9,8},{10,11... | collective-permute-start | bytes 98312 | tf_op jit(solution)/shard_map/ppermute | solution.py:186
  21.1 0.2 collective-permute-done.7
  21.3 2.6 %collective-permute-start.8 = (f32[64,128]{1,0:T(8,128)S(1)}, f32[64,128]{1,0:T(8,128)S(1)}, u32[]{:S(2)}, u32[]{:S(2)}) collective-permute-start(f32[64,128]{1,0:T(8,128)S(1)} %add.54), channel_id=1, source_target_pairs={{0,2},{1,3},{2,0},{3,1},{4,6},{5,7},{6,4},{7,5},{8,10},{9,11},{10,... | collective-permute-start | bytes 98312 | tf_op jit(solution)/shard_map/ppermute | solution.py:186
  23.9 2.6 %collective-permute-start.6 = (f32[64,128]{1,0:T(8,128)S(1)}, f32[64,128]{1,0:T(8,128)S(1)}, u32[]{:S(2)}, u32[]{:S(2)}) collective-permute-start(f32[64,128]{1,0:T(8,128)S(1)} %add.52), channel_id=1, source_target_pairs={{0,2},{1,3},{2,0},{3,1},{4,6},{5,7},{6,4},{7,5},{8,10},{9,11},{10,... | collective-permute-start | bytes 98312 | tf_op jit(solution)/shard_map/ppermute | solution.py:186
  26.5 1.1 %turn_blocks.1.proj = bf16[128,128,128]{2,1,0:T(8,128)(2,1)S(1)} custom-call(bf16[128,128,128]{2,1,0:T(8,128)(2,1)S(1)} %get-tuple-element.20.proj), custom_call_target="tpu_custom_call" | custom-call | bytes 8388608 | tf_op jit(solution)/shard_map/turn_blocks/pallas_call | solution.py:259
  27.7 1.1 %collective-permute-done.6 = f32[64,128]{1,0:T(8,128)S(1)} collective-permute-done((f32[64,128]{1,0:T(8,128)S(1)}, f32[64,128]{1,0:T(8,128)S(1)}, u32[]{:S(2)}, u32[]{:S(2)}) %collective-permute-start.6) | collective-permute-done | bytes 32800 | tf_op jit(solution)/shard_map/ppermute | solution.py:186
  28.8 1.0 %next_forward.1 = (f32[64,128]{1,0:T(8,128)S(1)}, f32[64,128]{1,0:T(8,128)S(1)}, f32[128,128]{1,0:T(8,128)S(1)}, f32[128,128]{1,0:T(8,128)S(1)}) custom-call(bf16[128,128,128]{2,1,0:T(8,128)(2,1)S(1)} %turn_blocks.1.proj, bf16[128,64]{1,0:T(8,128)(2,1)S(1)} %get-tuple-element.23.picks, bf16[256,128]{1,0:T(8,128)(2,1)S(1)} %get-tuple-element.24.places, ...), custom_call_target="tpu_custom_call" | custom-call | tf_op jit(solution)/shard_map/next_forward/pallas_call | solution.py:283
  29.9 1.2 %collective-permute-done.9 = f32[128,128]{1,0:T(8,128)S(1)} collective-permute-done((f32[128,128]{1,0:T(8,128)S(1)}, f32[128,128]{1,0:T(8,128)S(1)}, u32[]{:S(2)}, u32[]{:S(2)}) %collective-permute-start.9) | collective-permute-done | bytes 65568 | tf_op jit(solution)/shard_map/ppermute | solution.py:186
  31.2 1.3 %collective-permute-start.10 = (f32[128,128]{1,0:T(8,128)S(1)}, f32[128,128]{1,0:T(8,128)S(1)}, u32[]{:S(2)}, u32[]{:S(2)}) collective-permute-start(f32[128,128]{1,0:T(8,128)S(1)} %add.56), channel_id=1, source_target_pairs={{0,8},{4,12},{8,0},{12,4},{16,24},{20,28},{24,16},{28,20},{1,9},{5... | collective-permute-start | bytes 196616 | tf_op jit(solution)/shard_map/ppermute | solution.py:186
  32.5 0.8 %collective-permute-start.11 = (f32[128,128]{1,0:T(8,128)S(1)}, f32[128,128]{1,0:T(8,128)S(1)}, u32[]{:S(2)}, u32[]{:S(2)}) collective-permute-start(f32[128,128]{1,0:T(8,128)S(1)} %add.56), channel_id=1, source_target_pairs={{0,16},{4,20},{8,24},{12,28},{16,0},{20,4},{24,8},{28,12},{1,17},{... | collective-permute-start | bytes 196616 | tf_op jit(solution)/shard_map/ppermute | solution.py:186
  33.3 1.4 %collective-permute-start.12 = (f32[128,128]{1,0:T(8,128)S(1)}, f32[128,128]{1,0:T(8,128)S(1)}, u32[]{:S(2)}, u32[]{:S(2)}) collective-permute-start(f32[128,128]{1,0:T(8,128)S(1)} %add.56), channel_id=1, source_target_pairs={{0,24},{4,28},{8,16},{12,20},{16,8},{20,12},{24,0},{28,4},{1,25},{... | collective-permute-start | bytes 196616 | tf_op jit(solution)/shard_map/ppermute | solution.py:186
  34.7 0.8 %collective-permute-done.10 = f32[128,128]{1,0:T(8,128)S(1)} collective-permute-done((f32[128,128]{1,0:T(8,128)S(1)}, f32[128,128]{1,0:T(8,128)S(1)}, u32[]{:S(2)}, u32[]{:S(2)}) %collective-permute-start.10) | collective-permute-done | bytes 65568 | tf_op jit(solution)/shard_map/ppermute | solution.py:186
  35.5 1.9 %collective-permute-done.11 = f32[128,128]{1,0:T(8,128)S(1)} collective-permute-done((f32[128,128]{1,0:T(8,128)S(1)}, f32[128,128]{1,0:T(8,128)S(1)}, u32[]{:S(2)}, u32[]{:S(2)}) %collective-permute-start.11) | collective-permute-done | bytes 65568 | tf_op jit(solution)/shard_map/ppermute | solution.py:186
  37.4 1.0 %collective-permute-done.12 = f32[128,128]{1,0:T(8,128)S(1)} collective-permute-done((f32[128,128]{1,0:T(8,128)S(1)}, f32[128,128]{1,0:T(8,128)S(1)}, u32[]{:S(2)}, u32[]{:S(2)}) %collective-permute-start.12) | collective-permute-done | bytes 65568 | tf_op jit(solution)/shard_map/ppermute | solution.py:186
  38.6 1.2 %collective-permute-done.13.theirs = bf16[128,128]{1,0:T(8,128)(2,1)S(1)} collective-permute-done((bf16[128,128]{1,0:T(8,128)(2,1)S(1)}, bf16[128,128]{1,0:T(8,128)(2,1)S(1)}, u32[]{:S(2)}, u32[]{:S(2)}) %collective-permute-start.13) | collective-permute-done | bytes 32800 | tf_op jit(solution)/shard_map/ppermute | solution.py:186
  39.7 0.9 %last_backward.1 = f32[64,128]{1,0:T(8,128)S(1)} custom-call(bf16[128,128,128]{2,1,0:T(8,128)(2,1)S(1)} %get-tuple-element.20.proj, bf16[128,256]{1,0:T(8,128)(2,1)S(1)} %get-tuple-element.26.picks, bf16[64,128]{1,0:T(8,128)(2,1)S(1)} %get-tuple-element.27.places, bf16[128,128]{1,0:T(8,128)(2,1)S(1)} %get-tuple-element.38.mine, ...), custom_call_target="tpu_custom_call" | custom-call | tf_op jit(solution)/shard_map/last_backward/pallas_call | solution.py:296
  40.7 1.6 %collective-permute-start.14 = (f32[64,128]{1,0:T(8,128)S(1)}, f32[64,128]{1,0:T(8,128)S(1)}, u32[]{:S(2)}, u32[]{:S(2)}) collective-permute-start(f32[64,128]{1,0:T(8,128)S(1)} %last_backward.1), channel_id=1, source_target_pairs={{0,1},{1,0},{2,3},{3,2},{4,5},{5,4},{6,7},{7,6},{8,9},{9,8},{10,11... | collective-permute-start | bytes 98312 | tf_op jit(solution)/shard_map/ppermute | solution.py:186
  42.3 2.3 %collective-permute-done.14 = f32[64,128]{1,0:T(8,128)S(1)} collective-permute-done((f32[64,128]{1,0:T(8,128)S(1)}, f32[64,128]{1,0:T(8,128)S(1)}, u32[]{:S(2)}, u32[]{:S(2)}) %collective-permute-start.14) | collective-permute-done | bytes 32800 | tf_op jit(solution)/shard_map/ppermute | solution.py:186
  44.7 2.5 %collective-permute-start.15 = (f32[64,128]{1,0:T(8,128)S(1)}, f32[64,128]{1,0:T(8,128)S(1)}, u32[]{:S(2)}, u32[]{:S(2)}) collective-permute-start(f32[64,128]{1,0:T(8,128)S(1)} %add.60), channel_id=1, source_target_pairs={{0,2},{1,3},{2,0},{3,1},{4,6},{5,7},{6,4},{7,5},{8,10},{9,11},{10,... | collective-permute-start | bytes 98312 | tf_op jit(solution)/shard_map/ppermute | solution.py:186
  47.2 0.6 %constant_dynamic-slice_fusion = f32[32,128]{1,0:T(8,128)} fusion(f32[128,128]{1,0:T(8,128)S(1)} %get-tuple-element.39, s32[]{:T(128)S(6)} %select_n.3), kind=kLoop, calls=%fused_computation.7 | loop fusion | bytes 32772 | tf_op jit(solution)/shard_map/dynamic_slice | solution.py:294
  47.8 1.7 %collective-permute-done.15 = f32[64,128]{1,0:T(8,128)S(1)} collective-permute-done((f32[64,128]{1,0:T(8,128)S(1)}, f32[64,128]{1,0:T(8,128)S(1)}, u32[]{:S(2)}, u32[]{:S(2)}) %collective-permute-start.15) | collective-permute-done | bytes 32800 | tf_op jit(solution)/shard_map/ppermute | solution.py:186
  49.5 0.6 %multiply_add_fusion = f32[64,128]{1,0:T(8,128)} fusion(f32[64,128]{1,0:T(8,128)S(1)} %get-tuple-element.34, f32[64,128]{1,0:T(8,128)S(1)} %get-tuple-element.35, f32[64,128]{1,0:T(8,128)S(1)} %add.60, f32[64,128]{1,0:T(8,128)S(1)} %collective-permute-done.15), kind=kLoop, calls=%fused_computation.6 | loop fusion | flops 24576 | bytes 163840 | tf_op jit(solution)/shard_map/add | solution.py:305
  (18 shorter events, 0.4 us)
Async XLA Ops:
  4.7 1.5 %collective-permute-start = (f32[256,128]{1,0:T(8,128)S(1)}, f32[256,128]{1,0:T(8,128)S(1)}, u32[]{:S(2)}, u32[]{:S(2)}) collective-permute-start(f32[256,128]{1,0:T(8,128)S(1)} %get-tuple-element.29), channel_id=1, source_target_pairs={{0,4},{4,0},{8,12},{12,8},{16,20},{20,16},{24,28},{28,24},{1,5},{5... | collective-permute-start | bytes 393224 | tf_op jit(solution)/shard_map/ppermute | solution.py:186
  6.2 6.8 %collective-permute-start.1 = (f32[256,128]{1,0:T(8,128)S(1)}, f32[256,128]{1,0:T(8,128)S(1)}, u32[]{:S(2)}, u32[]{:S(2)}) collective-permute-start(f32[256,128]{1,0:T(8,128)S(1)} %add.48), channel_id=1, source_target_pairs={{0,8},{4,12},{8,0},{12,4},{16,24},{20,28},{24,16},{28,20},{1,9},{5... | collective-permute-start | bytes 393224 | tf_op jit(solution)/shard_map/ppermute | solution.py:186
  9.1 8.1 %collective-permute-start.2 = (f32[256,128]{1,0:T(8,128)S(1)}, f32[256,128]{1,0:T(8,128)S(1)}, u32[]{:S(2)}, u32[]{:S(2)}) collective-permute-start(f32[256,128]{1,0:T(8,128)S(1)} %add.48), channel_id=1, source_target_pairs={{0,16},{4,20},{8,24},{12,28},{16,0},{20,4},{24,8},{28,12},{1,17},{... | collective-permute-start | bytes 393224 | tf_op jit(solution)/shard_map/ppermute | solution.py:186
  10.6 6.6 %collective-permute-start.3 = (f32[256,128]{1,0:T(8,128)S(1)}, f32[256,128]{1,0:T(8,128)S(1)}, u32[]{:S(2)}, u32[]{:S(2)}) collective-permute-start(f32[256,128]{1,0:T(8,128)S(1)} %add.48), channel_id=1, source_target_pairs={{0,24},{4,28},{8,16},{12,20},{16,8},{20,12},{24,0},{28,4},{1,25},{... | collective-permute-start | bytes 393224 | tf_op jit(solution)/shard_map/ppermute | solution.py:186
  17.3 1.7 %collective-permute-start.4 = (bf16[128,128]{1,0:T(8,128)(2,1)S(1)}, bf16[128,128]{1,0:T(8,128)(2,1)S(1)}, u32[]{:S(2)}, u32[]{:S(2)}) collective-permute-start(bf16[128,128]{1,0:T(8,128)(2,1)S(1)} %fusion.mine), channel_id=1, source_target_pairs={{0,4},{4,0},{8,12},{12,8},{16,20},{20,16},{24,28},{28,24},{1,5},{5... | collective-permute-start | bytes 98312 | tf_op jit(solution)/shard_map/ppermute | solution.py:186
  17.3 4.0 %collective-permute-start.7 = (f32[64,128]{1,0:T(8,128)S(1)}, f32[64,128]{1,0:T(8,128)S(1)}, u32[]{:S(2)}, u32[]{:S(2)}) collective-permute-start(f32[64,128]{1,0:T(8,128)S(1)} %get-tuple-element.32), channel_id=1, source_target_pairs={{0,1},{1,0},{2,3},{3,2},{4,5},{5,4},{6,7},{7,6},{8,9},{9,8},{10,11... | collective-permute-start | bytes 98312 | tf_op jit(solution)/shard_map/ppermute | solution.py:186
  19.9 4.0 %collective-permute-start.5 = (f32[64,128]{1,0:T(8,128)S(1)}, f32[64,128]{1,0:T(8,128)S(1)}, u32[]{:S(2)}, u32[]{:S(2)}) collective-permute-start(f32[64,128]{1,0:T(8,128)S(1)} %first_backward.1), channel_id=1, source_target_pairs={{0,1},{1,0},{2,3},{3,2},{4,5},{5,4},{6,7},{7,6},{8,9},{9,8},{10,11... | collective-permute-start | bytes 98312 | tf_op jit(solution)/shard_map/ppermute | solution.py:186
  21.3 6.3 %collective-permute-start.8 = (f32[64,128]{1,0:T(8,128)S(1)}, f32[64,128]{1,0:T(8,128)S(1)}, u32[]{:S(2)}, u32[]{:S(2)}) collective-permute-start(f32[64,128]{1,0:T(8,128)S(1)} %add.54), channel_id=1, source_target_pairs={{0,2},{1,3},{2,0},{3,1},{4,6},{5,7},{6,4},{7,5},{8,10},{9,11},{10,... | collective-permute-start | bytes 98312 | tf_op jit(solution)/shard_map/ppermute | solution.py:186
  23.9 4.9 %collective-permute-start.6 = (f32[64,128]{1,0:T(8,128)S(1)}, f32[64,128]{1,0:T(8,128)S(1)}, u32[]{:S(2)}, u32[]{:S(2)}) collective-permute-start(f32[64,128]{1,0:T(8,128)S(1)} %add.52), channel_id=1, source_target_pairs={{0,2},{1,3},{2,0},{3,1},{4,6},{5,7},{6,4},{7,5},{8,10},{9,11},{10,... | collective-permute-start | bytes 98312 | tf_op jit(solution)/shard_map/ppermute | solution.py:186
  29.8 1.3 %collective-permute-start.9 = (f32[128,128]{1,0:T(8,128)S(1)}, f32[128,128]{1,0:T(8,128)S(1)}, u32[]{:S(2)}, u32[]{:S(2)}) collective-permute-start(f32[128,128]{1,0:T(8,128)S(1)} %get-tuple-element.37), channel_id=1, source_target_pairs={{0,4},{4,0},{8,12},{12,8},{16,20},{20,16},{24,28},{28,24},{1,5},{5... | collective-permute-start | bytes 196616 | tf_op jit(solution)/shard_map/ppermute | solution.py:186
  31.2 4.3 %collective-permute-start.10 = (f32[128,128]{1,0:T(8,128)S(1)}, f32[128,128]{1,0:T(8,128)S(1)}, u32[]{:S(2)}, u32[]{:S(2)}) collective-permute-start(f32[128,128]{1,0:T(8,128)S(1)} %add.56), channel_id=1, source_target_pairs={{0,8},{4,12},{8,0},{12,4},{16,24},{20,28},{24,16},{28,20},{1,9},{5... | collective-permute-start | bytes 196616 | tf_op jit(solution)/shard_map/ppermute | solution.py:186
  32.5 5.0 %collective-permute-start.11 = (f32[128,128]{1,0:T(8,128)S(1)}, f32[128,128]{1,0:T(8,128)S(1)}, u32[]{:S(2)}, u32[]{:S(2)}) collective-permute-start(f32[128,128]{1,0:T(8,128)S(1)} %add.56), channel_id=1, source_target_pairs={{0,16},{4,20},{8,24},{12,28},{16,0},{20,4},{24,8},{28,12},{1,17},{... | collective-permute-start | bytes 196616 | tf_op jit(solution)/shard_map/ppermute | solution.py:186
  33.3 5.2 %collective-permute-start.12 = (f32[128,128]{1,0:T(8,128)S(1)}, f32[128,128]{1,0:T(8,128)S(1)}, u32[]{:S(2)}, u32[]{:S(2)}) collective-permute-start(f32[128,128]{1,0:T(8,128)S(1)} %add.56), channel_id=1, source_target_pairs={{0,24},{4,28},{8,16},{12,20},{16,8},{20,12},{24,0},{28,4},{1,25},{... | collective-permute-start | bytes 196616 | tf_op jit(solution)/shard_map/ppermute | solution.py:186
  38.5 1.3 %collective-permute-start.13 = (bf16[128,128]{1,0:T(8,128)(2,1)S(1)}, bf16[128,128]{1,0:T(8,128)(2,1)S(1)}, u32[]{:S(2)}, u32[]{:S(2)}) collective-permute-start(bf16[128,128]{1,0:T(8,128)(2,1)S(1)} %get-tuple-element.38.mine), channel_id=1, source_target_pairs={{0,4},{4,0},{8,12},{12,8},{16,20},{20,16},{24,28},{28,24},{1,5},{5... | collective-permute-start | bytes 98312 | tf_op jit(solution)/shard_map/ppermute | solution.py:186
  40.7 4.0 %collective-permute-start.14 = (f32[64,128]{1,0:T(8,128)S(1)}, f32[64,128]{1,0:T(8,128)S(1)}, u32[]{:S(2)}, u32[]{:S(2)}) collective-permute-start(f32[64,128]{1,0:T(8,128)S(1)} %last_backward.1), channel_id=1, source_target_pairs={{0,1},{1,0},{2,3},{3,2},{4,5},{5,4},{6,7},{7,6},{8,9},{9,8},{10,11... | collective-permute-start | bytes 98312 | tf_op jit(solution)/shard_map/ppermute | solution.py:186
  44.7 4.8 %collective-permute-start.15 = (f32[64,128]{1,0:T(8,128)S(1)}, f32[64,128]{1,0:T(8,128)S(1)}, u32[]{:S(2)}, u32[]{:S(2)}) collective-permute-start(f32[64,128]{1,0:T(8,128)S(1)} %add.60), channel_id=1, source_target_pairs={{0,2},{1,3},{2,0},{3,1},{4,6},{5,7},{6,4},{7,5},{8,10},{9,11},{10,... | collective-permute-start | bytes 98312 | tf_op jit(solution)/shard_map/ppermute | solution.py:186

commit v6 on v5

--- a/solution.py
+++ b/solution.py
@@ -100,6 +100,26 @@
 def turn_blocks(proj, turned):
     for k in range(proj.shape[0]):
         turned[k] = proj[k].T
+
+
+def last_to_voxels(early, late, picks, places, mine, theirs, corr):
+    picked = dot(picks[...], join_halves(mine, theirs))
+    count = early.shape[0]
+    columns = [products(early, picked[:count]), products(late, picked[count:])]
+    corr[...] = collect(places[...], jnp.concatenate(columns, 0))
+
+
+def last_update(volume, weight, corr, far, mid, near, out):
+    out[...] = volume[...] + weight[...] * ((corr[...] + near[...]) + (mid[...] + far[...]))
+
+
+def fetch_blocks(start):
+    def kernel(proj_hbm, proj, sem):
+        copy = pltpu.make_async_copy(proj_hbm.at[pl.ds(start, proj.shape[0])], proj, sem)
+        copy.start()
+        copy.wait()
+
+    return kernel
 
 
 def put_partial(sums, sino, mine, theirs, ray_dev):
@@ -186,22 +206,27 @@
     return lax.ppermute(x, axis, [(i, i ^ bit) for i in range(size)])
 
 
-def over_slabs(mine, theirs, beside=None):
+def over_slabs(mine, theirs, beside=None, after=None):
     slabs = lax.axis_size("slab")
     x = mine + swap(theirs, "slab", 1)
+    if after is not None:
+        x, after = lax.optimization_barrier((x, after))
     bits = [1 << b for b in range(1, slabs.bit_length() - 1)]
+    waiting = beside is not None
     while bits:
         if len(bits) == 1:
             x, bits = x + swap(x, "slab", bits[0]), []
             continue
         first, second, bits = bits[0], bits[1], bits[2:]
         near = swap(x, "slab", first)
-        other = swap(x, "slab", second) , swap(x, "slab", first | second)
-        if beside is not None and not bits:
+        other = swap(x, "slab", second), swap(x, "slab", first | second)
+        if waiting and not bits:
             near, beside = lax.optimization_barrier((near, beside))
-            beside = beside + swap(beside, "angle", 1)
+            beside, waiting = beside + swap(beside, "angle", 1), False
         x = (x + near) + (other[0] + other[1])
-    return x if beside is None else (x, beside)
+    if waiting:
+        beside = beside + swap(beside, "angle", 1)
+    return x, after if beside is None else beside
 
 
 def over_angles(x, done=0):
@@ -288,21 +313,47 @@
         compiler_params=params,
         name="next_forward",
     )(turned, from_vox, to_rays, volume, corr, col_total, sino)
-    residual = row_weight * over_slabs(mine, theirs)
+    residual, projector = over_slabs(mine, theirs, None, projector)
+    count = blocks * 3 // 4
+    fetched = [
+        pl.pallas_call(
+            fetch_blocks(low),
+            out_shape=pltpu.VMEM((size,) + projector.shape[1:], BF16),
+            in_specs=[whole(pl.ANY)],
+            out_specs=whole(),
+            scratch_shapes=[pltpu.SemaphoreType.DMA],
+            compiler_params=params,
+            cost_estimate=pl.CostEstimate(flops=0, bytes_accessed=size << 16, transcendentals=0),
+            name="fetch_blocks",
+        )(pltpu.with_memory_space_constraint(projector, pltpu.HBM))
+        for low, size in ((0, count), (count, blocks - count))
+    ]
+    early, late = fetched
+    residual, early = lax.optimization_barrier((residual, early))
+    residual = row_weight * residual
     weighted = residual.astype(BF16)
     start = lax.div(lax.axis_index("slab"), 2) * ray_dev
     residual = lax.dynamic_slice_in_dim(residual, start, ray_dev)
 
     corr = pl.pallas_call(
-        to_voxels,
+        last_to_voxels,
         out_shape=vmem(vox_dev),
-        in_specs=[whole()] * 5,
+        in_specs=[whole()] * 6,
         out_specs=whole(),
         compiler_params=params,
         name="last_backward",
-    )(proj, from_rays, to_vox, weighted, swap(weighted, "slab", 1))
-    corr = over_angles(corr)
-    return volume + col_weight * corr, residual
+    )(early, late, from_rays, to_vox, weighted, swap(weighted, "slab", 1))
+    corr = over_angles(corr, 2)
+    far, mid, near = (swap(corr, "angle", bit) for bit in (3, 2, 1))
+    volume = pl.pallas_call(
+        last_update,
+        out_shape=jax.ShapeDtypeStruct((vox_dev, BLK), F32),
+        in_specs=[whole()] * 6,
+        out_specs=whole(),
+        compiler_params=params,
+        name="last_update",
+    )(volume, col_weight, corr, far, mid, near)
+    return volume, residual
 
 
 def solution(mesh):

time: 50.3 us -> 49.6 us (0.986)
  waiting for transfers between devices: 18.2 us -> 14 us
  Pallas kernels: 8.22 us -> 12 us
  other arithmetic: 0.75 us -> 0.14 us
    pallas_call x0 -> x4, Pallas kernels: none -> 4.71 us  [the longest x2 3.13 us: local(): pl.pallas_call(fetch_blocks(low), out_shape=pltpu.VMEM((size,) + projecto...]
    ppermute x16 -> x17, waiting for transfers between devices: 18.2 us -> 14 us  [swap(): return lax.ppermute(x, axis, [(i, i ^ bit) for i in range(size)])]
    pallas_call x2 -> x1, Pallas kernels: 1.89 us -> 0.94 us  [local(): pl.pallas_call(to_voxels, out_shape=vmem(vox_dev), in_specs=[whole()] * 5...]
    add x2 -> x1, other arithmetic: 0.63 us -> 0.01 us  [over_slabs(): beside, waiting = (beside + swap(beside, 'angle', 1), False)]
    ppermute x16 -> x17, starting transfers between devices: 20.9 us -> 21.2 us  [swap(): return lax.ppermute(x, axis, [(i, i ^ bit) for i in range(size)])]
  transfers between devices with their start and end apart: 16 -> 17, of which waited for: 12 -> 10; matrix products, arithmetic and copies ran while one was open for 1% -> 1% of each run, Pallas kernels for 6% -> 12%
where the time goes in v6:
time: 49.6 us; the launch traced here: 49.4 us
  starting transfers between devices  21.2 us (43%)
  waiting for transfers between devices  14 us (28%)
  Pallas kernels  12 us (24%)
  between operations  1.45 us (3%)
  local copies, waits for them, and re-layouts  0.61 us (1%)
    ppermute x17, starting transfers between devices, swap(): return lax.ppermute(x, axis, [(i, i ^ bit) for i in range(size)])  21.2 us
    ppermute x17, waiting for transfers between devices, swap(): return lax.ppermute(x, axis, [(i, i ^ bit) for i in range(size)])  14 us
    pallas_call x1, Pallas kernels, local(): pl.pallas_call(first_forward(slabs, capacity, ray_dev), out_shape=(pltpu....  3.4 us
    pallas_call x2, Pallas kernels, local(): pl.pallas_call(fetch_blocks(low), out_shape=pltpu.VMEM((size,) + projecto...  3.13 us
    pallas_call x1, Pallas kernels, local(): pl.pallas_call(turn_blocks, out_shape=pltpu.VMEM(projector.shape, BF16),...  1.13 us
    pallas_call x1, Pallas kernels, local(): pl.pallas_call(next_forward(ray_dev), out_shape=(vmem(vox_dev), vmem(vox_...  1 us
  transfers between devices with their start and end apart: 17, of which 10 were waited for; matrix products, arithmetic and copies ran while one was open for 1% of the time, Pallas kernels for 12%

profile of v6, /device:TPU:0, one launch (start us, length us, event | category | flops | bytes accessed | tf_op | source)
XLA Modules:
  0.0 49.4 jit_solution(1844597020683322722)
XLA Ops:
  1.3 3.4 %first_forward.1 = (bf16[128,128,128]{2,1,0:T(8,128)(2,1)S(1)}, s32[1,128]{1,0:T(1,128)S(1)}, s32[1,128]{1,0:T(1,128)S(1)}, f32[64,128]{1,0:T(8,128)S(1)}, f32[3...) custom-call(bf16[128,128,128]{2,1,0:T(8,128)(2,1)} %proj_hbm.3, s32[1,128]{1,0:T(1,128)} %bitcast.4, ...), custom_call_target="tpu_custom_call" | custom-call | tf_op jit(solution)/shard_map/first_forward/pallas_call | solution.py:254
  4.7 0.5 %collective-permute-start = (f32[256,128]{1,0:T(8,128)S(1)}, f32[256,128]{1,0:T(8,128)S(1)}, u32[]{:S(2)}, u32[]{:S(2)}) collective-permute-start(f32[256,128]{1,0:T(8,128)S(1)} %get-tuple-element.33), channel_id=1, source_target_pairs={{0,4},{4,0},{8,12},{12,8},{16,20},{20,16},{24,28},{28,24},{1,5},{5... | collective-permute-start | bytes 393224 | tf_op jit(solution)/shard_map/ppermute | solution.py:206
  5.2 1.0 %collective-permute-done = f32[256,128]{1,0:T(8,128)S(1)} collective-permute-done((f32[256,128]{1,0:T(8,128)S(1)}, f32[256,128]{1,0:T(8,128)S(1)}, u32[]{:S(2)}, u32[]{:S(2)}) %collective-permute-start) | collective-permute-done | bytes 131104 | tf_op jit(solution)/shard_map/ppermute | solution.py:206
  6.2 2.9 %collective-permute-start.1 = (f32[256,128]{1,0:T(8,128)S(1)}, f32[256,128]{1,0:T(8,128)S(1)}, u32[]{:S(2)}, u32[]{:S(2)}) collective-permute-start(f32[256,128]{1,0:T(8,128)S(1)} %add.39), channel_id=1, source_target_pairs={{0,8},{4,12},{8,0},{12,4},{16,24},{20,28},{24,16},{28,20},{1,9},{5... | collective-permute-start | bytes 393224 | tf_op jit(solution)/shard_map/ppermute | solution.py:206
  9.1 1.5 %collective-permute-start.2 = (f32[256,128]{1,0:T(8,128)S(1)}, f32[256,128]{1,0:T(8,128)S(1)}, u32[]{:S(2)}, u32[]{:S(2)}) collective-permute-start(f32[256,128]{1,0:T(8,128)S(1)} %add.39), channel_id=1, source_target_pairs={{0,16},{4,20},{8,24},{12,28},{16,0},{20,4},{24,8},{28,12},{1,17},{... | collective-permute-start | bytes 393224 | tf_op jit(solution)/shard_map/ppermute | solution.py:206
  10.7 0.8 %name_places.1 = (bf16[128,256]{1,0:T(8,128)(2,1)S(1)}, bf16[256,128]{1,0:T(8,128)(2,1)S(1)}, bf16[128,64]{1,0:T(8,128)(2,1)S(1)}, bf16[64,128]{1,0:T(8,128)(2,1)S(1)}, f32[64,128]{1,0:T(8,128)S(1)}) custom-call(bf16[128,128,128]{2,1,0:T(8,128)(2,1)S(1)} %get-tuple-element.24.proj, s32[1,128]{1,0:T(1,128)S(1)} %get-tuple-element.25.rows, ...), custom_call_target="tpu_custom_call" | custom-call | bytes 1048576 | tf_op jit(solution)/shard_map/name_places/pallas_call | solution.py:272
  11.5 1.6 %collective-permute-done.1 = f32[256,128]{1,0:T(8,128)S(1)} collective-permute-done((f32[256,128]{1,0:T(8,128)S(1)}, f32[256,128]{1,0:T(8,128)S(1)}, u32[]{:S(2)}, u32[]{:S(2)}) %collective-permute-start.1) | collective-permute-done | bytes 131104 | tf_op jit(solution)/shard_map/ppermute | solution.py:206
  13.0 4.2 %collective-permute-done.2 = f32[256,128]{1,0:T(8,128)S(1)} collective-permute-done((f32[256,128]{1,0:T(8,128)S(1)}, f32[256,128]{1,0:T(8,128)S(1)}, u32[]{:S(2)}, u32[]{:S(2)}) %collective-permute-start.2) | collective-permute-done | bytes 131104 | tf_op jit(solution)/shard_map/ppermute | solution.py:206
  17.3 1.6 %collective-permute-start.7 = (f32[64,128]{1,0:T(8,128)S(1)}, f32[64,128]{1,0:T(8,128)S(1)}, u32[]{:S(2)}, u32[]{:S(2)}) collective-permute-start(f32[64,128]{1,0:T(8,128)S(1)} %get-tuple-element.36), channel_id=1, source_target_pairs={{0,1},{1,0},{2,3},{3,2},{4,5},{5,4},{6,7},{7,6},{8,9},{9,8},{10,11... | collective-permute-start | bytes 98312 | tf_op jit(solution)/shard_map/ppermute | solution.py:206
  19.0 0.9 %first_backward.1 = f32[64,128]{1,0:T(8,128)S(1)} custom-call(bf16[128,128,128]{2,1,0:T(8,128)(2,1)S(1)} %get-tuple-element.24.proj, bf16[128,256]{1,0:T(8,128)(2,1)S(1)} %get-tuple-element.30.picks, bf16[64,128]{1,0:T(8,128)(2,1)S(1)} %get-tuple-element.31.places, bf16[128,128]{1,0:T(8,128)(2,1)S(1)} %fusion.mine, ...), custom_call_target="tpu_custom_call" | custom-call | tf_op jit(solution)/shard_map/first_backward/pallas_call | solution.py:298
  19.9 1.2 %collective-permute-start.5 = (f32[64,128]{1,0:T(8,128)S(1)}, f32[64,128]{1,0:T(8,128)S(1)}, u32[]{:S(2)}, u32[]{:S(2)}) collective-permute-start(f32[64,128]{1,0:T(8,128)S(1)} %first_backward.1), channel_id=1, source_target_pairs={{0,1},{1,0},{2,3},{3,2},{4,5},{5,4},{6,7},{7,6},{8,9},{9,8},{10,11... | collective-permute-start | bytes 98312 | tf_op jit(solution)/shard_map/ppermute | solution.py:206
  21.1 0.2 collective-permute-done.7
  21.3 2.6 %collective-permute-start.8 = (f32[64,128]{1,0:T(8,128)S(1)}, f32[64,128]{1,0:T(8,128)S(1)}, u32[]{:S(2)}, u32[]{:S(2)}) collective-permute-start(f32[64,128]{1,0:T(8,128)S(1)} %add.45), channel_id=1, source_target_pairs={{0,2},{1,3},{2,0},{3,1},{4,6},{5,7},{6,4},{7,5},{8,10},{9,11},{10,... | collective-permute-start | bytes 98312 | tf_op jit(solution)/shard_map/ppermute | solution.py:206
  23.9 2.6 %collective-permute-start.6 = (f32[64,128]{1,0:T(8,128)S(1)}, f32[64,128]{1,0:T(8,128)S(1)}, u32[]{:S(2)}, u32[]{:S(2)}) collective-permute-start(f32[64,128]{1,0:T(8,128)S(1)} %add.43), channel_id=1, source_target_pairs={{0,2},{1,3},{2,0},{3,1},{4,6},{5,7},{6,4},{7,5},{8,10},{9,11},{10,... | collective-permute-start | bytes 98312 | tf_op jit(solution)/shard_map/ppermute | solution.py:206
  26.5 1.1 %turn_blocks.1.proj = bf16[128,128,128]{2,1,0:T(8,128)(2,1)S(1)} custom-call(bf16[128,128,128]{2,1,0:T(8,128)(2,1)S(1)} %get-tuple-element.24.proj), custom_call_target="tpu_custom_call" | custom-call | bytes 8388608 | tf_op jit(solution)/shard_map/turn_blocks/pallas_call | solution.py:284
  27.7 1.1 %collective-permute-done.6 = f32[64,128]{1,0:T(8,128)S(1)} collective-permute-done((f32[64,128]{1,0:T(8,128)S(1)}, f32[64,128]{1,0:T(8,128)S(1)}, u32[]{:S(2)}, u32[]{:S(2)}) %collective-permute-start.6) | collective-permute-done | bytes 32800 | tf_op jit(solution)/shard_map/ppermute | solution.py:206
  28.8 1.0 %next_forward.1 = (f32[64,128]{1,0:T(8,128)S(1)}, f32[64,128]{1,0:T(8,128)S(1)}, f32[128,128]{1,0:T(8,128)S(1)}, f32[128,128]{1,0:T(8,128)S(1)}) custom-call(bf16[128,128,128]{2,1,0:T(8,128)(2,1)S(1)} %turn_blocks.1.proj, bf16[128,64]{1,0:T(8,128)(2,1)S(1)} %get-tuple-element.27.picks, bf16[256,128]{1,0:T(8,128)(2,1)S(1)} %get-tuple-element.28.places, ...), custom_call_target="tpu_custom_call" | custom-call | tf_op jit(solution)/shard_map/next_forward/pallas_call | solution.py:308
  29.9 1.2 %collective-permute-done.9 = f32[128,128]{1,0:T(8,128)S(1)} collective-permute-done((f32[128,128]{1,0:T(8,128)S(1)}, f32[128,128]{1,0:T(8,128)S(1)}, u32[]{:S(2)}, u32[]{:S(2)}) %collective-permute-start.9) | collective-permute-done | bytes 65568 | tf_op jit(solution)/shard_map/ppermute | solution.py:206
  31.2 1.3 %collective-permute-start.10 = (f32[128,128]{1,0:T(8,128)S(1)}, f32[128,128]{1,0:T(8,128)S(1)}, u32[]{:S(2)}, u32[]{:S(2)}) collective-permute-start(f32[128,128]{1,0:T(8,128)S(1)} %add.47), channel_id=1, source_target_pairs={{0,8},{4,12},{8,0},{12,4},{16,24},{20,28},{24,16},{28,20},{1,9},{5... | collective-permute-start | bytes 196616 | tf_op jit(solution)/shard_map/ppermute | solution.py:206
  32.5 0.8 %collective-permute-start.11 = (f32[128,128]{1,0:T(8,128)S(1)}, f32[128,128]{1,0:T(8,128)S(1)}, u32[]{:S(2)}, u32[]{:S(2)}) collective-permute-start(f32[128,128]{1,0:T(8,128)S(1)} %add.47), channel_id=1, source_target_pairs={{0,16},{4,20},{8,24},{12,28},{16,0},{20,4},{24,8},{28,12},{1,17},{... | collective-permute-start | bytes 196616 | tf_op jit(solution)/shard_map/ppermute | solution.py:206
  33.3 1.4 %collective-permute-start.12 = (f32[128,128]{1,0:T(8,128)S(1)}, f32[128,128]{1,0:T(8,128)S(1)}, u32[]{:S(2)}, u32[]{:S(2)}) collective-permute-start(f32[128,128]{1,0:T(8,128)S(1)} %add.47), channel_id=1, source_target_pairs={{0,24},{4,28},{8,16},{12,20},{16,8},{20,12},{24,0},{28,4},{1,25},{... | collective-permute-start | bytes 196616 | tf_op jit(solution)/shard_map/ppermute | solution.py:206
  34.7 1.9 %fetch_blocks.2.early = bf16[96,128,128]{2,1,0:T(8,128)(2,1)S(1)} custom-call(bf16[128,128,128]{2,1,0:T(8,128)(2,1)} %proj_hbm.3), custom_call_target="tpu_custom_call" | custom-call | bytes 6291456 | tf_op jit(solution)/shard_map/fetch_blocks/pallas_call | solution.py:319
  36.6 0.8 %collective-permute-done.11 = f32[128,128]{1,0:T(8,128)S(1)} collective-permute-done((f32[128,128]{1,0:T(8,128)S(1)}, f32[128,128]{1,0:T(8,128)S(1)}, u32[]{:S(2)}, u32[]{:S(2)}) %collective-permute-start.11) | collective-permute-done | bytes 65568 | tf_op jit(solution)/shard_map/ppermute | solution.py:206
  37.4 1.0 %collective-permute-done.12 = f32[128,128]{1,0:T(8,128)S(1)} collective-permute-done((f32[128,128]{1,0:T(8,128)S(1)}, f32[128,128]{1,0:T(8,128)S(1)}, u32[]{:S(2)}, u32[]{:S(2)}) %collective-permute-start.12) | collective-permute-done | bytes 65568 | tf_op jit(solution)/shard_map/ppermute | solution.py:206
  38.6 1.2 %fetch_blocks.3.late = bf16[32,128,128]{2,1,0:T(8,128)(2,1)S(1)} custom-call(bf16[128,128,128]{2,1,0:T(8,128)(2,1)} %proj_hbm.3), custom_call_target="tpu_custom_call" | custom-call | bytes 2097152 | tf_op jit(solution)/shard_map/fetch_blocks/pallas_call | solution.py:319
  39.8 0.9 %last_backward.1.corr = f32[64,128]{1,0:T(8,128)S(1)} custom-call(bf16[96,128,128]{2,1,0:T(8,128)(2,1)S(1)} %fetch_blocks.2.early, bf16[32,128,128]{2,1,0:T(8,128)(2,1)S(1)} %fetch_blocks.3.late, bf16[128,256]{1,0:T(8,128)(2,1)S(1)} %get-tuple-element.30.picks, bf16[64,128]{1,0:T(8,128)(2,1)S(1)} %get-tuple-element.31.places, ...), custom_call_target="tpu_custom_call" | custom-call | tf_op jit(solution)/shard_map/last_backward/pallas_call | solution.py:338
  40.8 3.2 %collective-permute-start.14 = (f32[64,128]{1,0:T(8,128)S(1)}, f32[64,128]{1,0:T(8,128)S(1)}, u32[]{:S(2)}, u32[]{:S(2)}) collective-permute-start(f32[64,128]{1,0:T(8,128)S(1)} %last_backward.1.corr), channel_id=1, source_target_pairs={{0,3},{1,2},{2,1},{3,0},{4,7},{5,6},{6,5},{7,4},{8,11},{9,10},{10,... | collective-permute-start | bytes 98312 | tf_op jit(solution)/shard_map/ppermute | solution.py:206
  44.0 1.3 %collective-permute-start.16 = (f32[64,128]{1,0:T(8,128)S(1)}, f32[64,128]{1,0:T(8,128)S(1)}, u32[]{:S(2)}, u32[]{:S(2)}) collective-permute-start(f32[64,128]{1,0:T(8,128)S(1)} %last_backward.1.corr), channel_id=1, source_target_pairs={{0,1},{1,0},{2,3},{3,2},{4,5},{5,4},{6,7},{7,6},{8,9},{9,8},{10,11... | collective-permute-start | bytes 98312 | tf_op jit(solution)/shard_map/ppermute | solution.py:206
  45.2 0.6 %constant_dynamic-slice_fusion = f32[32,128]{1,0:T(8,128)} fusion(f32[128,128]{1,0:T(8,128)S(1)} %get-tuple-element.47, s32[]{:T(128)S(6)} %select_n.3), kind=kLoop, calls=%fused_computation.7 | loop fusion | bytes 32772 | tf_op jit(solution)/shard_map/dynamic_slice | solution.py:336
  45.9 0.7 %collective-permute-done.14.far = f32[64,128]{1,0:T(8,128)S(1)} collective-permute-done((f32[64,128]{1,0:T(8,128)S(1)}, f32[64,128]{1,0:T(8,128)S(1)}, u32[]{:S(2)}, u32[]{:S(2)}) %collective-permute-start.14) | collective-permute-done | bytes 32800 | tf_op jit(solution)/shard_map/ppermute | solution.py:206
  46.6 2.2 %collective-permute-done.15.mid = f32[64,128]{1,0:T(8,128)S(1)} collective-permute-done((f32[64,128]{1,0:T(8,128)S(1)}, f32[64,128]{1,0:T(8,128)S(1)}, u32[]{:S(2)}, u32[]{:S(2)}) %collective-permute-start.15) | collective-permute-done | bytes 32800 | tf_op jit(solution)/shard_map/ppermute | solution.py:206
  48.8 0.6 %last_update.1 = f32[64,128]{1,0:T(8,128)} custom-call(f32[64,128]{1,0:T(8,128)S(1)} %get-tuple-element.38.volume, f32[64,128]{1,0:T(8,128)S(1)} %get-tuple-element.39.weight, f32[64,128]{1,0:T(8,128)S(1)} %last_backward.1.corr, f32[64,128]{1,0:T(8,128)S(1)} %collective-permute-done.14.far, f32[64,128]{1,0:T(8,128)S(1)} %collective-permute-done.15.mid, ...), custom_call_target="tpu_custom_call" | custom-call | tf_op jit(solution)/shard_map/last_update/pallas_call | solution.py:348
  (22 shorter events, 0.4 us)
Async XLA Ops:
  4.7 1.5 %collective-permute-start = (f32[256,128]{1,0:T(8,128)S(1)}, f32[256,128]{1,0:T(8,128)S(1)}, u32[]{:S(2)}, u32[]{:S(2)}) collective-permute-start(f32[256,128]{1,0:T(8,128)S(1)} %get-tuple-element.33), channel_id=1, source_target_pairs={{0,4},{4,0},{8,12},{12,8},{16,20},{20,16},{24,28},{28,24},{1,5},{5... | collective-permute-start | bytes 393224 | tf_op jit(solution)/shard_map/ppermute | solution.py:206
  6.2 6.8 %collective-permute-start.1 = (f32[256,128]{1,0:T(8,128)S(1)}, f32[256,128]{1,0:T(8,128)S(1)}, u32[]{:S(2)}, u32[]{:S(2)}) collective-permute-start(f32[256,128]{1,0:T(8,128)S(1)} %add.39), channel_id=1, source_target_pairs={{0,8},{4,12},{8,0},{12,4},{16,24},{20,28},{24,16},{28,20},{1,9},{5... | collective-permute-start | bytes 393224 | tf_op jit(solution)/shard_map/ppermute | solution.py:206
  9.1 8.1 %collective-permute-start.2 = (f32[256,128]{1,0:T(8,128)S(1)}, f32[256,128]{1,0:T(8,128)S(1)}, u32[]{:S(2)}, u32[]{:S(2)}) collective-permute-start(f32[256,128]{1,0:T(8,128)S(1)} %add.39), channel_id=1, source_target_pairs={{0,16},{4,20},{8,24},{12,28},{16,0},{20,4},{24,8},{28,12},{1,17},{... | collective-permute-start | bytes 393224 | tf_op jit(solution)/shard_map/ppermute | solution.py:206
  10.6 6.6 %collective-permute-start.3 = (f32[256,128]{1,0:T(8,128)S(1)}, f32[256,128]{1,0:T(8,128)S(1)}, u32[]{:S(2)}, u32[]{:S(2)}) collective-permute-start(f32[256,128]{1,0:T(8,128)S(1)} %add.39), channel_id=1, source_target_pairs={{0,24},{4,28},{8,16},{12,20},{16,8},{20,12},{24,0},{28,4},{1,25},{... | collective-permute-start | bytes 393224 | tf_op jit(solution)/shard_map/ppermute | solution.py:206
  17.3 1.7 %collective-permute-start.4 = (bf16[128,128]{1,0:T(8,128)(2,1)S(1)}, bf16[128,128]{1,0:T(8,128)(2,1)S(1)}, u32[]{:S(2)}, u32[]{:S(2)}) collective-permute-start(bf16[128,128]{1,0:T(8,128)(2,1)S(1)} %fusion.mine), channel_id=1, source_target_pairs={{0,4},{4,0},{8,12},{12,8},{16,20},{20,16},{24,28},{28,24},{1,5},{5... | collective-permute-start | bytes 98312 | tf_op jit(solution)/shard_map/ppermute | solution.py:206
  17.3 4.0 %collective-permute-start.7 = (f32[64,128]{1,0:T(8,128)S(1)}, f32[64,128]{1,0:T(8,128)S(1)}, u32[]{:S(2)}, u32[]{:S(2)}) collective-permute-start(f32[64,128]{1,0:T(8,128)S(1)} %get-tuple-element.36), channel_id=1, source_target_pairs={{0,1},{1,0},{2,3},{3,2},{4,5},{5,4},{6,7},{7,6},{8,9},{9,8},{10,11... | collective-permute-start | bytes 98312 | tf_op jit(solution)/shard_map/ppermute | solution.py:206
  19.9 4.0 %collective-permute-start.5 = (f32[64,128]{1,0:T(8,128)S(1)}, f32[64,128]{1,0:T(8,128)S(1)}, u32[]{:S(2)}, u32[]{:S(2)}) collective-permute-start(f32[64,128]{1,0:T(8,128)S(1)} %first_backward.1), channel_id=1, source_target_pairs={{0,1},{1,0},{2,3},{3,2},{4,5},{5,4},{6,7},{7,6},{8,9},{9,8},{10,11... | collective-permute-start | bytes 98312 | tf_op jit(solution)/shard_map/ppermute | solution.py:206
  21.3 6.3 %collective-permute-start.8 = (f32[64,128]{1,0:T(8,128)S(1)}, f32[64,128]{1,0:T(8,128)S(1)}, u32[]{:S(2)}, u32[]{:S(2)}) collective-permute-start(f32[64,128]{1,0:T(8,128)S(1)} %add.45), channel_id=1, source_target_pairs={{0,2},{1,3},{2,0},{3,1},{4,6},{5,7},{6,4},{7,5},{8,10},{9,11},{10,... | collective-permute-start | bytes 98312 | tf_op jit(solution)/shard_map/ppermute | solution.py:206
  23.9 4.9 %collective-permute-start.6 = (f32[64,128]{1,0:T(8,128)S(1)}, f32[64,128]{1,0:T(8,128)S(1)}, u32[]{:S(2)}, u32[]{:S(2)}) collective-permute-start(f32[64,128]{1,0:T(8,128)S(1)} %add.43), channel_id=1, source_target_pairs={{0,2},{1,3},{2,0},{3,1},{4,6},{5,7},{6,4},{7,5},{8,10},{9,11},{10,... | collective-permute-start | bytes 98312 | tf_op jit(solution)/shard_map/ppermute | solution.py:206
  29.8 1.3 %collective-permute-start.9 = (f32[128,128]{1,0:T(8,128)S(1)}, f32[128,128]{1,0:T(8,128)S(1)}, u32[]{:S(2)}, u32[]{:S(2)}) collective-permute-start(f32[128,128]{1,0:T(8,128)S(1)} %get-tuple-element.41), channel_id=1, source_target_pairs={{0,4},{4,0},{8,12},{12,8},{16,20},{20,16},{24,28},{28,24},{1,5},{5... | collective-permute-start | bytes 196616 | tf_op jit(solution)/shard_map/ppermute | solution.py:206
  31.2 5.5 %collective-permute-start.10 = (f32[128,128]{1,0:T(8,128)S(1)}, f32[128,128]{1,0:T(8,128)S(1)}, u32[]{:S(2)}, u32[]{:S(2)}) collective-permute-start(f32[128,128]{1,0:T(8,128)S(1)} %add.47), channel_id=1, source_target_pairs={{0,8},{4,12},{8,0},{12,4},{16,24},{20,28},{24,16},{28,20},{1,9},{5... | collective-permute-start | bytes 196616 | tf_op jit(solution)/shard_map/ppermute | solution.py:206
  32.5 5.0 %collective-permute-start.11 = (f32[128,128]{1,0:T(8,128)S(1)}, f32[128,128]{1,0:T(8,128)S(1)}, u32[]{:S(2)}, u32[]{:S(2)}) collective-permute-start(f32[128,128]{1,0:T(8,128)S(1)} %add.47), channel_id=1, source_target_pairs={{0,16},{4,20},{8,24},{12,28},{16,0},{20,4},{24,8},{28,12},{1,17},{... | collective-permute-start | bytes 196616 | tf_op jit(solution)/shard_map/ppermute | solution.py:206
  33.3 5.2 %collective-permute-start.12 = (f32[128,128]{1,0:T(8,128)S(1)}, f32[128,128]{1,0:T(8,128)S(1)}, u32[]{:S(2)}, u32[]{:S(2)}) collective-permute-start(f32[128,128]{1,0:T(8,128)S(1)} %add.47), channel_id=1, source_target_pairs={{0,24},{4,28},{8,16},{12,20},{16,8},{20,12},{24,0},{28,4},{1,25},{... | collective-permute-start | bytes 196616 | tf_op jit(solution)/shard_map/ppermute | solution.py:206
  38.5 1.3 %collective-permute-start.13 = (bf16[128,128]{1,0:T(8,128)(2,1)S(1)}, bf16[128,128]{1,0:T(8,128)(2,1)S(1)}, u32[]{:S(2)}, u32[]{:S(2)}) collective-permute-start(bf16[128,128]{1,0:T(8,128)(2,1)S(1)} %get-tuple-element.46.mine), channel_id=1, source_target_pairs={{0,4},{4,0},{8,12},{12,8},{16,20},{20,16},{24,28},{28,24},{1,5},{5... | collective-permute-start | bytes 98312 | tf_op jit(solution)/shard_map/ppermute | solution.py:206
  40.8 5.8 %collective-permute-start.14 = (f32[64,128]{1,0:T(8,128)S(1)}, f32[64,128]{1,0:T(8,128)S(1)}, u32[]{:S(2)}, u32[]{:S(2)}) collective-permute-start(f32[64,128]{1,0:T(8,128)S(1)} %last_backward.1.corr), channel_id=1, source_target_pairs={{0,3},{1,2},{2,1},{3,0},{4,7},{5,6},{6,5},{7,4},{8,11},{9,10},{10,... | collective-permute-start | bytes 98312 | tf_op jit(solution)/shard_map/ppermute | solution.py:206
  43.9 4.8 %collective-permute-start.15 = (f32[64,128]{1,0:T(8,128)S(1)}, f32[64,128]{1,0:T(8,128)S(1)}, u32[]{:S(2)}, u32[]{:S(2)}) collective-permute-start(f32[64,128]{1,0:T(8,128)S(1)} %last_backward.1.corr), channel_id=1, source_target_pairs={{0,2},{1,3},{2,0},{3,1},{4,6},{5,7},{6,4},{7,5},{8,10},{9,11},{10,... | collective-permute-start | bytes 98312 | tf_op jit(solution)/shard_map/ppermute | solution.py:206
  44.0 4.8 %collective-permute-start.16 = (f32[64,128]{1,0:T(8,128)S(1)}, f32[64,128]{1,0:T(8,128)S(1)}, u32[]{:S(2)}, u32[]{:S(2)}) collective-permute-start(f32[64,128]{1,0:T(8,128)S(1)} %last_backward.1.corr), channel_id=1, source_target_pairs={{0,1},{1,0},{2,3},{3,2},{4,5},{5,4},{6,7},{7,6},{8,9},{9,8},{10,11... | collective-permute-start | bytes 98312 | tf_op jit(solution)/shard_map/ppermute | solution.py:206

commit v7 on v6

--- a/solution.py
+++ b/solution.py
@@ -10,6 +10,7 @@
 BF16 = jnp.bfloat16
 BLK = 128
 CHUNKS = 2
+ORDER = (1, 2, 3)
 
 
 def whole(space=pltpu.VMEM):
@@ -109,7 +110,7 @@
     corr[...] = collect(places[...], jnp.concatenate(columns, 0))
 
 
-def last_update(volume, weight, corr, far, mid, near, out):
+def last_update(volume, weight, corr, near, mid, far, out):
     out[...] = volume[...] + weight[...] * ((corr[...] + near[...]) + (mid[...] + far[...]))
 
 
@@ -186,10 +187,12 @@
 
 
 def next_forward(ray_dev):
-    def kernel(proj, picks, places, volume, corr, col_total, sino, volume_out, weight_out, mine, theirs):
-        weights = 1.0 / jnp.maximum(col_total[...], 1.0)
+    def kernel(proj, picks, places, volume, own, near, mid, far, sino, volume_out, weight_out, mine, theirs):
+        vox_dev = volume.shape[0]
+        sums = (own[...] + near[...]) + (mid[...] + far[...])
+        weights = 1.0 / jnp.maximum(sums[vox_dev:], 1.0)
         weight_out[...] = weights
-        updated = volume[...] + weights * corr[...]
+        updated = volume[...] + weights * sums[:vox_dev]
         volume_out[...] = updated
         sums = forward_turned(proj, updated, picks[...], places[...])
         put_partial(sums, sino[...], mine, theirs, ray_dev)
@@ -197,8 +200,10 @@
     return kernel
 
 
-def to_voxels(proj, picks, places, mine, theirs, corr):
-    corr[...] = backward(proj, join_halves(mine, theirs), picks[...], places[...])
+def first_backward(proj, picks, places, mine, theirs, col_total, corr):
+    vox_dev = col_total.shape[0]
+    corr[0:vox_dev, :] = backward(proj, join_halves(mine, theirs), picks[...], places[...])
+    corr[vox_dev:2 * vox_dev, :] = col_total[...]
 
 
 def swap(x, axis, bit):
@@ -206,13 +211,12 @@
     return lax.ppermute(x, axis, [(i, i ^ bit) for i in range(size)])
 
 
-def over_slabs(mine, theirs, beside=None, after=None):
+def over_slabs(mine, theirs, after=None):
     slabs = lax.axis_size("slab")
     x = mine + swap(theirs, "slab", 1)
     if after is not None:
         x, after = lax.optimization_barrier((x, after))
     bits = [1 << b for b in range(1, slabs.bit_length() - 1)]
-    waiting = beside is not None
     while bits:
         if len(bits) == 1:
             x, bits = x + swap(x, "slab", bits[0]), []
@@ -220,20 +224,15 @@
         first, second, bits = bits[0], bits[1], bits[2:]
         near = swap(x, "slab", first)
         other = swap(x, "slab", second), swap(x, "slab", first | second)
-        if waiting and not bits:
-            near, beside = lax.optimization_barrier((near, beside))
-            beside, waiting = beside + swap(beside, "angle", 1), False
         x = (x + near) + (other[0] + other[1])
-    if waiting:
-        beside = beside + swap(beside, "angle", 1)
-    return x, after if beside is None else beside
-
-
-def over_angles(x, done=0):
+    return x, after
+
+
+def over_angles(x):
     angles = lax.axis_size("angle")
-    for b in range(done, angles.bit_length() - 1):
+    for b in range(2, angles.bit_length() - 1):
         x = x + swap(x, "angle", 1 << b)
-    return x
+    return [x] + [swap(x, "angle", bit) for bit in ORDER]
 
 
 def local(projector, block_vox, block_slot, send_ray, block_count, prior, sinogram):
@@ -290,30 +289,28 @@
         cost_estimate=pl.CostEstimate(flops=0, bytes_accessed=2 * projector.size * 2, transcendentals=0),
         name="turn_blocks",
     )(proj)
-    sums, col_total = over_slabs(mine, theirs, col_total)
-    col_total = over_angles(col_total, 1)
+    sums, _ = over_slabs(mine, theirs)
     row_weight = 1.0 / jnp.maximum(sums[half:], 1.0)
     weighted = (row_weight * sums[:half]).astype(BF16)
 
     corr = pl.pallas_call(
-        to_voxels,
-        out_shape=vmem(vox_dev),
-        in_specs=[whole()] * 5,
+        first_backward,
+        out_shape=vmem(2 * vox_dev),
+        in_specs=[whole()] * 6,
         out_specs=whole(),
         compiler_params=params,
         name="first_backward",
-    )(proj, from_rays, to_vox, weighted, swap(weighted, "slab", 1))
-    corr = over_angles(corr)
+    )(proj, from_rays, to_vox, weighted, swap(weighted, "slab", 1), col_total)
 
     volume, col_weight, mine, theirs = pl.pallas_call(
         next_forward(ray_dev),
         out_shape=(vmem(vox_dev), vmem(vox_dev), vmem(half), vmem(half)),
-        in_specs=[whole()] * 7,
+        in_specs=[whole()] * 9,
         out_specs=(whole(),) * 4,
         compiler_params=params,
         name="next_forward",
-    )(turned, from_vox, to_rays, volume, corr, col_total, sino)
-    residual, projector = over_slabs(mine, theirs, None, projector)
+    )(turned, from_vox, to_rays, volume, *over_angles(corr), sino)
+    residual, projector = over_slabs(mine, theirs, projector)
     count = blocks * 3 // 4
     fetched = [
         pl.pallas_call(
@@ -343,8 +340,6 @@
         compiler_params=params,
         name="last_backward",
     )(early, late, from_rays, to_vox, weighted, swap(weighted, "slab", 1))
-    corr = over_angles(corr, 2)
-    far, mid, near = (swap(corr, "angle", bit) for bit in (3, 2, 1))
     volume = pl.pallas_call(
         last_update,
         out_shape=jax.ShapeDtypeStruct((vox_dev, BLK), F32),
@@ -352,7 +347,7 @@
         out_specs=whole(),
         compiler_params=params,
         name="last_update",
-    )(volume, col_weight, corr, far, mid, near)
+    )(volume, col_weight, *over_angles(corr))
     return volume, residual
 
 

time: 49.6 us -> 49 us (0.988)
  starting transfers between devices: 21.2 us -> 17.7 us
  waiting for transfers between devices: 14 us -> 17 us
    ppermute x17 -> x16, starting transfers between devices: 21.2 us -> 17.7 us  [swap(): return lax.ppermute(x, axis, [(i, i ^ bit) for i in range(size)])]
    ppermute x17 -> x16, waiting for transfers between devices: 14 us -> 17 us  [swap(): return lax.ppermute(x, axis, [(i, i ^ bit) for i in range(size)])]
  transfers between devices with their start and end apart: 17 -> 16, of which waited for: 10 -> 12; matrix products, arithmetic and copies ran while one was open for 1% -> 1% of each run, Pallas kernels for 12% -> 10%
where the time goes in v7:
time: 49 us; the launch traced here: 48.8 us
  starting transfers between devices  17.7 us (36%)
  waiting for transfers between devices  17 us (35%)
  Pallas kernels  12 us (24%)
  between operations  1.43 us (3%)
  local copies, waits for them, and re-layouts  0.61 us (1%)
    ppermute x16, starting transfers between devices, swap(): return lax.ppermute(x, axis, [(i, i ^ bit) for i in range(size)])  17.7 us
    ppermute x16, waiting for transfers between devices, swap(): return lax.ppermute(x, axis, [(i, i ^ bit) for i in range(size)])  17 us
    pallas_call x1, Pallas kernels, local(): pl.pallas_call(first_forward(slabs, capacity, ray_dev), out_shape=(pltpu....  3.4 us
    pallas_call x2, Pallas kernels, local(): pl.pallas_call(fetch_blocks(low), out_shape=pltpu.VMEM((size,) + projecto...  3.13 us
    pallas_call x1, Pallas kernels, local(): pl.pallas_call(turn_blocks, out_shape=pltpu.VMEM(projector.shape, BF16),...  1.13 us
    pallas_call x1, Pallas kernels, local(): pl.pallas_call(next_forward(ray_dev), out_shape=(vmem(vox_dev), vmem(vox_...  1.01 us
  transfers between devices with their start and end apart: 16, of which 12 were waited for; matrix products, arithmetic and copies ran while one was open for 1% of the time, Pallas kernels for 10%

profile of v7, /device:TPU:0, one launch (start us, length us, event | category | flops | bytes accessed | tf_op | source)
XLA Modules:
  0.0 48.8 jit_solution(17159849362809579979)
XLA Ops:
  1.3 3.4 %first_forward.1 = (bf16[128,128,128]{2,1,0:T(8,128)(2,1)S(1)}, s32[1,128]{1,0:T(1,128)S(1)}, s32[1,128]{1,0:T(1,128)S(1)}, f32[64,128]{1,0:T(8,128)S(1)}, f32[3...) custom-call(bf16[128,128,128]{2,1,0:T(8,128)(2,1)} %proj_hbm.3, s32[1,128]{1,0:T(1,128)} %bitcast.4, ...), custom_call_target="tpu_custom_call" | custom-call | tf_op jit(solution)/shard_map/first_forward/pallas_call | solution.py:253
  4.7 0.5 %collective-permute-start = (f32[256,128]{1,0:T(8,128)S(1)}, f32[256,128]{1,0:T(8,128)S(1)}, u32[]{:S(2)}, u32[]{:S(2)}) collective-permute-start(f32[256,128]{1,0:T(8,128)S(1)} %get-tuple-element.31), channel_id=1, source_target_pairs={{0,4},{4,0},{8,12},{12,8},{16,20},{20,16},{24,28},{28,24},{1,5},{5... | collective-permute-start | bytes 393224 | tf_op jit(solution)/shard_map/ppermute | solution.py:211
  5.2 1.0 %collective-permute-done = f32[256,128]{1,0:T(8,128)S(1)} collective-permute-done((f32[256,128]{1,0:T(8,128)S(1)}, f32[256,128]{1,0:T(8,128)S(1)}, u32[]{:S(2)}, u32[]{:S(2)}) %collective-permute-start) | collective-permute-done | bytes 131104 | tf_op jit(solution)/shard_map/ppermute | solution.py:211
  6.2 3.9 %collective-permute-start.3 = (f32[256,128]{1,0:T(8,128)S(1)}, f32[256,128]{1,0:T(8,128)S(1)}, u32[]{:S(2)}, u32[]{:S(2)}) collective-permute-start(f32[256,128]{1,0:T(8,128)S(1)} %add.27), channel_id=1, source_target_pairs={{0,24},{4,28},{8,16},{12,20},{16,8},{20,12},{24,0},{28,4},{1,25},{... | collective-permute-start | bytes 393224 | tf_op jit(solution)/shard_map/ppermute | solution.py:211
  10.1 0.5 %collective-permute-start.2 = (f32[256,128]{1,0:T(8,128)S(1)}, f32[256,128]{1,0:T(8,128)S(1)}, u32[]{:S(2)}, u32[]{:S(2)}) collective-permute-start(f32[256,128]{1,0:T(8,128)S(1)} %add.27), channel_id=1, source_target_pairs={{0,16},{4,20},{8,24},{12,28},{16,0},{20,4},{24,8},{28,12},{1,17},{... | collective-permute-start | bytes 393224 | tf_op jit(solution)/shard_map/ppermute | solution.py:211
  10.7 3.3 %collective-permute-done.3 = f32[256,128]{1,0:T(8,128)S(1)} collective-permute-done((f32[256,128]{1,0:T(8,128)S(1)}, f32[256,128]{1,0:T(8,128)S(1)}, u32[]{:S(2)}, u32[]{:S(2)}) %collective-permute-start.3) | collective-permute-done | bytes 131104 | tf_op jit(solution)/shard_map/ppermute | solution.py:211
  14.0 2.7 %collective-permute-done.2 = f32[256,128]{1,0:T(8,128)S(1)} collective-permute-done((f32[256,128]{1,0:T(8,128)S(1)}, f32[256,128]{1,0:T(8,128)S(1)}, u32[]{:S(2)}, u32[]{:S(2)}) %collective-permute-start.2) | collective-permute-done | bytes 131104 | tf_op jit(solution)/shard_map/ppermute | solution.py:211
  16.7 0.3 collective-permute-done.1
  17.1 0.8 %name_places.1 = (bf16[128,256]{1,0:T(8,128)(2,1)S(1)}, bf16[256,128]{1,0:T(8,128)(2,1)S(1)}, bf16[128,64]{1,0:T(8,128)(2,1)S(1)}, bf16[64,128]{1,0:T(8,128)(2,1)S(1)}, f32[64,128]{1,0:T(8,128)S(1)}) custom-call(bf16[128,128,128]{2,1,0:T(8,128)(2,1)S(1)} %get-tuple-element.22.proj, s32[1,128]{1,0:T(1,128)S(1)} %get-tuple-element.23.rows, ...), custom_call_target="tpu_custom_call" | custom-call | bytes 1048576 | tf_op jit(solution)/shard_map/name_places/pallas_call | solution.py:271
  17.9 0.4 collective-permute-done.4.theirs
  18.3 0.9 %first_backward.1.own = f32[128,128]{1,0:T(8,128)S(1)} custom-call(bf16[128,128,128]{2,1,0:T(8,128)(2,1)S(1)} %get-tuple-element.22.proj, bf16[128,256]{1,0:T(8,128)(2,1)S(1)} %get-tuple-element.28.picks, bf16[64,128]{1,0:T(8,128)(2,1)S(1)} %get-tuple-element.29.places, bf16[128,128]{1,0:T(8,128)(2,1)S(1)} %fusion.mine, ...), custom_call_target="tpu_custom_call" | custom-call | tf_op jit(solution)/shard_map/first_backward/pallas_call | solution.py:296
  19.3 3.7 %collective-permute-start.7 = (f32[128,128]{1,0:T(8,128)S(1)}, f32[128,128]{1,0:T(8,128)S(1)}, u32[]{:S(2)}, u32[]{:S(2)}) collective-permute-start(f32[128,128]{1,0:T(8,128)S(1)} %first_backward.1.own), channel_id=1, source_target_pairs={{0,3},{1,2},{2,1},{3,0},{4,7},{5,6},{6,5},{7,4},{8,11},{9,10},{10,... | collective-permute-start | bytes 196616 | tf_op jit(solution)/shard_map/ppermute | solution.py:211
  22.9 0.8 %collective-permute-start.5 = (f32[128,128]{1,0:T(8,128)S(1)}, f32[128,128]{1,0:T(8,128)S(1)}, u32[]{:S(2)}, u32[]{:S(2)}) collective-permute-start(f32[128,128]{1,0:T(8,128)S(1)} %first_backward.1.own), channel_id=1, source_target_pairs={{0,1},{1,0},{2,3},{3,2},{4,5},{5,4},{6,7},{7,6},{8,9},{9,8},{10,11... | collective-permute-start | bytes 196616 | tf_op jit(solution)/shard_map/ppermute | solution.py:211
  23.7 1.1 %turn_blocks.1.proj = bf16[128,128,128]{2,1,0:T(8,128)(2,1)S(1)} custom-call(bf16[128,128,128]{2,1,0:T(8,128)(2,1)S(1)} %get-tuple-element.22.proj), custom_call_target="tpu_custom_call" | custom-call | bytes 8388608 | tf_op jit(solution)/shard_map/turn_blocks/pallas_call | solution.py:283
  24.9 0.8 %collective-permute-done.7.far = f32[128,128]{1,0:T(8,128)S(1)} collective-permute-done((f32[128,128]{1,0:T(8,128)S(1)}, f32[128,128]{1,0:T(8,128)S(1)}, u32[]{:S(2)}, u32[]{:S(2)}) %collective-permute-start.7) | collective-permute-done | bytes 65568 | tf_op jit(solution)/shard_map/ppermute | solution.py:211
  25.6 3.2 %collective-permute-done.6.mid = f32[128,128]{1,0:T(8,128)S(1)} collective-permute-done((f32[128,128]{1,0:T(8,128)S(1)}, f32[128,128]{1,0:T(8,128)S(1)}, u32[]{:S(2)}, u32[]{:S(2)}) %collective-permute-start.6) | collective-permute-done | bytes 65568 | tf_op jit(solution)/shard_map/ppermute | solution.py:211
  28.8 1.0 %next_forward.1 = (f32[64,128]{1,0:T(8,128)S(1)}, f32[64,128]{1,0:T(8,128)S(1)}, f32[128,128]{1,0:T(8,128)S(1)}, f32[128,128]{1,0:T(8,128)S(1)}) custom-call(bf16[128,128,128]{2,1,0:T(8,128)(2,1)S(1)} %turn_blocks.1.proj, bf16[128,64]{1,0:T(8,128)(2,1)S(1)} %get-tuple-element.25.picks, bf16[256,128]{1,0:T(8,128)(2,1)S(1)} %get-tuple-element.26.places, ...), custom_call_target="tpu_custom_call" | custom-call | tf_op jit(solution)/shard_map/next_forward/pallas_call | solution.py:305
  29.9 1.2 %collective-permute-done.8 = f32[128,128]{1,0:T(8,128)S(1)} collective-permute-done((f32[128,128]{1,0:T(8,128)S(1)}, f32[128,128]{1,0:T(8,128)S(1)}, u32[]{:S(2)}, u32[]{:S(2)}) %collective-permute-start.8) | collective-permute-done | bytes 65568 | tf_op jit(solution)/shard_map/ppermute | solution.py:211
  31.2 1.7 %collective-permute-start.11 = (f32[128,128]{1,0:T(8,128)S(1)}, f32[128,128]{1,0:T(8,128)S(1)}, u32[]{:S(2)}, u32[]{:S(2)}) collective-permute-start(f32[128,128]{1,0:T(8,128)S(1)} %add.31), channel_id=1, source_target_pairs={{0,24},{4,28},{8,16},{12,20},{16,8},{20,12},{24,0},{28,4},{1,25},{... | collective-permute-start | bytes 196616 | tf_op jit(solution)/shard_map/ppermute | solution.py:211
  32.9 1.3 %collective-permute-start.10 = (f32[128,128]{1,0:T(8,128)S(1)}, f32[128,128]{1,0:T(8,128)S(1)}, u32[]{:S(2)}, u32[]{:S(2)}) collective-permute-start(f32[128,128]{1,0:T(8,128)S(1)} %add.31), channel_id=1, source_target_pairs={{0,16},{4,20},{8,24},{12,28},{16,0},{20,4},{24,8},{28,12},{1,17},{... | collective-permute-start | bytes 196616 | tf_op jit(solution)/shard_map/ppermute | solution.py:211
  34.2 0.5 %collective-permute-start.9 = (f32[128,128]{1,0:T(8,128)S(1)}, f32[128,128]{1,0:T(8,128)S(1)}, u32[]{:S(2)}, u32[]{:S(2)}) collective-permute-start(f32[128,128]{1,0:T(8,128)S(1)} %add.31), channel_id=1, source_target_pairs={{0,8},{4,12},{8,0},{12,4},{16,24},{20,28},{24,16},{28,20},{1,9},{5... | collective-permute-start | bytes 196616 | tf_op jit(solution)/shard_map/ppermute | solution.py:211
  34.7 1.9 %fetch_blocks.2.early = bf16[96,128,128]{2,1,0:T(8,128)(2,1)S(1)} custom-call(bf16[128,128,128]{2,1,0:T(8,128)(2,1)} %proj_hbm.3), custom_call_target="tpu_custom_call" | custom-call | bytes 6291456 | tf_op jit(solution)/shard_map/fetch_blocks/pallas_call | solution.py:316
  36.6 1.1 %collective-permute-done.10 = f32[128,128]{1,0:T(8,128)S(1)} collective-permute-done((f32[128,128]{1,0:T(8,128)S(1)}, f32[128,128]{1,0:T(8,128)S(1)}, u32[]{:S(2)}, u32[]{:S(2)}) %collective-permute-start.10) | collective-permute-done | bytes 65568 | tf_op jit(solution)/shard_map/ppermute | solution.py:211
  37.7 0.8 %collective-permute-done.9 = f32[128,128]{1,0:T(8,128)S(1)} collective-permute-done((f32[128,128]{1,0:T(8,128)S(1)}, f32[128,128]{1,0:T(8,128)S(1)}, u32[]{:S(2)}, u32[]{:S(2)}) %collective-permute-start.9) | collective-permute-done | bytes 65568 | tf_op jit(solution)/shard_map/ppermute | solution.py:211
  38.6 1.2 %fetch_blocks.3.late = bf16[32,128,128]{2,1,0:T(8,128)(2,1)S(1)} custom-call(bf16[128,128,128]{2,1,0:T(8,128)(2,1)} %proj_hbm.3), custom_call_target="tpu_custom_call" | custom-call | bytes 2097152 | tf_op jit(solution)/shard_map/fetch_blocks/pallas_call | solution.py:316
  39.9 0.9 %last_backward.1.corr = f32[64,128]{1,0:T(8,128)S(1)} custom-call(bf16[96,128,128]{2,1,0:T(8,128)(2,1)S(1)} %fetch_blocks.2.early, bf16[32,128,128]{2,1,0:T(8,128)(2,1)S(1)} %fetch_blocks.3.late, bf16[128,256]{1,0:T(8,128)(2,1)S(1)} %get-tuple-element.28.picks, bf16[64,128]{1,0:T(8,128)(2,1)S(1)} %get-tuple-element.29.places, ...), custom_call_target="tpu_custom_call" | custom-call | tf_op jit(solution)/shard_map/last_backward/pallas_call | solution.py:335
  40.8 2.5 %collective-permute-start.15 = (f32[64,128]{1,0:T(8,128)S(1)}, f32[64,128]{1,0:T(8,128)S(1)}, u32[]{:S(2)}, u32[]{:S(2)}) collective-permute-start(f32[64,128]{1,0:T(8,128)S(1)} %last_backward.1.corr), channel_id=1, source_target_pairs={{0,3},{1,2},{2,1},{3,0},{4,7},{5,6},{6,5},{7,4},{8,11},{9,10},{10,... | collective-permute-start | bytes 98312 | tf_op jit(solution)/shard_map/ppermute | solution.py:211
  43.5 1.8 %collective-permute-start.13 = (f32[64,128]{1,0:T(8,128)S(1)}, f32[64,128]{1,0:T(8,128)S(1)}, u32[]{:S(2)}, u32[]{:S(2)}) collective-permute-start(f32[64,128]{1,0:T(8,128)S(1)} %last_backward.1.corr), channel_id=1, source_target_pairs={{0,1},{1,0},{2,3},{3,2},{4,5},{5,4},{6,7},{7,6},{8,9},{9,8},{10,11... | collective-permute-start | bytes 98312 | tf_op jit(solution)/shard_map/ppermute | solution.py:211
  45.3 0.6 %constant_dynamic-slice_fusion = f32[32,128]{1,0:T(8,128)} fusion(f32[128,128]{1,0:T(8,128)S(1)} %get-tuple-element.43, s32[]{:T(128)S(6)} %select_n.3), kind=kLoop, calls=%fused_computation.7 | loop fusion | bytes 32772 | tf_op jit(solution)/shard_map/dynamic_slice | solution.py:333
  45.9 0.9 %collective-permute-done.15.far = f32[64,128]{1,0:T(8,128)S(1)} collective-permute-done((f32[64,128]{1,0:T(8,128)S(1)}, f32[64,128]{1,0:T(8,128)S(1)}, u32[]{:S(2)}, u32[]{:S(2)}) %collective-permute-start.15) | collective-permute-done | bytes 32800 | tf_op jit(solution)/shard_map/ppermute | solution.py:211
  46.8 1.4 %collective-permute-done.14.mid = f32[64,128]{1,0:T(8,128)S(1)} collective-permute-done((f32[64,128]{1,0:T(8,128)S(1)}, f32[64,128]{1,0:T(8,128)S(1)}, u32[]{:S(2)}, u32[]{:S(2)}) %collective-permute-start.14) | collective-permute-done | bytes 32800 | tf_op jit(solution)/shard_map/ppermute | solution.py:211
  48.2 0.6 %last_update.1 = f32[64,128]{1,0:T(8,128)} custom-call(f32[64,128]{1,0:T(8,128)S(1)} %get-tuple-element.34.volume, f32[64,128]{1,0:T(8,128)S(1)} %get-tuple-element.35.weight, f32[64,128]{1,0:T(8,128)S(1)} %last_backward.1.corr, f32[64,128]{1,0:T(8,128)S(1)} %collective-permute-done.13.near, f32[64,128]{1,0:T(8,128)S(1)} %collective-permute-done.14.mid, ...), custom_call_target="tpu_custom_call" | custom-call | tf_op jit(solution)/shard_map/last_update/pallas_call | solution.py:343
  (16 shorter events, 0.6 us)
Async XLA Ops:
  4.7 1.5 %collective-permute-start = (f32[256,128]{1,0:T(8,128)S(1)}, f32[256,128]{1,0:T(8,128)S(1)}, u32[]{:S(2)}, u32[]{:S(2)}) collective-permute-start(f32[256,128]{1,0:T(8,128)S(1)} %get-tuple-element.31), channel_id=1, source_target_pairs={{0,4},{4,0},{8,12},{12,8},{16,20},{20,16},{24,28},{28,24},{1,5},{5... | collective-permute-start | bytes 393224 | tf_op jit(solution)/shard_map/ppermute | solution.py:211
  6.2 7.8 %collective-permute-start.3 = (f32[256,128]{1,0:T(8,128)S(1)}, f32[256,128]{1,0:T(8,128)S(1)}, u32[]{:S(2)}, u32[]{:S(2)}) collective-permute-start(f32[256,128]{1,0:T(8,128)S(1)} %add.27), channel_id=1, source_target_pairs={{0,24},{4,28},{8,16},{12,20},{16,8},{20,12},{24,0},{28,4},{1,25},{... | collective-permute-start | bytes 393224 | tf_op jit(solution)/shard_map/ppermute | solution.py:211
  10.1 6.6 %collective-permute-start.2 = (f32[256,128]{1,0:T(8,128)S(1)}, f32[256,128]{1,0:T(8,128)S(1)}, u32[]{:S(2)}, u32[]{:S(2)}) collective-permute-start(f32[256,128]{1,0:T(8,128)S(1)} %add.27), channel_id=1, source_target_pairs={{0,16},{4,20},{8,24},{12,28},{16,0},{20,4},{24,8},{28,12},{1,17},{... | collective-permute-start | bytes 393224 | tf_op jit(solution)/shard_map/ppermute | solution.py:211
  10.6 6.4 %collective-permute-start.1 = (f32[256,128]{1,0:T(8,128)S(1)}, f32[256,128]{1,0:T(8,128)S(1)}, u32[]{:S(2)}, u32[]{:S(2)}) collective-permute-start(f32[256,128]{1,0:T(8,128)S(1)} %add.27), channel_id=1, source_target_pairs={{0,8},{4,12},{8,0},{12,4},{16,24},{20,28},{24,16},{28,20},{1,9},{5... | collective-permute-start | bytes 393224 | tf_op jit(solution)/shard_map/ppermute | solution.py:211
  17.0 1.3 %collective-permute-start.4 = (bf16[128,128]{1,0:T(8,128)(2,1)S(1)}, bf16[128,128]{1,0:T(8,128)(2,1)S(1)}, u32[]{:S(2)}, u32[]{:S(2)}) collective-permute-start(bf16[128,128]{1,0:T(8,128)(2,1)S(1)} %fusion.mine), channel_id=1, source_target_pairs={{0,4},{4,0},{8,12},{12,8},{16,20},{20,16},{24,28},{28,24},{1,5},{5... | collective-permute-start | bytes 98312 | tf_op jit(solution)/shard_map/ppermute | solution.py:211
  19.3 6.3 %collective-permute-start.7 = (f32[128,128]{1,0:T(8,128)S(1)}, f32[128,128]{1,0:T(8,128)S(1)}, u32[]{:S(2)}, u32[]{:S(2)}) collective-permute-start(f32[128,128]{1,0:T(8,128)S(1)} %first_backward.1.own), channel_id=1, source_target_pairs={{0,3},{1,2},{2,1},{3,0},{4,7},{5,6},{6,5},{7,4},{8,11},{9,10},{10,... | collective-permute-start | bytes 196616 | tf_op jit(solution)/shard_map/ppermute | solution.py:211
  22.9 5.9 %collective-permute-start.6 = (f32[128,128]{1,0:T(8,128)S(1)}, f32[128,128]{1,0:T(8,128)S(1)}, u32[]{:S(2)}, u32[]{:S(2)}) collective-permute-start(f32[128,128]{1,0:T(8,128)S(1)} %first_backward.1.own), channel_id=1, source_target_pairs={{0,2},{1,3},{2,0},{3,1},{4,6},{5,7},{6,4},{7,5},{8,10},{9,11},{10,... | collective-permute-start | bytes 196616 | tf_op jit(solution)/shard_map/ppermute | solution.py:211
  22.9 5.9 %collective-permute-start.5 = (f32[128,128]{1,0:T(8,128)S(1)}, f32[128,128]{1,0:T(8,128)S(1)}, u32[]{:S(2)}, u32[]{:S(2)}) collective-permute-start(f32[128,128]{1,0:T(8,128)S(1)} %first_backward.1.own), channel_id=1, source_target_pairs={{0,1},{1,0},{2,3},{3,2},{4,5},{5,4},{6,7},{7,6},{8,9},{9,8},{10,11... | collective-permute-start | bytes 196616 | tf_op jit(solution)/shard_map/ppermute | solution.py:211
  29.8 1.3 %collective-permute-start.8 = (f32[128,128]{1,0:T(8,128)S(1)}, f32[128,128]{1,0:T(8,128)S(1)}, u32[]{:S(2)}, u32[]{:S(2)}) collective-permute-start(f32[128,128]{1,0:T(8,128)S(1)} %get-tuple-element.37), channel_id=1, source_target_pairs={{0,4},{4,0},{8,12},{12,8},{16,20},{20,16},{24,28},{28,24},{1,5},{5... | collective-permute-start | bytes 196616 | tf_op jit(solution)/shard_map/ppermute | solution.py:211
  31.2 5.5 %collective-permute-start.11 = (f32[128,128]{1,0:T(8,128)S(1)}, f32[128,128]{1,0:T(8,128)S(1)}, u32[]{:S(2)}, u32[]{:S(2)}) collective-permute-start(f32[128,128]{1,0:T(8,128)S(1)} %add.31), channel_id=1, source_target_pairs={{0,24},{4,28},{8,16},{12,20},{16,8},{20,12},{24,0},{28,4},{1,25},{... | collective-permute-start | bytes 196616 | tf_op jit(solution)/shard_map/ppermute | solution.py:211
  32.9 4.8 %collective-permute-start.10 = (f32[128,128]{1,0:T(8,128)S(1)}, f32[128,128]{1,0:T(8,128)S(1)}, u32[]{:S(2)}, u32[]{:S(2)}) collective-permute-start(f32[128,128]{1,0:T(8,128)S(1)} %add.31), channel_id=1, source_target_pairs={{0,16},{4,20},{8,24},{12,28},{16,0},{20,4},{24,8},{28,12},{1,17},{... | collective-permute-start | bytes 196616 | tf_op jit(solution)/shard_map/ppermute | solution.py:211
  34.2 4.3 %collective-permute-start.9 = (f32[128,128]{1,0:T(8,128)S(1)}, f32[128,128]{1,0:T(8,128)S(1)}, u32[]{:S(2)}, u32[]{:S(2)}) collective-permute-start(f32[128,128]{1,0:T(8,128)S(1)} %add.31), channel_id=1, source_target_pairs={{0,8},{4,12},{8,0},{12,4},{16,24},{20,28},{24,16},{28,20},{1,9},{5... | collective-permute-start | bytes 196616 | tf_op jit(solution)/shard_map/ppermute | solution.py:211
  38.5 1.3 %collective-permute-start.12 = (bf16[128,128]{1,0:T(8,128)(2,1)S(1)}, bf16[128,128]{1,0:T(8,128)(2,1)S(1)}, u32[]{:S(2)}, u32[]{:S(2)}) collective-permute-start(bf16[128,128]{1,0:T(8,128)(2,1)S(1)} %get-tuple-element.42.mine), channel_id=1, source_target_pairs={{0,4},{4,0},{8,12},{12,8},{16,20},{20,16},{24,28},{28,24},{1,5},{5... | collective-permute-start | bytes 98312 | tf_op jit(solution)/shard_map/ppermute | solution.py:211
  40.8 6.0 %collective-permute-start.15 = (f32[64,128]{1,0:T(8,128)S(1)}, f32[64,128]{1,0:T(8,128)S(1)}, u32[]{:S(2)}, u32[]{:S(2)}) collective-permute-start(f32[64,128]{1,0:T(8,128)S(1)} %last_backward.1.corr), channel_id=1, source_target_pairs={{0,3},{1,2},{2,1},{3,0},{4,7},{5,6},{6,5},{7,4},{8,11},{9,10},{10,... | collective-permute-start | bytes 98312 | tf_op jit(solution)/shard_map/ppermute | solution.py:211
  43.4 4.8 %collective-permute-start.14 = (f32[64,128]{1,0:T(8,128)S(1)}, f32[64,128]{1,0:T(8,128)S(1)}, u32[]{:S(2)}, u32[]{:S(2)}) collective-permute-start(f32[64,128]{1,0:T(8,128)S(1)} %last_backward.1.corr), channel_id=1, source_target_pairs={{0,2},{1,3},{2,0},{3,1},{4,6},{5,7},{6,4},{7,5},{8,10},{9,11},{10,... | collective-permute-start | bytes 98312 | tf_op jit(solution)/shard_map/ppermute | solution.py:211
  43.5 4.7 %collective-permute-start.13 = (f32[64,128]{1,0:T(8,128)S(1)}, f32[64,128]{1,0:T(8,128)S(1)}, u32[]{:S(2)}, u32[]{:S(2)}) collective-permute-start(f32[64,128]{1,0:T(8,128)S(1)} %last_backward.1.corr), channel_id=1, source_target_pairs={{0,1},{1,0},{2,3},{3,2},{4,5},{5,4},{6,7},{7,6},{8,9},{9,8},{10,11... | collective-permute-start | bytes 98312 | tf_op jit(solution)/shard_map/ppermute | solution.py:211

commit v8 on v7

--- a/solution.py
+++ b/solution.py
@@ -187,12 +187,10 @@
 
 
 def next_forward(ray_dev):
-    def kernel(proj, picks, places, volume, own, near, mid, far, sino, volume_out, weight_out, mine, theirs):
-        vox_dev = volume.shape[0]
-        sums = (own[...] + near[...]) + (mid[...] + far[...])
-        weights = 1.0 / jnp.maximum(sums[vox_dev:], 1.0)
+    def kernel(proj, picks, places, volume, col_total, own, near, mid, far, sino, volume_out, weight_out, mine, theirs):
+        weights = 1.0 / jnp.maximum(col_total[...], 1.0)
         weight_out[...] = weights
-        updated = volume[...] + weights * sums[:vox_dev]
+        updated = volume[...] + weights * ((own[...] + near[...]) + (mid[...] + far[...]))
         volume_out[...] = updated
         sums = forward_turned(proj, updated, picks[...], places[...])
         put_partial(sums, sino[...], mine, theirs, ray_dev)
@@ -200,10 +198,8 @@
     return kernel
 
 
-def first_backward(proj, picks, places, mine, theirs, col_total, corr):
-    vox_dev = col_total.shape[0]
-    corr[0:vox_dev, :] = backward(proj, join_halves(mine, theirs), picks[...], places[...])
-    corr[vox_dev:2 * vox_dev, :] = col_total[...]
+def first_backward(proj, picks, places, mine, theirs, corr):
+    corr[...] = backward(proj, join_halves(mine, theirs), picks[...], places[...])
 
 
 def swap(x, axis, bit):
@@ -292,24 +288,28 @@
     sums, _ = over_slabs(mine, theirs)
     row_weight = 1.0 / jnp.maximum(sums[half:], 1.0)
     weighted = (row_weight * sums[:half]).astype(BF16)
+    col_total = col_total + swap(col_total, "angle", 1)
 
     corr = pl.pallas_call(
         first_backward,
-        out_shape=vmem(2 * vox_dev),
-        in_specs=[whole()] * 6,
+        out_shape=vmem(vox_dev),
+        in_specs=[whole()] * 5,
         out_specs=whole(),
         compiler_params=params,
         name="first_backward",
-    )(proj, from_rays, to_vox, weighted, swap(weighted, "slab", 1), col_total)
+    )(proj, from_rays, to_vox, weighted, swap(weighted, "slab", 1))
+    angles = lax.axis_size("angle")
+    for b in range(1, angles.bit_length() - 1):
+        col_total = col_total + swap(col_total, "angle", 1 << b)
 
     volume, col_weight, mine, theirs = pl.pallas_call(
         next_forward(ray_dev),
         out_shape=(vmem(vox_dev), vmem(vox_dev), vmem(half), vmem(half)),
-        in_specs=[whole()] * 9,
+        in_specs=[whole()] * 10,
         out_specs=(whole(),) * 4,
         compiler_params=params,
         name="next_forward",
-    )(turned, from_vox, to_rays, volume, *over_angles(corr), sino)
+    )(turned, from_vox, to_rays, volume, col_total, *over_angles(corr), sino)
     residual, projector = over_slabs(mine, theirs, projector)
     count = blocks * 3 // 4
     fetched = [

time: 49 us -> 48.1 us (0.982)
  waiting for transfers between devices: 17 us -> 11.3 us
  starting transfers between devices: 17.7 us -> 22.4 us
    ppermute x16 -> x18, waiting for transfers between devices: 17 us -> 11.3 us  [swap(): return lax.ppermute(x, axis, [(i, i ^ bit) for i in range(size)])]
    ppermute x16 -> x18, starting transfers between devices: 17.7 us -> 22.4 us  [swap(): return lax.ppermute(x, axis, [(i, i ^ bit) for i in range(size)])]
  transfers between devices with their start and end apart: 16 -> 18, of which waited for: 12 -> 12; matrix products, arithmetic and copies ran while one was open for 1% -> 1% of each run, Pallas kernels for 10% -> 13%
where the time goes in v8:
time: 48.1 us; the launch traced here: 47.9 us
  starting transfers between devices  22.4 us (47%)
  Pallas kernels  12 us (25%)
  waiting for transfers between devices  11.3 us (23%)
  between operations  1.46 us (3%)
  local copies, waits for them, and re-layouts  0.61 us (1%)
    ppermute x18, starting transfers between devices, swap(): return lax.ppermute(x, axis, [(i, i ^ bit) for i in range(size)])  22.4 us
    ppermute x18, waiting for transfers between devices, swap(): return lax.ppermute(x, axis, [(i, i ^ bit) for i in range(size)])  11.3 us
    pallas_call x1, Pallas kernels, local(): pl.pallas_call(first_forward(slabs, capacity, ray_dev), out_shape=(pltpu....  3.4 us
    pallas_call x2, Pallas kernels, local(): pl.pallas_call(fetch_blocks(low), out_shape=pltpu.VMEM((size,) + projecto...  3.13 us
    pallas_call x1, Pallas kernels, local(): pl.pallas_call(turn_blocks, out_shape=pltpu.VMEM(projector.shape, BF16),...  1.13 us
    pallas_call x1, Pallas kernels, local(): pl.pallas_call(next_forward(ray_dev), out_shape=(vmem(vox_dev), vmem(vox_...  1 us
  transfers between devices with their start and end apart: 18, of which 12 were waited for; matrix products, arithmetic and copies ran while one was open for 1% of the time, Pallas kernels for 13%

profile of v8, /device:TPU:0, one launch (start us, length us, event | category | flops | bytes accessed | tf_op | source)
XLA Modules:
  0.0 47.9 jit_solution(14891826704248618943)
XLA Ops:
  1.3 3.4 %first_forward.1 = (bf16[128,128,128]{2,1,0:T(8,128)(2,1)S(1)}, s32[1,128]{1,0:T(1,128)S(1)}, s32[1,128]{1,0:T(1,128)S(1)}, f32[64,128]{1,0:T(8,128)S(1)}, f32[3...) custom-call(bf16[128,128,128]{2,1,0:T(8,128)(2,1)} %proj_hbm.3, s32[1,128]{1,0:T(1,128)} %bitcast.4, ...), custom_call_target="tpu_custom_call" | custom-call | tf_op jit(solution)/shard_map/first_forward/pallas_call | solution.py:249
  4.7 0.5 %collective-permute-start.2 = (f32[256,128]{1,0:T(8,128)S(1)}, f32[256,128]{1,0:T(8,128)S(1)}, u32[]{:S(2)}, u32[]{:S(2)}) collective-permute-start(f32[256,128]{1,0:T(8,128)S(1)} %get-tuple-element.32), channel_id=1, source_target_pairs={{0,4},{4,0},{8,12},{12,8},{16,20},{20,16},{24,28},{28,24},{1,5},{5... | collective-permute-start | bytes 393224 | tf_op jit(solution)/shard_map/ppermute | solution.py:207
  5.2 1.0 %collective-permute-done.2 = f32[256,128]{1,0:T(8,128)S(1)} collective-permute-done((f32[256,128]{1,0:T(8,128)S(1)}, f32[256,128]{1,0:T(8,128)S(1)}, u32[]{:S(2)}, u32[]{:S(2)}) %collective-permute-start.2) | collective-permute-done | bytes 131104 | tf_op jit(solution)/shard_map/ppermute | solution.py:207
  6.2 3.9 %collective-permute-start.5 = (f32[256,128]{1,0:T(8,128)S(1)}, f32[256,128]{1,0:T(8,128)S(1)}, u32[]{:S(2)}, u32[]{:S(2)}) collective-permute-start(f32[256,128]{1,0:T(8,128)S(1)} %add.35), channel_id=1, source_target_pairs={{0,24},{4,28},{8,16},{12,20},{16,8},{20,12},{24,0},{28,4},{1,25},{... | collective-permute-start | bytes 393224 | tf_op jit(solution)/shard_map/ppermute | solution.py:207
  10.1 0.5 %collective-permute-start.4 = (f32[256,128]{1,0:T(8,128)S(1)}, f32[256,128]{1,0:T(8,128)S(1)}, u32[]{:S(2)}, u32[]{:S(2)}) collective-permute-start(f32[256,128]{1,0:T(8,128)S(1)} %add.35), channel_id=1, source_target_pairs={{0,16},{4,20},{8,24},{12,28},{16,0},{20,4},{24,8},{28,12},{1,17},{... | collective-permute-start | bytes 393224 | tf_op jit(solution)/shard_map/ppermute | solution.py:207
  10.7 0.8 %name_places.1 = (bf16[128,256]{1,0:T(8,128)(2,1)S(1)}, bf16[256,128]{1,0:T(8,128)(2,1)S(1)}, bf16[128,64]{1,0:T(8,128)(2,1)S(1)}, bf16[64,128]{1,0:T(8,128)(2,1)S(1)}, f32[64,128]{1,0:T(8,128)S(1)}) custom-call(bf16[128,128,128]{2,1,0:T(8,128)(2,1)S(1)} %get-tuple-element.22.proj, s32[1,128]{1,0:T(1,128)S(1)} %get-tuple-element.23.rows, ...), custom_call_target="tpu_custom_call" | custom-call | bytes 1048576 | tf_op jit(solution)/shard_map/name_places/pallas_call | solution.py:267
  11.5 2.0 %collective-permute-start = (f32[64,128]{1,0:T(8,128)S(1)}, f32[64,128]{1,0:T(8,128)S(1)}, u32[]{:S(2)}, u32[]{:S(2)}) collective-permute-start(f32[64,128]{1,0:T(8,128)S(1)} %get-tuple-element.28), channel_id=1, source_target_pairs={{0,1},{1,0},{2,3},{3,2},{4,5},{5,4},{6,7},{7,6},{8,9},{9,8},{10,11... | collective-permute-start | bytes 98312 | tf_op jit(solution)/shard_map/ppermute | solution.py:207
  14.0 2.7 %collective-permute-done.4 = f32[256,128]{1,0:T(8,128)S(1)} collective-permute-done((f32[256,128]{1,0:T(8,128)S(1)}, f32[256,128]{1,0:T(8,128)S(1)}, u32[]{:S(2)}, u32[]{:S(2)}) %collective-permute-start.4) | collective-permute-done | bytes 131104 | tf_op jit(solution)/shard_map/ppermute | solution.py:207
  17.1 2.7 %collective-permute-start.1 = (f32[64,128]{1,0:T(8,128)S(1)}, f32[64,128]{1,0:T(8,128)S(1)}, u32[]{:S(2)}, u32[]{:S(2)}) collective-permute-start(f32[64,128]{1,0:T(8,128)S(1)} %add.33), channel_id=1, source_target_pairs={{0,2},{1,3},{2,0},{3,1},{4,6},{5,7},{6,4},{7,5},{8,10},{9,11},{10,... | collective-permute-start | bytes 98312 | tf_op jit(solution)/shard_map/ppermute | solution.py:207
  19.8 0.9 %first_backward.1.own = f32[64,128]{1,0:T(8,128)S(1)} custom-call(bf16[128,128,128]{2,1,0:T(8,128)(2,1)S(1)} %get-tuple-element.22.proj, bf16[128,256]{1,0:T(8,128)(2,1)S(1)} %get-tuple-element.29.picks, bf16[64,128]{1,0:T(8,128)(2,1)S(1)} %get-tuple-element.30.places, bf16[128,128]{1,0:T(8,128)(2,1)S(1)} %fusion.mine, ...), custom_call_target="tpu_custom_call" | custom-call | tf_op jit(solution)/shard_map/first_backward/pallas_call | solution.py:293
  20.8 2.2 %collective-permute-start.9 = (f32[64,128]{1,0:T(8,128)S(1)}, f32[64,128]{1,0:T(8,128)S(1)}, u32[]{:S(2)}, u32[]{:S(2)}) collective-permute-start(f32[64,128]{1,0:T(8,128)S(1)} %first_backward.1.own), channel_id=1, source_target_pairs={{0,3},{1,2},{2,1},{3,0},{4,7},{5,6},{6,5},{7,4},{8,11},{9,10},{10,... | collective-permute-start | bytes 98312 | tf_op jit(solution)/shard_map/ppermute | solution.py:207
  22.9 0.9 %collective-permute-start.8 = (f32[64,128]{1,0:T(8,128)S(1)}, f32[64,128]{1,0:T(8,128)S(1)}, u32[]{:S(2)}, u32[]{:S(2)}) collective-permute-start(f32[64,128]{1,0:T(8,128)S(1)} %first_backward.1.own), channel_id=1, source_target_pairs={{0,2},{1,3},{2,0},{3,1},{4,6},{5,7},{6,4},{7,5},{8,10},{9,11},{10,... | collective-permute-start | bytes 98312 | tf_op jit(solution)/shard_map/ppermute | solution.py:207
  23.9 1.3 %collective-permute-start.7 = (f32[64,128]{1,0:T(8,128)S(1)}, f32[64,128]{1,0:T(8,128)S(1)}, u32[]{:S(2)}, u32[]{:S(2)}) collective-permute-start(f32[64,128]{1,0:T(8,128)S(1)} %first_backward.1.own), channel_id=1, source_target_pairs={{0,1},{1,0},{2,3},{3,2},{4,5},{5,4},{6,7},{7,6},{8,9},{9,8},{10,11... | collective-permute-start | bytes 98312 | tf_op jit(solution)/shard_map/ppermute | solution.py:207
  25.2 1.1 %turn_blocks.1.proj = bf16[128,128,128]{2,1,0:T(8,128)(2,1)S(1)} custom-call(bf16[128,128,128]{2,1,0:T(8,128)(2,1)S(1)} %get-tuple-element.22.proj), custom_call_target="tpu_custom_call" | custom-call | bytes 8388608 | tf_op jit(solution)/shard_map/turn_blocks/pallas_call | solution.py:279
  26.7 1.2 %collective-permute-done.8.mid = f32[64,128]{1,0:T(8,128)S(1)} collective-permute-done((f32[64,128]{1,0:T(8,128)S(1)}, f32[64,128]{1,0:T(8,128)S(1)}, u32[]{:S(2)}, u32[]{:S(2)}) %collective-permute-start.8) | collective-permute-done | bytes 32800 | tf_op jit(solution)/shard_map/ppermute | solution.py:207
  28.2 1.0 %next_forward.1 = (f32[64,128]{1,0:T(8,128)S(1)}, f32[64,128]{1,0:T(8,128)S(1)}, f32[128,128]{1,0:T(8,128)S(1)}, f32[128,128]{1,0:T(8,128)S(1)}) custom-call(bf16[128,128,128]{2,1,0:T(8,128)(2,1)S(1)} %turn_blocks.1.proj, bf16[128,64]{1,0:T(8,128)(2,1)S(1)} %get-tuple-element.25.picks, bf16[256,128]{1,0:T(8,128)(2,1)S(1)} %get-tuple-element.26.places, ...), custom_call_target="tpu_custom_call" | custom-call | tf_op jit(solution)/shard_map/next_forward/pallas_call | solution.py:305
  29.3 1.2 %collective-permute-done.10 = f32[128,128]{1,0:T(8,128)S(1)} collective-permute-done((f32[128,128]{1,0:T(8,128)S(1)}, f32[128,128]{1,0:T(8,128)S(1)}, u32[]{:S(2)}, u32[]{:S(2)}) %collective-permute-start.10) | collective-permute-done | bytes 65568 | tf_op jit(solution)/shard_map/ppermute | solution.py:207
  30.5 1.7 %collective-permute-start.13 = (f32[128,128]{1,0:T(8,128)S(1)}, f32[128,128]{1,0:T(8,128)S(1)}, u32[]{:S(2)}, u32[]{:S(2)}) collective-permute-start(f32[128,128]{1,0:T(8,128)S(1)} %add.39), channel_id=1, source_target_pairs={{0,24},{4,28},{8,16},{12,20},{16,8},{20,12},{24,0},{28,4},{1,25},{... | collective-permute-start | bytes 196616 | tf_op jit(solution)/shard_map/ppermute | solution.py:207
  32.3 1.3 %collective-permute-start.12 = (f32[128,128]{1,0:T(8,128)S(1)}, f32[128,128]{1,0:T(8,128)S(1)}, u32[]{:S(2)}, u32[]{:S(2)}) collective-permute-start(f32[128,128]{1,0:T(8,128)S(1)} %add.39), channel_id=1, source_target_pairs={{0,16},{4,20},{8,24},{12,28},{16,0},{20,4},{24,8},{28,12},{1,17},{... | collective-permute-start | bytes 196616 | tf_op jit(solution)/shard_map/ppermute | solution.py:207
  33.6 0.5 %collective-permute-start.11 = (f32[128,128]{1,0:T(8,128)S(1)}, f32[128,128]{1,0:T(8,128)S(1)}, u32[]{:S(2)}, u32[]{:S(2)}) collective-permute-start(f32[128,128]{1,0:T(8,128)S(1)} %add.39), channel_id=1, source_target_pairs={{0,8},{4,12},{8,0},{12,4},{16,24},{20,28},{24,16},{28,20},{1,9},{5... | collective-permute-start | bytes 196616 | tf_op jit(solution)/shard_map/ppermute | solution.py:207
  34.1 1.9 %fetch_blocks.2.early = bf16[96,128,128]{2,1,0:T(8,128)(2,1)S(1)} custom-call(bf16[128,128,128]{2,1,0:T(8,128)(2,1)} %proj_hbm.3), custom_call_target="tpu_custom_call" | custom-call | bytes 6291456 | tf_op jit(solution)/shard_map/fetch_blocks/pallas_call | solution.py:316
  36.0 1.1 %collective-permute-done.12 = f32[128,128]{1,0:T(8,128)S(1)} collective-permute-done((f32[128,128]{1,0:T(8,128)S(1)}, f32[128,128]{1,0:T(8,128)S(1)}, u32[]{:S(2)}, u32[]{:S(2)}) %collective-permute-start.12) | collective-permute-done | bytes 65568 | tf_op jit(solution)/shard_map/ppermute | solution.py:207
  37.1 0.8 %collective-permute-done.11 = f32[128,128]{1,0:T(8,128)S(1)} collective-permute-done((f32[128,128]{1,0:T(8,128)S(1)}, f32[128,128]{1,0:T(8,128)S(1)}, u32[]{:S(2)}, u32[]{:S(2)}) %collective-permute-start.11) | collective-permute-done | bytes 65568 | tf_op jit(solution)/shard_map/ppermute | solution.py:207
  38.0 1.2 %fetch_blocks.3.late = bf16[32,128,128]{2,1,0:T(8,128)(2,1)S(1)} custom-call(bf16[128,128,128]{2,1,0:T(8,128)(2,1)} %proj_hbm.3), custom_call_target="tpu_custom_call" | custom-call | bytes 2097152 | tf_op jit(solution)/shard_map/fetch_blocks/pallas_call | solution.py:316
  39.2 0.9 %last_backward.1.corr = f32[64,128]{1,0:T(8,128)S(1)} custom-call(bf16[96,128,128]{2,1,0:T(8,128)(2,1)S(1)} %fetch_blocks.2.early, bf16[32,128,128]{2,1,0:T(8,128)(2,1)S(1)} %fetch_blocks.3.late, bf16[128,256]{1,0:T(8,128)(2,1)S(1)} %get-tuple-element.29.picks, bf16[64,128]{1,0:T(8,128)(2,1)S(1)} %get-tuple-element.30.places, ...), custom_call_target="tpu_custom_call" | custom-call | tf_op jit(solution)/shard_map/last_backward/pallas_call | solution.py:335
  40.2 1.7 %collective-permute-start.17 = (f32[64,128]{1,0:T(8,128)S(1)}, f32[64,128]{1,0:T(8,128)S(1)}, u32[]{:S(2)}, u32[]{:S(2)}) collective-permute-start(f32[64,128]{1,0:T(8,128)S(1)} %last_backward.1.corr), channel_id=1, source_target_pairs={{0,3},{1,2},{2,1},{3,0},{4,7},{5,6},{6,5},{7,4},{8,11},{9,10},{10,... | collective-permute-start | bytes 98312 | tf_op jit(solution)/shard_map/ppermute | solution.py:207
  41.9 0.8 %collective-permute-start.16 = (f32[64,128]{1,0:T(8,128)S(1)}, f32[64,128]{1,0:T(8,128)S(1)}, u32[]{:S(2)}, u32[]{:S(2)}) collective-permute-start(f32[64,128]{1,0:T(8,128)S(1)} %last_backward.1.corr), channel_id=1, source_target_pairs={{0,2},{1,3},{2,0},{3,1},{4,6},{5,7},{6,4},{7,5},{8,10},{9,11},{10,... | collective-permute-start | bytes 98312 | tf_op jit(solution)/shard_map/ppermute | solution.py:207
  42.6 2.0 %collective-permute-start.15 = (f32[64,128]{1,0:T(8,128)S(1)}, f32[64,128]{1,0:T(8,128)S(1)}, u32[]{:S(2)}, u32[]{:S(2)}) collective-permute-start(f32[64,128]{1,0:T(8,128)S(1)} %last_backward.1.corr), channel_id=1, source_target_pairs={{0,1},{1,0},{2,3},{3,2},{4,5},{5,4},{6,7},{7,6},{8,9},{9,8},{10,11... | collective-permute-start | bytes 98312 | tf_op jit(solution)/shard_map/ppermute | solution.py:207
  44.6 0.6 %constant_dynamic-slice_fusion = f32[32,128]{1,0:T(8,128)} fusion(f32[128,128]{1,0:T(8,128)S(1)} %get-tuple-element.43, s32[]{:T(128)S(6)} %select_n.3), kind=kLoop, calls=%fused_computation.7 | loop fusion | bytes 32772 | tf_op jit(solution)/shard_map/dynamic_slice | solution.py:333
  45.3 1.0 %collective-permute-done.17.far = f32[64,128]{1,0:T(8,128)S(1)} collective-permute-done((f32[64,128]{1,0:T(8,128)S(1)}, f32[64,128]{1,0:T(8,128)S(1)}, u32[]{:S(2)}, u32[]{:S(2)}) %collective-permute-start.17) | collective-permute-done | bytes 32800 | tf_op jit(solution)/shard_map/ppermute | solution.py:207
  46.3 1.0 %collective-permute-done.16.mid = f32[64,128]{1,0:T(8,128)S(1)} collective-permute-done((f32[64,128]{1,0:T(8,128)S(1)}, f32[64,128]{1,0:T(8,128)S(1)}, u32[]{:S(2)}, u32[]{:S(2)}) %collective-permute-start.16) | collective-permute-done | bytes 32800 | tf_op jit(solution)/shard_map/ppermute | solution.py:207
  47.3 0.6 %last_update.1 = f32[64,128]{1,0:T(8,128)} custom-call(f32[64,128]{1,0:T(8,128)S(1)} %get-tuple-element.34.volume, f32[64,128]{1,0:T(8,128)S(1)} %get-tuple-element.35.weight, f32[64,128]{1,0:T(8,128)S(1)} %last_backward.1.corr, f32[64,128]{1,0:T(8,128)S(1)} %collective-permute-done.15.near, f32[64,128]{1,0:T(8,128)S(1)} %collective-permute-done.16.mid, ...), custom_call_target="tpu_custom_call" | custom-call | tf_op jit(solution)/shard_map/last_update/pallas_call | solution.py:343
  (22 shorter events, 1.8 us)
Async XLA Ops:
  4.7 1.5 %collective-permute-start.2 = (f32[256,128]{1,0:T(8,128)S(1)}, f32[256,128]{1,0:T(8,128)S(1)}, u32[]{:S(2)}, u32[]{:S(2)}) collective-permute-start(f32[256,128]{1,0:T(8,128)S(1)} %get-tuple-element.32), channel_id=1, source_target_pairs={{0,4},{4,0},{8,12},{12,8},{16,20},{20,16},{24,28},{28,24},{1,5},{5... | collective-permute-start | bytes 393224 | tf_op jit(solution)/shard_map/ppermute | solution.py:207
  6.2 7.8 %collective-permute-start.5 = (f32[256,128]{1,0:T(8,128)S(1)}, f32[256,128]{1,0:T(8,128)S(1)}, u32[]{:S(2)}, u32[]{:S(2)}) collective-permute-start(f32[256,128]{1,0:T(8,128)S(1)} %add.35), channel_id=1, source_target_pairs={{0,24},{4,28},{8,16},{12,20},{16,8},{20,12},{24,0},{28,4},{1,25},{... | collective-permute-start | bytes 393224 | tf_op jit(solution)/shard_map/ppermute | solution.py:207
  10.1 6.6 %collective-permute-start.4 = (f32[256,128]{1,0:T(8,128)S(1)}, f32[256,128]{1,0:T(8,128)S(1)}, u32[]{:S(2)}, u32[]{:S(2)}) collective-permute-start(f32[256,128]{1,0:T(8,128)S(1)} %add.35), channel_id=1, source_target_pairs={{0,16},{4,20},{8,24},{12,28},{16,0},{20,4},{24,8},{28,12},{1,17},{... | collective-permute-start | bytes 393224 | tf_op jit(solution)/shard_map/ppermute | solution.py:207
  10.6 6.4 %collective-permute-start.3 = (f32[256,128]{1,0:T(8,128)S(1)}, f32[256,128]{1,0:T(8,128)S(1)}, u32[]{:S(2)}, u32[]{:S(2)}) collective-permute-start(f32[256,128]{1,0:T(8,128)S(1)} %add.35), channel_id=1, source_target_pairs={{0,8},{4,12},{8,0},{12,4},{16,24},{20,28},{24,16},{28,20},{1,9},{5... | collective-permute-start | bytes 393224 | tf_op jit(solution)/shard_map/ppermute | solution.py:207
  11.5 5.6 %collective-permute-start = (f32[64,128]{1,0:T(8,128)S(1)}, f32[64,128]{1,0:T(8,128)S(1)}, u32[]{:S(2)}, u32[]{:S(2)}) collective-permute-start(f32[64,128]{1,0:T(8,128)S(1)} %get-tuple-element.28), channel_id=1, source_target_pairs={{0,1},{1,0},{2,3},{3,2},{4,5},{5,4},{6,7},{7,6},{8,9},{9,8},{10,11... | collective-permute-start | bytes 98312 | tf_op jit(solution)/shard_map/ppermute | solution.py:207
  17.0 2.8 %collective-permute-start.6 = (bf16[128,128]{1,0:T(8,128)(2,1)S(1)}, bf16[128,128]{1,0:T(8,128)(2,1)S(1)}, u32[]{:S(2)}, u32[]{:S(2)}) collective-permute-start(bf16[128,128]{1,0:T(8,128)(2,1)S(1)} %fusion.mine), channel_id=1, source_target_pairs={{0,4},{4,0},{8,12},{12,8},{16,20},{20,16},{24,28},{28,24},{1,5},{5... | collective-permute-start | bytes 98312 | tf_op jit(solution)/shard_map/ppermute | solution.py:207
  17.1 9.2 %collective-permute-start.1 = (f32[64,128]{1,0:T(8,128)S(1)}, f32[64,128]{1,0:T(8,128)S(1)}, u32[]{:S(2)}, u32[]{:S(2)}) collective-permute-start(f32[64,128]{1,0:T(8,128)S(1)} %add.33), channel_id=1, source_target_pairs={{0,2},{1,3},{2,0},{3,1},{4,6},{5,7},{6,4},{7,5},{8,10},{9,11},{10,... | collective-permute-start | bytes 98312 | tf_op jit(solution)/shard_map/ppermute | solution.py:207
  20.8 5.9 %collective-permute-start.9 = (f32[64,128]{1,0:T(8,128)S(1)}, f32[64,128]{1,0:T(8,128)S(1)}, u32[]{:S(2)}, u32[]{:S(2)}) collective-permute-start(f32[64,128]{1,0:T(8,128)S(1)} %first_backward.1.own), channel_id=1, source_target_pairs={{0,3},{1,2},{2,1},{3,0},{4,7},{5,6},{6,5},{7,4},{8,11},{9,10},{10,... | collective-permute-start | bytes 98312 | tf_op jit(solution)/shard_map/ppermute | solution.py:207
  22.9 5.0 %collective-permute-start.8 = (f32[64,128]{1,0:T(8,128)S(1)}, f32[64,128]{1,0:T(8,128)S(1)}, u32[]{:S(2)}, u32[]{:S(2)}) collective-permute-start(f32[64,128]{1,0:T(8,128)S(1)} %first_backward.1.own), channel_id=1, source_target_pairs={{0,2},{1,3},{2,0},{3,1},{4,6},{5,7},{6,4},{7,5},{8,10},{9,11},{10,... | collective-permute-start | bytes 98312 | tf_op jit(solution)/shard_map/ppermute | solution.py:207
  23.9 4.3 %collective-permute-start.7 = (f32[64,128]{1,0:T(8,128)S(1)}, f32[64,128]{1,0:T(8,128)S(1)}, u32[]{:S(2)}, u32[]{:S(2)}) collective-permute-start(f32[64,128]{1,0:T(8,128)S(1)} %first_backward.1.own), channel_id=1, source_target_pairs={{0,1},{1,0},{2,3},{3,2},{4,5},{5,4},{6,7},{7,6},{8,9},{9,8},{10,11... | collective-permute-start | bytes 98312 | tf_op jit(solution)/shard_map/ppermute | solution.py:207
  29.2 1.3 %collective-permute-start.10 = (f32[128,128]{1,0:T(8,128)S(1)}, f32[128,128]{1,0:T(8,128)S(1)}, u32[]{:S(2)}, u32[]{:S(2)}) collective-permute-start(f32[128,128]{1,0:T(8,128)S(1)} %get-tuple-element.37), channel_id=1, source_target_pairs={{0,4},{4,0},{8,12},{12,8},{16,20},{20,16},{24,28},{28,24},{1,5},{5... | collective-permute-start | bytes 196616 | tf_op jit(solution)/shard_map/ppermute | solution.py:207
  30.5 5.5 %collective-permute-start.13 = (f32[128,128]{1,0:T(8,128)S(1)}, f32[128,128]{1,0:T(8,128)S(1)}, u32[]{:S(2)}, u32[]{:S(2)}) collective-permute-start(f32[128,128]{1,0:T(8,128)S(1)} %add.39), channel_id=1, source_target_pairs={{0,24},{4,28},{8,16},{12,20},{16,8},{20,12},{24,0},{28,4},{1,25},{... | collective-permute-start | bytes 196616 | tf_op jit(solution)/shard_map/ppermute | solution.py:207
  32.3 4.8 %collective-permute-start.12 = (f32[128,128]{1,0:T(8,128)S(1)}, f32[128,128]{1,0:T(8,128)S(1)}, u32[]{:S(2)}, u32[]{:S(2)}) collective-permute-start(f32[128,128]{1,0:T(8,128)S(1)} %add.39), channel_id=1, source_target_pairs={{0,16},{4,20},{8,24},{12,28},{16,0},{20,4},{24,8},{28,12},{1,17},{... | collective-permute-start | bytes 196616 | tf_op jit(solution)/shard_map/ppermute | solution.py:207
  33.6 4.3 %collective-permute-start.11 = (f32[128,128]{1,0:T(8,128)S(1)}, f32[128,128]{1,0:T(8,128)S(1)}, u32[]{:S(2)}, u32[]{:S(2)}) collective-permute-start(f32[128,128]{1,0:T(8,128)S(1)} %add.39), channel_id=1, source_target_pairs={{0,8},{4,12},{8,0},{12,4},{16,24},{20,28},{24,16},{28,20},{1,9},{5... | collective-permute-start | bytes 196616 | tf_op jit(solution)/shard_map/ppermute | solution.py:207
  37.9 1.3 %collective-permute-start.14 = (bf16[128,128]{1,0:T(8,128)(2,1)S(1)}, bf16[128,128]{1,0:T(8,128)(2,1)S(1)}, u32[]{:S(2)}, u32[]{:S(2)}) collective-permute-start(bf16[128,128]{1,0:T(8,128)(2,1)S(1)} %get-tuple-element.42.mine), channel_id=1, source_target_pairs={{0,4},{4,0},{8,12},{12,8},{16,20},{20,16},{24,28},{28,24},{1,5},{5... | collective-permute-start | bytes 98312 | tf_op jit(solution)/shard_map/ppermute | solution.py:207
  40.2 6.1 %collective-permute-start.17 = (f32[64,128]{1,0:T(8,128)S(1)}, f32[64,128]{1,0:T(8,128)S(1)}, u32[]{:S(2)}, u32[]{:S(2)}) collective-permute-start(f32[64,128]{1,0:T(8,128)S(1)} %last_backward.1.corr), channel_id=1, source_target_pairs={{0,3},{1,2},{2,1},{3,0},{4,7},{5,6},{6,5},{7,4},{8,11},{9,10},{10,... | collective-permute-start | bytes 98312 | tf_op jit(solution)/shard_map/ppermute | solution.py:207
  41.9 5.4 %collective-permute-start.16 = (f32[64,128]{1,0:T(8,128)S(1)}, f32[64,128]{1,0:T(8,128)S(1)}, u32[]{:S(2)}, u32[]{:S(2)}) collective-permute-start(f32[64,128]{1,0:T(8,128)S(1)} %last_backward.1.corr), channel_id=1, source_target_pairs={{0,2},{1,3},{2,0},{3,1},{4,6},{5,7},{6,4},{7,5},{8,10},{9,11},{10,... | collective-permute-start | bytes 98312 | tf_op jit(solution)/shard_map/ppermute | solution.py:207
  42.6 4.6 %collective-permute-start.15 = (f32[64,128]{1,0:T(8,128)S(1)}, f32[64,128]{1,0:T(8,128)S(1)}, u32[]{:S(2)}, u32[]{:S(2)}) collective-permute-start(f32[64,128]{1,0:T(8,128)S(1)} %last_backward.1.corr), channel_id=1, source_target_pairs={{0,1},{1,0},{2,3},{3,2},{4,5},{5,4},{6,7},{7,6},{8,9},{9,8},{10,11... | collective-permute-start | bytes 98312 | tf_op jit(solution)/shard_map/ppermute | solution.py:207

commit v9 on v8

--- a/solution.py
+++ b/solution.py
@@ -288,7 +288,9 @@
     sums, _ = over_slabs(mine, theirs)
     row_weight = 1.0 / jnp.maximum(sums[half:], 1.0)
     weighted = (row_weight * sums[:half]).astype(BF16)
-    col_total = col_total + swap(col_total, "angle", 1)
+    angles = lax.axis_size("angle")
+    for b in reversed(range(1, angles.bit_length() - 1)):
+        col_total = col_total + swap(col_total, "angle", 1 << b)
 
     corr = pl.pallas_call(
         first_backward,
@@ -298,9 +300,7 @@
         compiler_params=params,
         name="first_backward",
     )(proj, from_rays, to_vox, weighted, swap(weighted, "slab", 1))
-    angles = lax.axis_size("angle")
-    for b in range(1, angles.bit_length() - 1):
-        col_total = col_total + swap(col_total, "angle", 1 << b)
+    col_total = col_total + swap(col_total, "angle", 1)
 
     volume, col_weight, mine, theirs = pl.pallas_call(
         next_forward(ray_dev),

time: 48.1 us -> 47.6 us (0.990)
  waiting for transfers between devices: 11.3 us -> 10.8 us
    ppermute x18, waiting for transfers between devices: 11.3 us -> 10.8 us  [swap(): return lax.ppermute(x, axis, [(i, i ^ bit) for i in range(size)])]
  transfers between devices with their start and end apart: 18 -> 18, of which waited for: 12 -> 11; matrix products, arithmetic and copies ran while one was open for 1% -> 1% of each run, Pallas kernels for 13% -> 13%
where the time goes in v9:
time: 47.6 us; the launch traced here: 47.4 us
  starting transfers between devices  22.4 us (47%)
  Pallas kernels  12 us (25%)
  waiting for transfers between devices  10.8 us (23%)
  between operations  1.46 us (3%)
  local copies, waits for them, and re-layouts  0.61 us (1%)
    ppermute x18, starting transfers between devices, swap(): return lax.ppermute(x, axis, [(i, i ^ bit) for i in range(size)])  22.4 us
    ppermute x18, waiting for transfers between devices, swap(): return lax.ppermute(x, axis, [(i, i ^ bit) for i in range(size)])  10.8 us
    pallas_call x1, Pallas kernels, local(): pl.pallas_call(first_forward(slabs, capacity, ray_dev), out_shape=(pltpu....  3.4 us
    pallas_call x2, Pallas kernels, local(): pl.pallas_call(fetch_blocks(low), out_shape=pltpu.VMEM((size,) + projecto...  3.13 us
    pallas_call x1, Pallas kernels, local(): pl.pallas_call(turn_blocks, out_shape=pltpu.VMEM(projector.shape, BF16),...  1.13 us
    pallas_call x1, Pallas kernels, local(): pl.pallas_call(next_forward(ray_dev), out_shape=(vmem(vox_dev), vmem(vox_...  1 us
  transfers between devices with their start and end apart: 18, of which 11 were waited for; matrix products, arithmetic and copies ran while one was open for 1% of the time, Pallas kernels for 13%

profile of v9, /device:TPU:0, one launch (start us, length us, event | category | flops | bytes accessed | tf_op | source)
XLA Modules:
  0.0 47.4 jit_solution(11988622148080609919)
XLA Ops:
  1.3 3.4 %first_forward.1 = (bf16[128,128,128]{2,1,0:T(8,128)(2,1)S(1)}, s32[1,128]{1,0:T(1,128)S(1)}, s32[1,128]{1,0:T(1,128)S(1)}, f32[64,128]{1,0:T(8,128)S(1)}, f32[3...) custom-call(bf16[128,128,128]{2,1,0:T(8,128)(2,1)} %proj_hbm.3, s32[1,128]{1,0:T(1,128)} %bitcast.4, ...), custom_call_target="tpu_custom_call" | custom-call | tf_op jit(solution)/shard_map/first_forward/pallas_call | solution.py:249
  4.7 0.5 %collective-permute-start.2 = (f32[256,128]{1,0:T(8,128)S(1)}, f32[256,128]{1,0:T(8,128)S(1)}, u32[]{:S(2)}, u32[]{:S(2)}) collective-permute-start(f32[256,128]{1,0:T(8,128)S(1)} %get-tuple-element.32), channel_id=1, source_target_pairs={{0,4},{4,0},{8,12},{12,8},{16,20},{20,16},{24,28},{28,24},{1,5},{5... | collective-permute-start | bytes 393224 | tf_op jit(solution)/shard_map/ppermute | solution.py:207
  5.2 1.0 %collective-permute-done.2 = f32[256,128]{1,0:T(8,128)S(1)} collective-permute-done((f32[256,128]{1,0:T(8,128)S(1)}, f32[256,128]{1,0:T(8,128)S(1)}, u32[]{:S(2)}, u32[]{:S(2)}) %collective-permute-start.2) | collective-permute-done | bytes 131104 | tf_op jit(solution)/shard_map/ppermute | solution.py:207
  6.2 3.9 %collective-permute-start.5 = (f32[256,128]{1,0:T(8,128)S(1)}, f32[256,128]{1,0:T(8,128)S(1)}, u32[]{:S(2)}, u32[]{:S(2)}) collective-permute-start(f32[256,128]{1,0:T(8,128)S(1)} %add.35), channel_id=1, source_target_pairs={{0,24},{4,28},{8,16},{12,20},{16,8},{20,12},{24,0},{28,4},{1,25},{... | collective-permute-start | bytes 393224 | tf_op jit(solution)/shard_map/ppermute | solution.py:207
  10.1 0.5 %collective-permute-start.4 = (f32[256,128]{1,0:T(8,128)S(1)}, f32[256,128]{1,0:T(8,128)S(1)}, u32[]{:S(2)}, u32[]{:S(2)}) collective-permute-start(f32[256,128]{1,0:T(8,128)S(1)} %add.35), channel_id=1, source_target_pairs={{0,16},{4,20},{8,24},{12,28},{16,0},{20,4},{24,8},{28,12},{1,17},{... | collective-permute-start | bytes 393224 | tf_op jit(solution)/shard_map/ppermute | solution.py:207
  10.7 0.8 %name_places.1 = (bf16[128,256]{1,0:T(8,128)(2,1)S(1)}, bf16[256,128]{1,0:T(8,128)(2,1)S(1)}, bf16[128,64]{1,0:T(8,128)(2,1)S(1)}, bf16[64,128]{1,0:T(8,128)(2,1)S(1)}, f32[64,128]{1,0:T(8,128)S(1)}) custom-call(bf16[128,128,128]{2,1,0:T(8,128)(2,1)S(1)} %get-tuple-element.22.proj, s32[1,128]{1,0:T(1,128)S(1)} %get-tuple-element.23.rows, ...), custom_call_target="tpu_custom_call" | custom-call | bytes 1048576 | tf_op jit(solution)/shard_map/name_places/pallas_call | solution.py:267
  11.5 3.1 %collective-permute-start = (f32[64,128]{1,0:T(8,128)S(1)}, f32[64,128]{1,0:T(8,128)S(1)}, u32[]{:S(2)}, u32[]{:S(2)}) collective-permute-start(f32[64,128]{1,0:T(8,128)S(1)} %get-tuple-element.28), channel_id=1, source_target_pairs={{0,2},{1,3},{2,0},{3,1},{4,6},{5,7},{6,4},{7,5},{8,10},{9,11},{10,... | collective-permute-start | bytes 98312 | tf_op jit(solution)/shard_map/ppermute | solution.py:207
  14.6 2.1 %collective-permute-done.4 = f32[256,128]{1,0:T(8,128)S(1)} collective-permute-done((f32[256,128]{1,0:T(8,128)S(1)}, f32[256,128]{1,0:T(8,128)S(1)}, u32[]{:S(2)}, u32[]{:S(2)}) %collective-permute-start.4) | collective-permute-done | bytes 131104 | tf_op jit(solution)/shard_map/ppermute | solution.py:207
  16.7 0.3 collective-permute-done.3
  17.1 1.6 %collective-permute-start.1 = (f32[64,128]{1,0:T(8,128)S(1)}, f32[64,128]{1,0:T(8,128)S(1)}, u32[]{:S(2)}, u32[]{:S(2)}) collective-permute-start(f32[64,128]{1,0:T(8,128)S(1)} %add.33), channel_id=1, source_target_pairs={{0,1},{1,0},{2,3},{3,2},{4,5},{5,4},{6,7},{7,6},{8,9},{9,8},{10,11... | collective-permute-start | bytes 98312 | tf_op jit(solution)/shard_map/ppermute | solution.py:207
  18.8 0.9 %first_backward.1.own = f32[64,128]{1,0:T(8,128)S(1)} custom-call(bf16[128,128,128]{2,1,0:T(8,128)(2,1)S(1)} %get-tuple-element.22.proj, bf16[128,256]{1,0:T(8,128)(2,1)S(1)} %get-tuple-element.29.picks, bf16[64,128]{1,0:T(8,128)(2,1)S(1)} %get-tuple-element.30.places, bf16[128,128]{1,0:T(8,128)(2,1)S(1)} %fusion.mine, ...), custom_call_target="tpu_custom_call" | custom-call | tf_op jit(solution)/shard_map/first_backward/pallas_call | solution.py:295
  19.7 3.2 %collective-permute-start.9 = (f32[64,128]{1,0:T(8,128)S(1)}, f32[64,128]{1,0:T(8,128)S(1)}, u32[]{:S(2)}, u32[]{:S(2)}) collective-permute-start(f32[64,128]{1,0:T(8,128)S(1)} %first_backward.1.own), channel_id=1, source_target_pairs={{0,3},{1,2},{2,1},{3,0},{4,7},{5,6},{6,5},{7,4},{8,11},{9,10},{10,... | collective-permute-start | bytes 98312 | tf_op jit(solution)/shard_map/ppermute | solution.py:207
  22.9 1.3 %collective-permute-start.7 = (f32[64,128]{1,0:T(8,128)S(1)}, f32[64,128]{1,0:T(8,128)S(1)}, u32[]{:S(2)}, u32[]{:S(2)}) collective-permute-start(f32[64,128]{1,0:T(8,128)S(1)} %first_backward.1.own), channel_id=1, source_target_pairs={{0,1},{1,0},{2,3},{3,2},{4,5},{5,4},{6,7},{7,6},{8,9},{9,8},{10,11... | collective-permute-start | bytes 98312 | tf_op jit(solution)/shard_map/ppermute | solution.py:207
  24.2 1.1 %turn_blocks.1.proj = bf16[128,128,128]{2,1,0:T(8,128)(2,1)S(1)} custom-call(bf16[128,128,128]{2,1,0:T(8,128)(2,1)S(1)} %get-tuple-element.22.proj), custom_call_target="tpu_custom_call" | custom-call | bytes 8388608 | tf_op jit(solution)/shard_map/turn_blocks/pallas_call | solution.py:279
  25.5 2.2 %collective-permute-done.8.mid = f32[64,128]{1,0:T(8,128)S(1)} collective-permute-done((f32[64,128]{1,0:T(8,128)S(1)}, f32[64,128]{1,0:T(8,128)S(1)}, u32[]{:S(2)}, u32[]{:S(2)}) %collective-permute-start.8) | collective-permute-done | bytes 32800 | tf_op jit(solution)/shard_map/ppermute | solution.py:207
  27.7 1.0 %next_forward.1 = (f32[64,128]{1,0:T(8,128)S(1)}, f32[64,128]{1,0:T(8,128)S(1)}, f32[128,128]{1,0:T(8,128)S(1)}, f32[128,128]{1,0:T(8,128)S(1)}) custom-call(bf16[128,128,128]{2,1,0:T(8,128)(2,1)S(1)} %turn_blocks.1.proj, bf16[128,64]{1,0:T(8,128)(2,1)S(1)} %get-tuple-element.25.picks, bf16[256,128]{1,0:T(8,128)(2,1)S(1)} %get-tuple-element.26.places, ...), custom_call_target="tpu_custom_call" | custom-call | tf_op jit(solution)/shard_map/next_forward/pallas_call | solution.py:305
  28.8 1.2 %collective-permute-done.10 = f32[128,128]{1,0:T(8,128)S(1)} collective-permute-done((f32[128,128]{1,0:T(8,128)S(1)}, f32[128,128]{1,0:T(8,128)S(1)}, u32[]{:S(2)}, u32[]{:S(2)}) %collective-permute-start.10) | collective-permute-done | bytes 65568 | tf_op jit(solution)/shard_map/ppermute | solution.py:207
  30.1 2.0 %collective-permute-start.13 = (f32[128,128]{1,0:T(8,128)S(1)}, f32[128,128]{1,0:T(8,128)S(1)}, u32[]{:S(2)}, u32[]{:S(2)}) collective-permute-start(f32[128,128]{1,0:T(8,128)S(1)} %add.39), channel_id=1, source_target_pairs={{0,24},{4,28},{8,16},{12,20},{16,8},{20,12},{24,0},{28,4},{1,25},{... | collective-permute-start | bytes 196616 | tf_op jit(solution)/shard_map/ppermute | solution.py:207
  32.1 1.1 %collective-permute-start.12 = (f32[128,128]{1,0:T(8,128)S(1)}, f32[128,128]{1,0:T(8,128)S(1)}, u32[]{:S(2)}, u32[]{:S(2)}) collective-permute-start(f32[128,128]{1,0:T(8,128)S(1)} %add.39), channel_id=1, source_target_pairs={{0,16},{4,20},{8,24},{12,28},{16,0},{20,4},{24,8},{28,12},{1,17},{... | collective-permute-start | bytes 196616 | tf_op jit(solution)/shard_map/ppermute | solution.py:207
  33.1 0.5 %collective-permute-start.11 = (f32[128,128]{1,0:T(8,128)S(1)}, f32[128,128]{1,0:T(8,128)S(1)}, u32[]{:S(2)}, u32[]{:S(2)}) collective-permute-start(f32[128,128]{1,0:T(8,128)S(1)} %add.39), channel_id=1, source_target_pairs={{0,8},{4,12},{8,0},{12,4},{16,24},{20,28},{24,16},{28,20},{1,9},{5... | collective-permute-start | bytes 196616 | tf_op jit(solution)/shard_map/ppermute | solution.py:207
  33.6 1.9 %fetch_blocks.2.early = bf16[96,128,128]{2,1,0:T(8,128)(2,1)S(1)} custom-call(bf16[128,128,128]{2,1,0:T(8,128)(2,1)} %proj_hbm.3), custom_call_target="tpu_custom_call" | custom-call | bytes 6291456 | tf_op jit(solution)/shard_map/fetch_blocks/pallas_call | solution.py:316
  35.6 1.1 %collective-permute-done.12 = f32[128,128]{1,0:T(8,128)S(1)} collective-permute-done((f32[128,128]{1,0:T(8,128)S(1)}, f32[128,128]{1,0:T(8,128)S(1)}, u32[]{:S(2)}, u32[]{:S(2)}) %collective-permute-start.12) | collective-permute-done | bytes 65568 | tf_op jit(solution)/shard_map/ppermute | solution.py:207
  36.6 0.7 %collective-permute-done.11 = f32[128,128]{1,0:T(8,128)S(1)} collective-permute-done((f32[128,128]{1,0:T(8,128)S(1)}, f32[128,128]{1,0:T(8,128)S(1)}, u32[]{:S(2)}, u32[]{:S(2)}) %collective-permute-start.11) | collective-permute-done | bytes 65568 | tf_op jit(solution)/shard_map/ppermute | solution.py:207
  37.5 1.2 %fetch_blocks.3.late = bf16[32,128,128]{2,1,0:T(8,128)(2,1)S(1)} custom-call(bf16[128,128,128]{2,1,0:T(8,128)(2,1)} %proj_hbm.3), custom_call_target="tpu_custom_call" | custom-call | bytes 2097152 | tf_op jit(solution)/shard_map/fetch_blocks/pallas_call | solution.py:316
  38.8 0.9 %last_backward.1.corr = f32[64,128]{1,0:T(8,128)S(1)} custom-call(bf16[96,128,128]{2,1,0:T(8,128)(2,1)S(1)} %fetch_blocks.2.early, bf16[32,128,128]{2,1,0:T(8,128)(2,1)S(1)} %fetch_blocks.3.late, bf16[128,256]{1,0:T(8,128)(2,1)S(1)} %get-tuple-element.29.picks, bf16[64,128]{1,0:T(8,128)(2,1)S(1)} %get-tuple-element.30.places, ...), custom_call_target="tpu_custom_call" | custom-call | tf_op jit(solution)/shard_map/last_backward/pallas_call | solution.py:335
  39.7 1.6 %collective-permute-start.17 = (f32[64,128]{1,0:T(8,128)S(1)}, f32[64,128]{1,0:T(8,128)S(1)}, u32[]{:S(2)}, u32[]{:S(2)}) collective-permute-start(f32[64,128]{1,0:T(8,128)S(1)} %last_backward.1.corr), channel_id=1, source_target_pairs={{0,3},{1,2},{2,1},{3,0},{4,7},{5,6},{6,5},{7,4},{8,11},{9,10},{10,... | collective-permute-start | bytes 98312 | tf_op jit(solution)/shard_map/ppermute | solution.py:207
  41.4 0.5 %collective-permute-start.16 = (f32[64,128]{1,0:T(8,128)S(1)}, f32[64,128]{1,0:T(8,128)S(1)}, u32[]{:S(2)}, u32[]{:S(2)}) collective-permute-start(f32[64,128]{1,0:T(8,128)S(1)} %last_backward.1.corr), channel_id=1, source_target_pairs={{0,2},{1,3},{2,0},{3,1},{4,6},{5,7},{6,4},{7,5},{8,10},{9,11},{10,... | collective-permute-start | bytes 98312 | tf_op jit(solution)/shard_map/ppermute | solution.py:207
  41.9 2.3 %collective-permute-start.15 = (f32[64,128]{1,0:T(8,128)S(1)}, f32[64,128]{1,0:T(8,128)S(1)}, u32[]{:S(2)}, u32[]{:S(2)}) collective-permute-start(f32[64,128]{1,0:T(8,128)S(1)} %last_backward.1.corr), channel_id=1, source_target_pairs={{0,1},{1,0},{2,3},{3,2},{4,5},{5,4},{6,7},{7,6},{8,9},{9,8},{10,11... | collective-permute-start | bytes 98312 | tf_op jit(solution)/shard_map/ppermute | solution.py:207
  44.2 0.6 %constant_dynamic-slice_fusion = f32[32,128]{1,0:T(8,128)} fusion(f32[128,128]{1,0:T(8,128)S(1)} %get-tuple-element.43, s32[]{:T(128)S(6)} %select_n.3), kind=kLoop, calls=%fused_computation.7 | loop fusion | bytes 32772 | tf_op jit(solution)/shard_map/dynamic_slice | solution.py:333
  44.8 0.9 %collective-permute-done.17.far = f32[64,128]{1,0:T(8,128)S(1)} collective-permute-done((f32[64,128]{1,0:T(8,128)S(1)}, f32[64,128]{1,0:T(8,128)S(1)}, u32[]{:S(2)}, u32[]{:S(2)}) %collective-permute-start.17) | collective-permute-done | bytes 32800 | tf_op jit(solution)/shard_map/ppermute | solution.py:207
  45.7 1.0 %collective-permute-done.16.mid = f32[64,128]{1,0:T(8,128)S(1)} collective-permute-done((f32[64,128]{1,0:T(8,128)S(1)}, f32[64,128]{1,0:T(8,128)S(1)}, u32[]{:S(2)}, u32[]{:S(2)}) %collective-permute-start.16) | collective-permute-done | bytes 32800 | tf_op jit(solution)/shard_map/ppermute | solution.py:207
  46.8 0.6 %last_update.1 = f32[64,128]{1,0:T(8,128)} custom-call(f32[64,128]{1,0:T(8,128)S(1)} %get-tuple-element.34.volume, f32[64,128]{1,0:T(8,128)S(1)} %get-tuple-element.35.weight, f32[64,128]{1,0:T(8,128)S(1)} %last_backward.1.corr, f32[64,128]{1,0:T(8,128)S(1)} %collective-permute-done.15.near, f32[64,128]{1,0:T(8,128)S(1)} %collective-permute-done.16.mid, ...), custom_call_target="tpu_custom_call" | custom-call | tf_op jit(solution)/shard_map/last_update/pallas_call | solution.py:343
  (22 shorter events, 0.8 us)
Async XLA Ops:
  4.7 1.5 %collective-permute-start.2 = (f32[256,128]{1,0:T(8,128)S(1)}, f32[256,128]{1,0:T(8,128)S(1)}, u32[]{:S(2)}, u32[]{:S(2)}) collective-permute-start(f32[256,128]{1,0:T(8,128)S(1)} %get-tuple-element.32), channel_id=1, source_target_pairs={{0,4},{4,0},{8,12},{12,8},{16,20},{20,16},{24,28},{28,24},{1,5},{5... | collective-permute-start | bytes 393224 | tf_op jit(solution)/shard_map/ppermute | solution.py:207
  6.2 8.4 %collective-permute-start.5 = (f32[256,128]{1,0:T(8,128)S(1)}, f32[256,128]{1,0:T(8,128)S(1)}, u32[]{:S(2)}, u32[]{:S(2)}) collective-permute-start(f32[256,128]{1,0:T(8,128)S(1)} %add.35), channel_id=1, source_target_pairs={{0,24},{4,28},{8,16},{12,20},{16,8},{20,12},{24,0},{28,4},{1,25},{... | collective-permute-start | bytes 393224 | tf_op jit(solution)/shard_map/ppermute | solution.py:207
  10.1 6.6 %collective-permute-start.4 = (f32[256,128]{1,0:T(8,128)S(1)}, f32[256,128]{1,0:T(8,128)S(1)}, u32[]{:S(2)}, u32[]{:S(2)}) collective-permute-start(f32[256,128]{1,0:T(8,128)S(1)} %add.35), channel_id=1, source_target_pairs={{0,16},{4,20},{8,24},{12,28},{16,0},{20,4},{24,8},{28,12},{1,17},{... | collective-permute-start | bytes 393224 | tf_op jit(solution)/shard_map/ppermute | solution.py:207
  10.6 6.4 %collective-permute-start.3 = (f32[256,128]{1,0:T(8,128)S(1)}, f32[256,128]{1,0:T(8,128)S(1)}, u32[]{:S(2)}, u32[]{:S(2)}) collective-permute-start(f32[256,128]{1,0:T(8,128)S(1)} %add.35), channel_id=1, source_target_pairs={{0,8},{4,12},{8,0},{12,4},{16,24},{20,28},{24,16},{28,20},{1,9},{5... | collective-permute-start | bytes 393224 | tf_op jit(solution)/shard_map/ppermute | solution.py:207
  11.5 5.6 %collective-permute-start = (f32[64,128]{1,0:T(8,128)S(1)}, f32[64,128]{1,0:T(8,128)S(1)}, u32[]{:S(2)}, u32[]{:S(2)}) collective-permute-start(f32[64,128]{1,0:T(8,128)S(1)} %get-tuple-element.28), channel_id=1, source_target_pairs={{0,2},{1,3},{2,0},{3,1},{4,6},{5,7},{6,4},{7,5},{8,10},{9,11},{10,... | collective-permute-start | bytes 98312 | tf_op jit(solution)/shard_map/ppermute | solution.py:207
  17.0 1.7 %collective-permute-start.6 = (bf16[128,128]{1,0:T(8,128)(2,1)S(1)}, bf16[128,128]{1,0:T(8,128)(2,1)S(1)}, u32[]{:S(2)}, u32[]{:S(2)}) collective-permute-start(bf16[128,128]{1,0:T(8,128)(2,1)S(1)} %fusion.mine), channel_id=1, source_target_pairs={{0,4},{4,0},{8,12},{12,8},{16,20},{20,16},{24,28},{28,24},{1,5},{5... | collective-permute-start | bytes 98312 | tf_op jit(solution)/shard_map/ppermute | solution.py:207
  17.1 8.2 %collective-permute-start.1 = (f32[64,128]{1,0:T(8,128)S(1)}, f32[64,128]{1,0:T(8,128)S(1)}, u32[]{:S(2)}, u32[]{:S(2)}) collective-permute-start(f32[64,128]{1,0:T(8,128)S(1)} %add.33), channel_id=1, source_target_pairs={{0,1},{1,0},{2,3},{3,2},{4,5},{5,4},{6,7},{7,6},{8,9},{9,8},{10,11... | collective-permute-start | bytes 98312 | tf_op jit(solution)/shard_map/ppermute | solution.py:207
  19.7 5.8 %collective-permute-start.9 = (f32[64,128]{1,0:T(8,128)S(1)}, f32[64,128]{1,0:T(8,128)S(1)}, u32[]{:S(2)}, u32[]{:S(2)}) collective-permute-start(f32[64,128]{1,0:T(8,128)S(1)} %first_backward.1.own), channel_id=1, source_target_pairs={{0,3},{1,2},{2,1},{3,0},{4,7},{5,6},{6,5},{7,4},{8,11},{9,10},{10,... | collective-permute-start | bytes 98312 | tf_op jit(solution)/shard_map/ppermute | solution.py:207
  22.9 4.8 %collective-permute-start.8 = (f32[64,128]{1,0:T(8,128)S(1)}, f32[64,128]{1,0:T(8,128)S(1)}, u32[]{:S(2)}, u32[]{:S(2)}) collective-permute-start(f32[64,128]{1,0:T(8,128)S(1)} %first_backward.1.own), channel_id=1, source_target_pairs={{0,2},{1,3},{2,0},{3,1},{4,6},{5,7},{6,4},{7,5},{8,10},{9,11},{10,... | collective-permute-start | bytes 98312 | tf_op jit(solution)/shard_map/ppermute | solution.py:207
  22.9 4.8 %collective-permute-start.7 = (f32[64,128]{1,0:T(8,128)S(1)}, f32[64,128]{1,0:T(8,128)S(1)}, u32[]{:S(2)}, u32[]{:S(2)}) collective-permute-start(f32[64,128]{1,0:T(8,128)S(1)} %first_backward.1.own), channel_id=1, source_target_pairs={{0,1},{1,0},{2,3},{3,2},{4,5},{5,4},{6,7},{7,6},{8,9},{9,8},{10,11... | collective-permute-start | bytes 98312 | tf_op jit(solution)/shard_map/ppermute | solution.py:207
  28.8 1.3 %collective-permute-start.10 = (f32[128,128]{1,0:T(8,128)S(1)}, f32[128,128]{1,0:T(8,128)S(1)}, u32[]{:S(2)}, u32[]{:S(2)}) collective-permute-start(f32[128,128]{1,0:T(8,128)S(1)} %get-tuple-element.37), channel_id=1, source_target_pairs={{0,4},{4,0},{8,12},{12,8},{16,20},{20,16},{24,28},{28,24},{1,5},{5... | collective-permute-start | bytes 196616 | tf_op jit(solution)/shard_map/ppermute | solution.py:207
  30.1 5.5 %collective-permute-start.13 = (f32[128,128]{1,0:T(8,128)S(1)}, f32[128,128]{1,0:T(8,128)S(1)}, u32[]{:S(2)}, u32[]{:S(2)}) collective-permute-start(f32[128,128]{1,0:T(8,128)S(1)} %add.39), channel_id=1, source_target_pairs={{0,24},{4,28},{8,16},{12,20},{16,8},{20,12},{24,0},{28,4},{1,25},{... | collective-permute-start | bytes 196616 | tf_op jit(solution)/shard_map/ppermute | solution.py:207
  32.1 4.6 %collective-permute-start.12 = (f32[128,128]{1,0:T(8,128)S(1)}, f32[128,128]{1,0:T(8,128)S(1)}, u32[]{:S(2)}, u32[]{:S(2)}) collective-permute-start(f32[128,128]{1,0:T(8,128)S(1)} %add.39), channel_id=1, source_target_pairs={{0,16},{4,20},{8,24},{12,28},{16,0},{20,4},{24,8},{28,12},{1,17},{... | collective-permute-start | bytes 196616 | tf_op jit(solution)/shard_map/ppermute | solution.py:207
  33.1 4.3 %collective-permute-start.11 = (f32[128,128]{1,0:T(8,128)S(1)}, f32[128,128]{1,0:T(8,128)S(1)}, u32[]{:S(2)}, u32[]{:S(2)}) collective-permute-start(f32[128,128]{1,0:T(8,128)S(1)} %add.39), channel_id=1, source_target_pairs={{0,8},{4,12},{8,0},{12,4},{16,24},{20,28},{24,16},{28,20},{1,9},{5... | collective-permute-start | bytes 196616 | tf_op jit(solution)/shard_map/ppermute | solution.py:207
  37.4 1.3 %collective-permute-start.14 = (bf16[128,128]{1,0:T(8,128)(2,1)S(1)}, bf16[128,128]{1,0:T(8,128)(2,1)S(1)}, u32[]{:S(2)}, u32[]{:S(2)}) collective-permute-start(bf16[128,128]{1,0:T(8,128)(2,1)S(1)} %get-tuple-element.42.mine), channel_id=1, source_target_pairs={{0,4},{4,0},{8,12},{12,8},{16,20},{20,16},{24,28},{28,24},{1,5},{5... | collective-permute-start | bytes 98312 | tf_op jit(solution)/shard_map/ppermute | solution.py:207
  39.7 5.9 %collective-permute-start.17 = (f32[64,128]{1,0:T(8,128)S(1)}, f32[64,128]{1,0:T(8,128)S(1)}, u32[]{:S(2)}, u32[]{:S(2)}) collective-permute-start(f32[64,128]{1,0:T(8,128)S(1)} %last_backward.1.corr), channel_id=1, source_target_pairs={{0,3},{1,2},{2,1},{3,0},{4,7},{5,6},{6,5},{7,4},{8,11},{9,10},{10,... | collective-permute-start | bytes 98312 | tf_op jit(solution)/shard_map/ppermute | solution.py:207
  41.4 5.3 %collective-permute-start.16 = (f32[64,128]{1,0:T(8,128)S(1)}, f32[64,128]{1,0:T(8,128)S(1)}, u32[]{:S(2)}, u32[]{:S(2)}) collective-permute-start(f32[64,128]{1,0:T(8,128)S(1)} %last_backward.1.corr), channel_id=1, source_target_pairs={{0,2},{1,3},{2,0},{3,1},{4,6},{5,7},{6,4},{7,5},{8,10},{9,11},{10,... | collective-permute-start | bytes 98312 | tf_op jit(solution)/shard_map/ppermute | solution.py:207
  41.9 4.9 %collective-permute-start.15 = (f32[64,128]{1,0:T(8,128)S(1)}, f32[64,128]{1,0:T(8,128)S(1)}, u32[]{:S(2)}, u32[]{:S(2)}) collective-permute-start(f32[64,128]{1,0:T(8,128)S(1)} %last_backward.1.corr), channel_id=1, source_target_pairs={{0,1},{1,0},{2,3},{3,2},{4,5},{5,4},{6,7},{7,6},{8,9},{9,8},{10,11... | collective-permute-start | bytes 98312 | tf_op jit(solution)/shard_map/ppermute | solution.py:207

commit v10 on v9

--- a/solution.py
+++ b/solution.py
@@ -218,9 +218,8 @@
             x, bits = x + swap(x, "slab", bits[0]), []
             continue
         first, second, bits = bits[0], bits[1], bits[2:]
-        near = swap(x, "slab", first)
-        other = swap(x, "slab", second), swap(x, "slab", first | second)
-        x = (x + near) + (other[0] + other[1])
+        far = swap(x, "slab", first | second)
+        x = (x + swap(x, "slab", first)) + (swap(x, "slab", second) + far)
     return x, after
 
 

time: 47.6 us -> 47.6 us (level)
  no operation moved by 1% of the time
where the time goes in v10:
time: 47.6 us; the launch traced here: 47.4 us
  starting transfers between devices  22.4 us (47%)
  Pallas kernels  12 us (25%)
  waiting for transfers between devices  10.8 us (23%)
  between operations  1.46 us (3%)
  local copies, waits for them, and re-layouts  0.61 us (1%)
    ppermute x18, starting transfers between devices, swap(): return lax.ppermute(x, axis, [(i, i ^ bit) for i in range(size)])  22.4 us
    ppermute x18, waiting for transfers between devices, swap(): return lax.ppermute(x, axis, [(i, i ^ bit) for i in range(size)])  10.8 us
    pallas_call x1, Pallas kernels, local(): pl.pallas_call(first_forward(slabs, capacity, ray_dev), out_shape=(pltpu....  3.4 us
    pallas_call x2, Pallas kernels, local(): pl.pallas_call(fetch_blocks(low), out_shape=pltpu.VMEM((size,) + projecto...  3.13 us
    pallas_call x1, Pallas kernels, local(): pl.pallas_call(turn_blocks, out_shape=pltpu.VMEM(projector.shape, BF16),...  1.13 us
    pallas_call x1, Pallas kernels, local(): pl.pallas_call(next_forward(ray_dev), out_shape=(vmem(vox_dev), vmem(vox_...  1 us
  transfers between devices with their start and end apart: 18, of which 11 were waited for; matrix products, arithmetic and copies ran while one was open for 1% of the time, Pallas kernels for 13%

profile of v10, /device:TPU:0, one launch (start us, length us, event | category | flops | bytes accessed | tf_op | source)
XLA Modules:
  0.0 47.4 jit_solution(11988622148080609919)
XLA Ops:
  1.3 3.4 %first_forward.1 = (bf16[128,128,128]{2,1,0:T(8,128)(2,1)S(1)}, s32[1,128]{1,0:T(1,128)S(1)}, s32[1,128]{1,0:T(1,128)S(1)}, f32[64,128]{1,0:T(8,128)S(1)}, f32[3...) custom-call(bf16[128,128,128]{2,1,0:T(8,128)(2,1)} %proj_hbm.3, s32[1,128]{1,0:T(1,128)} %bitcast.4, ...), custom_call_target="tpu_custom_call" | custom-call | tf_op jit(solution)/shard_map/first_forward/pallas_call | solution.py:248
  4.7 0.5 %collective-permute-start.2 = (f32[256,128]{1,0:T(8,128)S(1)}, f32[256,128]{1,0:T(8,128)S(1)}, u32[]{:S(2)}, u32[]{:S(2)}) collective-permute-start(f32[256,128]{1,0:T(8,128)S(1)} %get-tuple-element.32), channel_id=1, source_target_pairs={{0,4},{4,0},{8,12},{12,8},{16,20},{20,16},{24,28},{28,24},{1,5},{5... | collective-permute-start | bytes 393224 | tf_op jit(solution)/shard_map/ppermute | solution.py:207
  5.2 1.0 %collective-permute-done.2 = f32[256,128]{1,0:T(8,128)S(1)} collective-permute-done((f32[256,128]{1,0:T(8,128)S(1)}, f32[256,128]{1,0:T(8,128)S(1)}, u32[]{:S(2)}, u32[]{:S(2)}) %collective-permute-start.2) | collective-permute-done | bytes 131104 | tf_op jit(solution)/shard_map/ppermute | solution.py:207
  6.2 3.9 %collective-permute-start.5 = (f32[256,128]{1,0:T(8,128)S(1)}, f32[256,128]{1,0:T(8,128)S(1)}, u32[]{:S(2)}, u32[]{:S(2)}) collective-permute-start(f32[256,128]{1,0:T(8,128)S(1)} %add.35), channel_id=1, source_target_pairs={{0,24},{4,28},{8,16},{12,20},{16,8},{20,12},{24,0},{28,4},{1,25},{... | collective-permute-start | bytes 393224 | tf_op jit(solution)/shard_map/ppermute | solution.py:207
  10.1 0.5 %collective-permute-start.4 = (f32[256,128]{1,0:T(8,128)S(1)}, f32[256,128]{1,0:T(8,128)S(1)}, u32[]{:S(2)}, u32[]{:S(2)}) collective-permute-start(f32[256,128]{1,0:T(8,128)S(1)} %add.35), channel_id=1, source_target_pairs={{0,16},{4,20},{8,24},{12,28},{16,0},{20,4},{24,8},{28,12},{1,17},{... | collective-permute-start | bytes 393224 | tf_op jit(solution)/shard_map/ppermute | solution.py:207
  10.7 0.8 %name_places.1 = (bf16[128,256]{1,0:T(8,128)(2,1)S(1)}, bf16[256,128]{1,0:T(8,128)(2,1)S(1)}, bf16[128,64]{1,0:T(8,128)(2,1)S(1)}, bf16[64,128]{1,0:T(8,128)(2,1)S(1)}, f32[64,128]{1,0:T(8,128)S(1)}) custom-call(bf16[128,128,128]{2,1,0:T(8,128)(2,1)S(1)} %get-tuple-element.22.proj, s32[1,128]{1,0:T(1,128)S(1)} %get-tuple-element.23.rows, ...), custom_call_target="tpu_custom_call" | custom-call | bytes 1048576 | tf_op jit(solution)/shard_map/name_places/pallas_call | solution.py:266
  11.5 3.1 %collective-permute-start = (f32[64,128]{1,0:T(8,128)S(1)}, f32[64,128]{1,0:T(8,128)S(1)}, u32[]{:S(2)}, u32[]{:S(2)}) collective-permute-start(f32[64,128]{1,0:T(8,128)S(1)} %get-tuple-element.28), channel_id=1, source_target_pairs={{0,2},{1,3},{2,0},{3,1},{4,6},{5,7},{6,4},{7,5},{8,10},{9,11},{10,... | collective-permute-start | bytes 98312 | tf_op jit(solution)/shard_map/ppermute | solution.py:207
  14.6 2.1 %collective-permute-done.4 = f32[256,128]{1,0:T(8,128)S(1)} collective-permute-done((f32[256,128]{1,0:T(8,128)S(1)}, f32[256,128]{1,0:T(8,128)S(1)}, u32[]{:S(2)}, u32[]{:S(2)}) %collective-permute-start.4) | collective-permute-done | bytes 131104 | tf_op jit(solution)/shard_map/ppermute | solution.py:207
  16.7 0.3 collective-permute-done.3
  17.1 1.6 %collective-permute-start.1 = (f32[64,128]{1,0:T(8,128)S(1)}, f32[64,128]{1,0:T(8,128)S(1)}, u32[]{:S(2)}, u32[]{:S(2)}) collective-permute-start(f32[64,128]{1,0:T(8,128)S(1)} %add.33), channel_id=1, source_target_pairs={{0,1},{1,0},{2,3},{3,2},{4,5},{5,4},{6,7},{7,6},{8,9},{9,8},{10,11... | collective-permute-start | bytes 98312 | tf_op jit(solution)/shard_map/ppermute | solution.py:207
  18.8 0.9 %first_backward.1.own = f32[64,128]{1,0:T(8,128)S(1)} custom-call(bf16[128,128,128]{2,1,0:T(8,128)(2,1)S(1)} %get-tuple-element.22.proj, bf16[128,256]{1,0:T(8,128)(2,1)S(1)} %get-tuple-element.29.picks, bf16[64,128]{1,0:T(8,128)(2,1)S(1)} %get-tuple-element.30.places, bf16[128,128]{1,0:T(8,128)(2,1)S(1)} %fusion.mine, ...), custom_call_target="tpu_custom_call" | custom-call | tf_op jit(solution)/shard_map/first_backward/pallas_call | solution.py:294
  19.7 3.2 %collective-permute-start.9 = (f32[64,128]{1,0:T(8,128)S(1)}, f32[64,128]{1,0:T(8,128)S(1)}, u32[]{:S(2)}, u32[]{:S(2)}) collective-permute-start(f32[64,128]{1,0:T(8,128)S(1)} %first_backward.1.own), channel_id=1, source_target_pairs={{0,3},{1,2},{2,1},{3,0},{4,7},{5,6},{6,5},{7,4},{8,11},{9,10},{10,... | collective-permute-start | bytes 98312 | tf_op jit(solution)/shard_map/ppermute | solution.py:207
  22.9 1.3 %collective-permute-start.7 = (f32[64,128]{1,0:T(8,128)S(1)}, f32[64,128]{1,0:T(8,128)S(1)}, u32[]{:S(2)}, u32[]{:S(2)}) collective-permute-start(f32[64,128]{1,0:T(8,128)S(1)} %first_backward.1.own), channel_id=1, source_target_pairs={{0,1},{1,0},{2,3},{3,2},{4,5},{5,4},{6,7},{7,6},{8,9},{9,8},{10,11... | collective-permute-start | bytes 98312 | tf_op jit(solution)/shard_map/ppermute | solution.py:207
  24.2 1.1 %turn_blocks.1.proj = bf16[128,128,128]{2,1,0:T(8,128)(2,1)S(1)} custom-call(bf16[128,128,128]{2,1,0:T(8,128)(2,1)S(1)} %get-tuple-element.22.proj), custom_call_target="tpu_custom_call" | custom-call | bytes 8388608 | tf_op jit(solution)/shard_map/turn_blocks/pallas_call | solution.py:278
  25.5 2.2 %collective-permute-done.8.mid = f32[64,128]{1,0:T(8,128)S(1)} collective-permute-done((f32[64,128]{1,0:T(8,128)S(1)}, f32[64,128]{1,0:T(8,128)S(1)}, u32[]{:S(2)}, u32[]{:S(2)}) %collective-permute-start.8) | collective-permute-done | bytes 32800 | tf_op jit(solution)/shard_map/ppermute | solution.py:207
  27.7 1.0 %next_forward.1 = (f32[64,128]{1,0:T(8,128)S(1)}, f32[64,128]{1,0:T(8,128)S(1)}, f32[128,128]{1,0:T(8,128)S(1)}, f32[128,128]{1,0:T(8,128)S(1)}) custom-call(bf16[128,128,128]{2,1,0:T(8,128)(2,1)S(1)} %turn_blocks.1.proj, bf16[128,64]{1,0:T(8,128)(2,1)S(1)} %get-tuple-element.25.picks, bf16[256,128]{1,0:T(8,128)(2,1)S(1)} %get-tuple-element.26.places, ...), custom_call_target="tpu_custom_call" | custom-call | tf_op jit(solution)/shard_map/next_forward/pallas_call | solution.py:304
  28.8 1.2 %collective-permute-done.10 = f32[128,128]{1,0:T(8,128)S(1)} collective-permute-done((f32[128,128]{1,0:T(8,128)S(1)}, f32[128,128]{1,0:T(8,128)S(1)}, u32[]{:S(2)}, u32[]{:S(2)}) %collective-permute-start.10) | collective-permute-done | bytes 65568 | tf_op jit(solution)/shard_map/ppermute | solution.py:207
  30.1 2.0 %collective-permute-start.13 = (f32[128,128]{1,0:T(8,128)S(1)}, f32[128,128]{1,0:T(8,128)S(1)}, u32[]{:S(2)}, u32[]{:S(2)}) collective-permute-start(f32[128,128]{1,0:T(8,128)S(1)} %add.39), channel_id=1, source_target_pairs={{0,24},{4,28},{8,16},{12,20},{16,8},{20,12},{24,0},{28,4},{1,25},{... | collective-permute-start | bytes 196616 | tf_op jit(solution)/shard_map/ppermute | solution.py:207
  32.1 1.1 %collective-permute-start.12 = (f32[128,128]{1,0:T(8,128)S(1)}, f32[128,128]{1,0:T(8,128)S(1)}, u32[]{:S(2)}, u32[]{:S(2)}) collective-permute-start(f32[128,128]{1,0:T(8,128)S(1)} %add.39), channel_id=1, source_target_pairs={{0,16},{4,20},{8,24},{12,28},{16,0},{20,4},{24,8},{28,12},{1,17},{... | collective-permute-start | bytes 196616 | tf_op jit(solution)/shard_map/ppermute | solution.py:207
  33.1 0.5 %collective-permute-start.11 = (f32[128,128]{1,0:T(8,128)S(1)}, f32[128,128]{1,0:T(8,128)S(1)}, u32[]{:S(2)}, u32[]{:S(2)}) collective-permute-start(f32[128,128]{1,0:T(8,128)S(1)} %add.39), channel_id=1, source_target_pairs={{0,8},{4,12},{8,0},{12,4},{16,24},{20,28},{24,16},{28,20},{1,9},{5... | collective-permute-start | bytes 196616 | tf_op jit(solution)/shard_map/ppermute | solution.py:207
  33.6 1.9 %fetch_blocks.2.early = bf16[96,128,128]{2,1,0:T(8,128)(2,1)S(1)} custom-call(bf16[128,128,128]{2,1,0:T(8,128)(2,1)} %proj_hbm.3), custom_call_target="tpu_custom_call" | custom-call | bytes 6291456 | tf_op jit(solution)/shard_map/fetch_blocks/pallas_call | solution.py:315
  35.6 1.1 %collective-permute-done.12 = f32[128,128]{1,0:T(8,128)S(1)} collective-permute-done((f32[128,128]{1,0:T(8,128)S(1)}, f32[128,128]{1,0:T(8,128)S(1)}, u32[]{:S(2)}, u32[]{:S(2)}) %collective-permute-start.12) | collective-permute-done | bytes 65568 | tf_op jit(solution)/shard_map/ppermute | solution.py:207
  36.6 0.7 %collective-permute-done.11 = f32[128,128]{1,0:T(8,128)S(1)} collective-permute-done((f32[128,128]{1,0:T(8,128)S(1)}, f32[128,128]{1,0:T(8,128)S(1)}, u32[]{:S(2)}, u32[]{:S(2)}) %collective-permute-start.11) | collective-permute-done | bytes 65568 | tf_op jit(solution)/shard_map/ppermute | solution.py:207
  37.5 1.2 %fetch_blocks.3.late = bf16[32,128,128]{2,1,0:T(8,128)(2,1)S(1)} custom-call(bf16[128,128,128]{2,1,0:T(8,128)(2,1)} %proj_hbm.3), custom_call_target="tpu_custom_call" | custom-call | bytes 2097152 | tf_op jit(solution)/shard_map/fetch_blocks/pallas_call | solution.py:315
  38.8 0.9 %last_backward.1.corr = f32[64,128]{1,0:T(8,128)S(1)} custom-call(bf16[96,128,128]{2,1,0:T(8,128)(2,1)S(1)} %fetch_blocks.2.early, bf16[32,128,128]{2,1,0:T(8,128)(2,1)S(1)} %fetch_blocks.3.late, bf16[128,256]{1,0:T(8,128)(2,1)S(1)} %get-tuple-element.29.picks, bf16[64,128]{1,0:T(8,128)(2,1)S(1)} %get-tuple-element.30.places, ...), custom_call_target="tpu_custom_call" | custom-call | tf_op jit(solution)/shard_map/last_backward/pallas_call | solution.py:334
  39.7 1.6 %collective-permute-start.17 = (f32[64,128]{1,0:T(8,128)S(1)}, f32[64,128]{1,0:T(8,128)S(1)}, u32[]{:S(2)}, u32[]{:S(2)}) collective-permute-start(f32[64,128]{1,0:T(8,128)S(1)} %last_backward.1.corr), channel_id=1, source_target_pairs={{0,3},{1,2},{2,1},{3,0},{4,7},{5,6},{6,5},{7,4},{8,11},{9,10},{10,... | collective-permute-start | bytes 98312 | tf_op jit(solution)/shard_map/ppermute | solution.py:207
  41.4 0.5 %collective-permute-start.16 = (f32[64,128]{1,0:T(8,128)S(1)}, f32[64,128]{1,0:T(8,128)S(1)}, u32[]{:S(2)}, u32[]{:S(2)}) collective-permute-start(f32[64,128]{1,0:T(8,128)S(1)} %last_backward.1.corr), channel_id=1, source_target_pairs={{0,2},{1,3},{2,0},{3,1},{4,6},{5,7},{6,4},{7,5},{8,10},{9,11},{10,... | collective-permute-start | bytes 98312 | tf_op jit(solution)/shard_map/ppermute | solution.py:207
  41.9 2.3 %collective-permute-start.15 = (f32[64,128]{1,0:T(8,128)S(1)}, f32[64,128]{1,0:T(8,128)S(1)}, u32[]{:S(2)}, u32[]{:S(2)}) collective-permute-start(f32[64,128]{1,0:T(8,128)S(1)} %last_backward.1.corr), channel_id=1, source_target_pairs={{0,1},{1,0},{2,3},{3,2},{4,5},{5,4},{6,7},{7,6},{8,9},{9,8},{10,11... | collective-permute-start | bytes 98312 | tf_op jit(solution)/shard_map/ppermute | solution.py:207
  44.2 0.6 %constant_dynamic-slice_fusion = f32[32,128]{1,0:T(8,128)} fusion(f32[128,128]{1,0:T(8,128)S(1)} %get-tuple-element.43, s32[]{:T(128)S(6)} %select_n.3), kind=kLoop, calls=%fused_computation.7 | loop fusion | bytes 32772 | tf_op jit(solution)/shard_map/dynamic_slice | solution.py:332
  44.8 0.9 %collective-permute-done.17.far = f32[64,128]{1,0:T(8,128)S(1)} collective-permute-done((f32[64,128]{1,0:T(8,128)S(1)}, f32[64,128]{1,0:T(8,128)S(1)}, u32[]{:S(2)}, u32[]{:S(2)}) %collective-permute-start.17) | collective-permute-done | bytes 32800 | tf_op jit(solution)/shard_map/ppermute | solution.py:207
  45.7 1.0 %collective-permute-done.16.mid = f32[64,128]{1,0:T(8,128)S(1)} collective-permute-done((f32[64,128]{1,0:T(8,128)S(1)}, f32[64,128]{1,0:T(8,128)S(1)}, u32[]{:S(2)}, u32[]{:S(2)}) %collective-permute-start.16) | collective-permute-done | bytes 32800 | tf_op jit(solution)/shard_map/ppermute | solution.py:207
  46.8 0.6 %last_update.1 = f32[64,128]{1,0:T(8,128)} custom-call(f32[64,128]{1,0:T(8,128)S(1)} %get-tuple-element.34.volume, f32[64,128]{1,0:T(8,128)S(1)} %get-tuple-element.35.weight, f32[64,128]{1,0:T(8,128)S(1)} %last_backward.1.corr, f32[64,128]{1,0:T(8,128)S(1)} %collective-permute-done.15.near, f32[64,128]{1,0:T(8,128)S(1)} %collective-permute-done.16.mid, ...), custom_call_target="tpu_custom_call" | custom-call | tf_op jit(solution)/shard_map/last_update/pallas_call | solution.py:342
  (22 shorter events, 0.8 us)
Async XLA Ops:
  4.7 1.5 %collective-permute-start.2 = (f32[256,128]{1,0:T(8,128)S(1)}, f32[256,128]{1,0:T(8,128)S(1)}, u32[]{:S(2)}, u32[]{:S(2)}) collective-permute-start(f32[256,128]{1,0:T(8,128)S(1)} %get-tuple-element.32), channel_id=1, source_target_pairs={{0,4},{4,0},{8,12},{12,8},{16,20},{20,16},{24,28},{28,24},{1,5},{5... | collective-permute-start | bytes 393224 | tf_op jit(solution)/shard_map/ppermute | solution.py:207
  6.2 8.4 %collective-permute-start.5 = (f32[256,128]{1,0:T(8,128)S(1)}, f32[256,128]{1,0:T(8,128)S(1)}, u32[]{:S(2)}, u32[]{:S(2)}) collective-permute-start(f32[256,128]{1,0:T(8,128)S(1)} %add.35), channel_id=1, source_target_pairs={{0,24},{4,28},{8,16},{12,20},{16,8},{20,12},{24,0},{28,4},{1,25},{... | collective-permute-start | bytes 393224 | tf_op jit(solution)/shard_map/ppermute | solution.py:207
  10.1 6.6 %collective-permute-start.4 = (f32[256,128]{1,0:T(8,128)S(1)}, f32[256,128]{1,0:T(8,128)S(1)}, u32[]{:S(2)}, u32[]{:S(2)}) collective-permute-start(f32[256,128]{1,0:T(8,128)S(1)} %add.35), channel_id=1, source_target_pairs={{0,16},{4,20},{8,24},{12,28},{16,0},{20,4},{24,8},{28,12},{1,17},{... | collective-permute-start | bytes 393224 | tf_op jit(solution)/shard_map/ppermute | solution.py:207
  10.6 6.4 %collective-permute-start.3 = (f32[256,128]{1,0:T(8,128)S(1)}, f32[256,128]{1,0:T(8,128)S(1)}, u32[]{:S(2)}, u32[]{:S(2)}) collective-permute-start(f32[256,128]{1,0:T(8,128)S(1)} %add.35), channel_id=1, source_target_pairs={{0,8},{4,12},{8,0},{12,4},{16,24},{20,28},{24,16},{28,20},{1,9},{5... | collective-permute-start | bytes 393224 | tf_op jit(solution)/shard_map/ppermute | solution.py:207
  11.5 5.6 %collective-permute-start = (f32[64,128]{1,0:T(8,128)S(1)}, f32[64,128]{1,0:T(8,128)S(1)}, u32[]{:S(2)}, u32[]{:S(2)}) collective-permute-start(f32[64,128]{1,0:T(8,128)S(1)} %get-tuple-element.28), channel_id=1, source_target_pairs={{0,2},{1,3},{2,0},{3,1},{4,6},{5,7},{6,4},{7,5},{8,10},{9,11},{10,... | collective-permute-start | bytes 98312 | tf_op jit(solution)/shard_map/ppermute | solution.py:207
  17.0 1.7 %collective-permute-start.6 = (bf16[128,128]{1,0:T(8,128)(2,1)S(1)}, bf16[128,128]{1,0:T(8,128)(2,1)S(1)}, u32[]{:S(2)}, u32[]{:S(2)}) collective-permute-start(bf16[128,128]{1,0:T(8,128)(2,1)S(1)} %fusion.mine), channel_id=1, source_target_pairs={{0,4},{4,0},{8,12},{12,8},{16,20},{20,16},{24,28},{28,24},{1,5},{5... | collective-permute-start | bytes 98312 | tf_op jit(solution)/shard_map/ppermute | solution.py:207
  17.1 8.2 %collective-permute-start.1 = (f32[64,128]{1,0:T(8,128)S(1)}, f32[64,128]{1,0:T(8,128)S(1)}, u32[]{:S(2)}, u32[]{:S(2)}) collective-permute-start(f32[64,128]{1,0:T(8,128)S(1)} %add.33), channel_id=1, source_target_pairs={{0,1},{1,0},{2,3},{3,2},{4,5},{5,4},{6,7},{7,6},{8,9},{9,8},{10,11... | collective-permute-start | bytes 98312 | tf_op jit(solution)/shard_map/ppermute | solution.py:207
  19.7 5.8 %collective-permute-start.9 = (f32[64,128]{1,0:T(8,128)S(1)}, f32[64,128]{1,0:T(8,128)S(1)}, u32[]{:S(2)}, u32[]{:S(2)}) collective-permute-start(f32[64,128]{1,0:T(8,128)S(1)} %first_backward.1.own), channel_id=1, source_target_pairs={{0,3},{1,2},{2,1},{3,0},{4,7},{5,6},{6,5},{7,4},{8,11},{9,10},{10,... | collective-permute-start | bytes 98312 | tf_op jit(solution)/shard_map/ppermute | solution.py:207
  22.9 4.8 %collective-permute-start.8 = (f32[64,128]{1,0:T(8,128)S(1)}, f32[64,128]{1,0:T(8,128)S(1)}, u32[]{:S(2)}, u32[]{:S(2)}) collective-permute-start(f32[64,128]{1,0:T(8,128)S(1)} %first_backward.1.own), channel_id=1, source_target_pairs={{0,2},{1,3},{2,0},{3,1},{4,6},{5,7},{6,4},{7,5},{8,10},{9,11},{10,... | collective-permute-start | bytes 98312 | tf_op jit(solution)/shard_map/ppermute | solution.py:207
  22.9 4.8 %collective-permute-start.7 = (f32[64,128]{1,0:T(8,128)S(1)}, f32[64,128]{1,0:T(8,128)S(1)}, u32[]{:S(2)}, u32[]{:S(2)}) collective-permute-start(f32[64,128]{1,0:T(8,128)S(1)} %first_backward.1.own), channel_id=1, source_target_pairs={{0,1},{1,0},{2,3},{3,2},{4,5},{5,4},{6,7},{7,6},{8,9},{9,8},{10,11... | collective-permute-start | bytes 98312 | tf_op jit(solution)/shard_map/ppermute | solution.py:207
  28.8 1.3 %collective-permute-start.10 = (f32[128,128]{1,0:T(8,128)S(1)}, f32[128,128]{1,0:T(8,128)S(1)}, u32[]{:S(2)}, u32[]{:S(2)}) collective-permute-start(f32[128,128]{1,0:T(8,128)S(1)} %get-tuple-element.37), channel_id=1, source_target_pairs={{0,4},{4,0},{8,12},{12,8},{16,20},{20,16},{24,28},{28,24},{1,5},{5... | collective-permute-start | bytes 196616 | tf_op jit(solution)/shard_map/ppermute | solution.py:207
  30.1 5.5 %collective-permute-start.13 = (f32[128,128]{1,0:T(8,128)S(1)}, f32[128,128]{1,0:T(8,128)S(1)}, u32[]{:S(2)}, u32[]{:S(2)}) collective-permute-start(f32[128,128]{1,0:T(8,128)S(1)} %add.39), channel_id=1, source_target_pairs={{0,24},{4,28},{8,16},{12,20},{16,8},{20,12},{24,0},{28,4},{1,25},{... | collective-permute-start | bytes 196616 | tf_op jit(solution)/shard_map/ppermute | solution.py:207
  32.1 4.6 %collective-permute-start.12 = (f32[128,128]{1,0:T(8,128)S(1)}, f32[128,128]{1,0:T(8,128)S(1)}, u32[]{:S(2)}, u32[]{:S(2)}) collective-permute-start(f32[128,128]{1,0:T(8,128)S(1)} %add.39), channel_id=1, source_target_pairs={{0,16},{4,20},{8,24},{12,28},{16,0},{20,4},{24,8},{28,12},{1,17},{... | collective-permute-start | bytes 196616 | tf_op jit(solution)/shard_map/ppermute | solution.py:207
  33.1 4.3 %collective-permute-start.11 = (f32[128,128]{1,0:T(8,128)S(1)}, f32[128,128]{1,0:T(8,128)S(1)}, u32[]{:S(2)}, u32[]{:S(2)}) collective-permute-start(f32[128,128]{1,0:T(8,128)S(1)} %add.39), channel_id=1, source_target_pairs={{0,8},{4,12},{8,0},{12,4},{16,24},{20,28},{24,16},{28,20},{1,9},{5... | collective-permute-start | bytes 196616 | tf_op jit(solution)/shard_map/ppermute | solution.py:207
  37.4 1.3 %collective-permute-start.14 = (bf16[128,128]{1,0:T(8,128)(2,1)S(1)}, bf16[128,128]{1,0:T(8,128)(2,1)S(1)}, u32[]{:S(2)}, u32[]{:S(2)}) collective-permute-start(bf16[128,128]{1,0:T(8,128)(2,1)S(1)} %get-tuple-element.42.mine), channel_id=1, source_target_pairs={{0,4},{4,0},{8,12},{12,8},{16,20},{20,16},{24,28},{28,24},{1,5},{5... | collective-permute-start | bytes 98312 | tf_op jit(solution)/shard_map/ppermute | solution.py:207
  39.7 5.9 %collective-permute-start.17 = (f32[64,128]{1,0:T(8,128)S(1)}, f32[64,128]{1,0:T(8,128)S(1)}, u32[]{:S(2)}, u32[]{:S(2)}) collective-permute-start(f32[64,128]{1,0:T(8,128)S(1)} %last_backward.1.corr), channel_id=1, source_target_pairs={{0,3},{1,2},{2,1},{3,0},{4,7},{5,6},{6,5},{7,4},{8,11},{9,10},{10,... | collective-permute-start | bytes 98312 | tf_op jit(solution)/shard_map/ppermute | solution.py:207
  41.4 5.3 %collective-permute-start.16 = (f32[64,128]{1,0:T(8,128)S(1)}, f32[64,128]{1,0:T(8,128)S(1)}, u32[]{:S(2)}, u32[]{:S(2)}) collective-permute-start(f32[64,128]{1,0:T(8,128)S(1)} %last_backward.1.corr), channel_id=1, source_target_pairs={{0,2},{1,3},{2,0},{3,1},{4,6},{5,7},{6,4},{7,5},{8,10},{9,11},{10,... | collective-permute-start | bytes 98312 | tf_op jit(solution)/shard_map/ppermute | solution.py:207
  41.9 4.9 %collective-permute-start.15 = (f32[64,128]{1,0:T(8,128)S(1)}, f32[64,128]{1,0:T(8,128)S(1)}, u32[]{:S(2)}, u32[]{:S(2)}) collective-permute-start(f32[64,128]{1,0:T(8,128)S(1)} %last_backward.1.corr), channel_id=1, source_target_pairs={{0,1},{1,0},{2,3},{3,2},{4,5},{5,4},{6,7},{7,6},{8,9},{9,8},{10,11... | collective-permute-start | bytes 98312 | tf_op jit(solution)/shard_map/ppermute | solution.py:207

commit v11 on v10

--- a/solution.py
+++ b/solution.py
@@ -284,7 +284,7 @@
         cost_estimate=pl.CostEstimate(flops=0, bytes_accessed=2 * projector.size * 2, transcendentals=0),
         name="turn_blocks",
     )(proj)
-    sums, _ = over_slabs(mine, theirs)
+    sums, to_vox = over_slabs(mine, theirs, to_vox)
     row_weight = 1.0 / jnp.maximum(sums[half:], 1.0)
     weighted = (row_weight * sums[:half]).astype(BF16)
     angles = lax.axis_size("angle")

time: 47.6 us -> 47.6 us (level)
  transfers between devices with their start and end apart: 18 -> 18, of which waited for: 11 -> 12; matrix products, arithmetic and copies ran while one was open for 1% -> 1% of each run, Pallas kernels for 13% -> 13%
where the time goes in v11:
time: 47.6 us; the launch traced here: 47.4 us
  starting transfers between devices  22.3 us (47%)
  Pallas kernels  12 us (25%)
  waiting for transfers between devices  10.9 us (23%)
  between operations  1.46 us (3%)
  local copies, waits for them, and re-layouts  0.61 us (1%)
    ppermute x18, starting transfers between devices, swap(): return lax.ppermute(x, axis, [(i, i ^ bit) for i in range(size)])  22.3 us
    ppermute x18, waiting for transfers between devices, swap(): return lax.ppermute(x, axis, [(i, i ^ bit) for i in range(size)])  10.9 us
    pallas_call x1, Pallas kernels, local(): pl.pallas_call(first_forward(slabs, capacity, ray_dev), out_shape=(pltpu....  3.4 us
    pallas_call x2, Pallas kernels, local(): pl.pallas_call(fetch_blocks(low), out_shape=pltpu.VMEM((size,) + projecto...  3.13 us
    pallas_call x1, Pallas kernels, local(): pl.pallas_call(turn_blocks, out_shape=pltpu.VMEM(projector.shape, BF16),...  1.13 us
    pallas_call x1, Pallas kernels, local(): pl.pallas_call(next_forward(ray_dev), out_shape=(vmem(vox_dev), vmem(vox_...  1 us
  transfers between devices with their start and end apart: 18, of which 12 were waited for; matrix products, arithmetic and copies ran while one was open for 1% of the time, Pallas kernels for 13%

profile of v11, /device:TPU:0, one launch (start us, length us, event | category | flops | bytes accessed | tf_op | source)
XLA Modules:
  0.0 47.4 jit_solution(5968710274343699016)
XLA Ops:
  1.3 3.4 %first_forward.1 = (bf16[128,128,128]{2,1,0:T(8,128)(2,1)S(1)}, s32[1,128]{1,0:T(1,128)S(1)}, s32[1,128]{1,0:T(1,128)S(1)}, f32[64,128]{1,0:T(8,128)S(1)}, f32[3...) custom-call(bf16[128,128,128]{2,1,0:T(8,128)(2,1)} %proj_hbm.3, s32[1,128]{1,0:T(1,128)} %bitcast.4, ...), custom_call_target="tpu_custom_call" | custom-call | tf_op jit(solution)/shard_map/first_forward/pallas_call | solution.py:248
  4.7 0.5 %collective-permute-start.2 = (f32[256,128]{1,0:T(8,128)S(1)}, f32[256,128]{1,0:T(8,128)S(1)}, u32[]{:S(2)}, u32[]{:S(2)}) collective-permute-start(f32[256,128]{1,0:T(8,128)S(1)} %get-tuple-element.33), channel_id=1, source_target_pairs={{0,4},{4,0},{8,12},{12,8},{16,20},{20,16},{24,28},{28,24},{1,5},{5... | collective-permute-start | bytes 393224 | tf_op jit(solution)/shard_map/ppermute | solution.py:207
  5.2 0.8 %name_places.1 = (bf16[128,256]{1,0:T(8,128)(2,1)S(1)}, bf16[256,128]{1,0:T(8,128)(2,1)S(1)}, bf16[128,64]{1,0:T(8,128)(2,1)S(1)}, bf16[64,128]{1,0:T(8,128)(2,1)S(1)}, f32[64,128]{1,0:T(8,128)S(1)}) custom-call(bf16[128,128,128]{2,1,0:T(8,128)(2,1)S(1)} %get-tuple-element.24.proj, s32[1,128]{1,0:T(1,128)S(1)} %get-tuple-element.25.rows, ...), custom_call_target="tpu_custom_call" | custom-call | bytes 1048576 | tf_op jit(solution)/shard_map/name_places/pallas_call | solution.py:266
  6.2 3.9 %collective-permute-start.5 = (f32[256,128]{1,0:T(8,128)S(1)}, f32[256,128]{1,0:T(8,128)S(1)}, u32[]{:S(2)}, u32[]{:S(2)}) collective-permute-start(f32[256,128]{1,0:T(8,128)S(1)} %add.35), channel_id=1, source_target_pairs={{0,24},{4,28},{8,16},{12,20},{16,8},{20,12},{24,0},{28,4},{1,25},{... | collective-permute-start | bytes 393224 | tf_op jit(solution)/shard_map/ppermute | solution.py:207
  10.1 0.5 %collective-permute-start.4 = (f32[256,128]{1,0:T(8,128)S(1)}, f32[256,128]{1,0:T(8,128)S(1)}, u32[]{:S(2)}, u32[]{:S(2)}) collective-permute-start(f32[256,128]{1,0:T(8,128)S(1)} %add.35), channel_id=1, source_target_pairs={{0,16},{4,20},{8,24},{12,28},{16,0},{20,4},{24,8},{28,12},{1,17},{... | collective-permute-start | bytes 393224 | tf_op jit(solution)/shard_map/ppermute | solution.py:207
  10.7 3.0 %collective-permute-start = (f32[64,128]{1,0:T(8,128)S(1)}, f32[64,128]{1,0:T(8,128)S(1)}, u32[]{:S(2)}, u32[]{:S(2)}) collective-permute-start(f32[64,128]{1,0:T(8,128)S(1)} %get-tuple-element.30), channel_id=1, source_target_pairs={{0,2},{1,3},{2,0},{3,1},{4,6},{5,7},{6,4},{7,5},{8,10},{9,11},{10,... | collective-permute-start | bytes 98312 | tf_op jit(solution)/shard_map/ppermute | solution.py:207
  13.7 0.3 collective-permute-done.5
  14.0 2.7 %collective-permute-done.4 = f32[256,128]{1,0:T(8,128)S(1)} collective-permute-done((f32[256,128]{1,0:T(8,128)S(1)}, f32[256,128]{1,0:T(8,128)S(1)}, u32[]{:S(2)}, u32[]{:S(2)}) %collective-permute-start.4) | collective-permute-done | bytes 131104 | tf_op jit(solution)/shard_map/ppermute | solution.py:207
  16.7 0.3 collective-permute-done.3
  17.1 1.6 %collective-permute-start.1 = (f32[64,128]{1,0:T(8,128)S(1)}, f32[64,128]{1,0:T(8,128)S(1)}, u32[]{:S(2)}, u32[]{:S(2)}) collective-permute-start(f32[64,128]{1,0:T(8,128)S(1)} %add.33), channel_id=1, source_target_pairs={{0,1},{1,0},{2,3},{3,2},{4,5},{5,4},{6,7},{7,6},{8,9},{9,8},{10,11... | collective-permute-start | bytes 98312 | tf_op jit(solution)/shard_map/ppermute | solution.py:207
  18.8 0.9 %first_backward.1.own = f32[64,128]{1,0:T(8,128)S(1)} custom-call(bf16[128,128,128]{2,1,0:T(8,128)(2,1)S(1)} %get-tuple-element.24.proj, bf16[128,256]{1,0:T(8,128)(2,1)S(1)} %get-tuple-element.31.picks, bf16[64,128]{1,0:T(8,128)(2,1)S(1)} %get-tuple-element.35.places, bf16[128,128]{1,0:T(8,128)(2,1)S(1)} %fusion.mine, ...), custom_call_target="tpu_custom_call" | custom-call | tf_op jit(solution)/shard_map/first_backward/pallas_call | solution.py:294
  19.7 3.2 %collective-permute-start.9 = (f32[64,128]{1,0:T(8,128)S(1)}, f32[64,128]{1,0:T(8,128)S(1)}, u32[]{:S(2)}, u32[]{:S(2)}) collective-permute-start(f32[64,128]{1,0:T(8,128)S(1)} %first_backward.1.own), channel_id=1, source_target_pairs={{0,3},{1,2},{2,1},{3,0},{4,7},{5,6},{6,5},{7,4},{8,11},{9,10},{10,... | collective-permute-start | bytes 98312 | tf_op jit(solution)/shard_map/ppermute | solution.py:207
  22.9 1.3 %collective-permute-start.7 = (f32[64,128]{1,0:T(8,128)S(1)}, f32[64,128]{1,0:T(8,128)S(1)}, u32[]{:S(2)}, u32[]{:S(2)}) collective-permute-start(f32[64,128]{1,0:T(8,128)S(1)} %first_backward.1.own), channel_id=1, source_target_pairs={{0,1},{1,0},{2,3},{3,2},{4,5},{5,4},{6,7},{7,6},{8,9},{9,8},{10,11... | collective-permute-start | bytes 98312 | tf_op jit(solution)/shard_map/ppermute | solution.py:207
  24.2 1.1 %turn_blocks.1.proj = bf16[128,128,128]{2,1,0:T(8,128)(2,1)S(1)} custom-call(bf16[128,128,128]{2,1,0:T(8,128)(2,1)S(1)} %get-tuple-element.24.proj), custom_call_target="tpu_custom_call" | custom-call | bytes 8388608 | tf_op jit(solution)/shard_map/turn_blocks/pallas_call | solution.py:278
  25.5 2.2 %collective-permute-done.8.mid = f32[64,128]{1,0:T(8,128)S(1)} collective-permute-done((f32[64,128]{1,0:T(8,128)S(1)}, f32[64,128]{1,0:T(8,128)S(1)}, u32[]{:S(2)}, u32[]{:S(2)}) %collective-permute-start.8) | collective-permute-done | bytes 32800 | tf_op jit(solution)/shard_map/ppermute | solution.py:207
  27.7 1.0 %next_forward.1 = (f32[64,128]{1,0:T(8,128)S(1)}, f32[64,128]{1,0:T(8,128)S(1)}, f32[128,128]{1,0:T(8,128)S(1)}, f32[128,128]{1,0:T(8,128)S(1)}) custom-call(bf16[128,128,128]{2,1,0:T(8,128)(2,1)S(1)} %turn_blocks.1.proj, bf16[128,64]{1,0:T(8,128)(2,1)S(1)} %get-tuple-element.27.picks, bf16[256,128]{1,0:T(8,128)(2,1)S(1)} %get-tuple-element.28.places, ...), custom_call_target="tpu_custom_call" | custom-call | tf_op jit(solution)/shard_map/next_forward/pallas_call | solution.py:304
  28.8 1.2 %collective-permute-done.10 = f32[128,128]{1,0:T(8,128)S(1)} collective-permute-done((f32[128,128]{1,0:T(8,128)S(1)}, f32[128,128]{1,0:T(8,128)S(1)}, u32[]{:S(2)}, u32[]{:S(2)}) %collective-permute-start.10) | collective-permute-done | bytes 65568 | tf_op jit(solution)/shard_map/ppermute | solution.py:207
  30.1 1.7 %collective-permute-start.13 = (f32[128,128]{1,0:T(8,128)S(1)}, f32[128,128]{1,0:T(8,128)S(1)}, u32[]{:S(2)}, u32[]{:S(2)}) collective-permute-start(f32[128,128]{1,0:T(8,128)S(1)} %add.39), channel_id=1, source_target_pairs={{0,24},{4,28},{8,16},{12,20},{16,8},{20,12},{24,0},{28,4},{1,25},{... | collective-permute-start | bytes 196616 | tf_op jit(solution)/shard_map/ppermute | solution.py:207
  31.8 1.3 %collective-permute-start.12 = (f32[128,128]{1,0:T(8,128)S(1)}, f32[128,128]{1,0:T(8,128)S(1)}, u32[]{:S(2)}, u32[]{:S(2)}) collective-permute-start(f32[128,128]{1,0:T(8,128)S(1)} %add.39), channel_id=1, source_target_pairs={{0,16},{4,20},{8,24},{12,28},{16,0},{20,4},{24,8},{28,12},{1,17},{... | collective-permute-start | bytes 196616 | tf_op jit(solution)/shard_map/ppermute | solution.py:207
  33.1 0.5 %collective-permute-start.11 = (f32[128,128]{1,0:T(8,128)S(1)}, f32[128,128]{1,0:T(8,128)S(1)}, u32[]{:S(2)}, u32[]{:S(2)}) collective-permute-start(f32[128,128]{1,0:T(8,128)S(1)} %add.39), channel_id=1, source_target_pairs={{0,8},{4,12},{8,0},{12,4},{16,24},{20,28},{24,16},{28,20},{1,9},{5... | collective-permute-start | bytes 196616 | tf_op jit(solution)/shard_map/ppermute | solution.py:207
  33.6 1.9 %fetch_blocks.2.early = bf16[96,128,128]{2,1,0:T(8,128)(2,1)S(1)} custom-call(bf16[128,128,128]{2,1,0:T(8,128)(2,1)} %proj_hbm.3), custom_call_target="tpu_custom_call" | custom-call | bytes 6291456 | tf_op jit(solution)/shard_map/fetch_blocks/pallas_call | solution.py:315
  35.6 1.1 %collective-permute-done.12 = f32[128,128]{1,0:T(8,128)S(1)} collective-permute-done((f32[128,128]{1,0:T(8,128)S(1)}, f32[128,128]{1,0:T(8,128)S(1)}, u32[]{:S(2)}, u32[]{:S(2)}) %collective-permute-start.12) | collective-permute-done | bytes 65568 | tf_op jit(solution)/shard_map/ppermute | solution.py:207
  36.6 0.8 %collective-permute-done.11 = f32[128,128]{1,0:T(8,128)S(1)} collective-permute-done((f32[128,128]{1,0:T(8,128)S(1)}, f32[128,128]{1,0:T(8,128)S(1)}, u32[]{:S(2)}, u32[]{:S(2)}) %collective-permute-start.11) | collective-permute-done | bytes 65568 | tf_op jit(solution)/shard_map/ppermute | solution.py:207
  37.5 1.2 %fetch_blocks.3.late = bf16[32,128,128]{2,1,0:T(8,128)(2,1)S(1)} custom-call(bf16[128,128,128]{2,1,0:T(8,128)(2,1)} %proj_hbm.3), custom_call_target="tpu_custom_call" | custom-call | bytes 2097152 | tf_op jit(solution)/shard_map/fetch_blocks/pallas_call | solution.py:315
  38.8 0.9 %last_backward.1.corr = f32[64,128]{1,0:T(8,128)S(1)} custom-call(bf16[96,128,128]{2,1,0:T(8,128)(2,1)S(1)} %fetch_blocks.2.early, bf16[32,128,128]{2,1,0:T(8,128)(2,1)S(1)} %fetch_blocks.3.late, bf16[128,256]{1,0:T(8,128)(2,1)S(1)} %get-tuple-element.31.picks, bf16[64,128]{1,0:T(8,128)(2,1)S(1)} %get-tuple-element.35.places, ...), custom_call_target="tpu_custom_call" | custom-call | tf_op jit(solution)/shard_map/last_backward/pallas_call | solution.py:334
  39.7 1.6 %collective-permute-start.17 = (f32[64,128]{1,0:T(8,128)S(1)}, f32[64,128]{1,0:T(8,128)S(1)}, u32[]{:S(2)}, u32[]{:S(2)}) collective-permute-start(f32[64,128]{1,0:T(8,128)S(1)} %last_backward.1.corr), channel_id=1, source_target_pairs={{0,3},{1,2},{2,1},{3,0},{4,7},{5,6},{6,5},{7,4},{8,11},{9,10},{10,... | collective-permute-start | bytes 98312 | tf_op jit(solution)/shard_map/ppermute | solution.py:207
  41.4 0.5 %collective-permute-start.16 = (f32[64,128]{1,0:T(8,128)S(1)}, f32[64,128]{1,0:T(8,128)S(1)}, u32[]{:S(2)}, u32[]{:S(2)}) collective-permute-start(f32[64,128]{1,0:T(8,128)S(1)} %last_backward.1.corr), channel_id=1, source_target_pairs={{0,2},{1,3},{2,0},{3,1},{4,6},{5,7},{6,4},{7,5},{8,10},{9,11},{10,... | collective-permute-start | bytes 98312 | tf_op jit(solution)/shard_map/ppermute | solution.py:207
  41.9 2.3 %collective-permute-start.15 = (f32[64,128]{1,0:T(8,128)S(1)}, f32[64,128]{1,0:T(8,128)S(1)}, u32[]{:S(2)}, u32[]{:S(2)}) collective-permute-start(f32[64,128]{1,0:T(8,128)S(1)} %last_backward.1.corr), channel_id=1, source_target_pairs={{0,1},{1,0},{2,3},{3,2},{4,5},{5,4},{6,7},{7,6},{8,9},{9,8},{10,11... | collective-permute-start | bytes 98312 | tf_op jit(solution)/shard_map/ppermute | solution.py:207
  44.2 0.6 %constant_dynamic-slice_fusion = f32[32,128]{1,0:T(8,128)} fusion(f32[128,128]{1,0:T(8,128)S(1)} %get-tuple-element.47, s32[]{:T(128)S(6)} %select_n.3), kind=kLoop, calls=%fused_computation.7 | loop fusion | bytes 32772 | tf_op jit(solution)/shard_map/dynamic_slice | solution.py:332
  44.8 0.9 %collective-permute-done.17.far = f32[64,128]{1,0:T(8,128)S(1)} collective-permute-done((f32[64,128]{1,0:T(8,128)S(1)}, f32[64,128]{1,0:T(8,128)S(1)}, u32[]{:S(2)}, u32[]{:S(2)}) %collective-permute-start.17) | collective-permute-done | bytes 32800 | tf_op jit(solution)/shard_map/ppermute | solution.py:207
  45.7 1.0 %collective-permute-done.16.mid = f32[64,128]{1,0:T(8,128)S(1)} collective-permute-done((f32[64,128]{1,0:T(8,128)S(1)}, f32[64,128]{1,0:T(8,128)S(1)}, u32[]{:S(2)}, u32[]{:S(2)}) %collective-permute-start.16) | collective-permute-done | bytes 32800 | tf_op jit(solution)/shard_map/ppermute | solution.py:207
  46.8 0.6 %last_update.1 = f32[64,128]{1,0:T(8,128)} custom-call(f32[64,128]{1,0:T(8,128)S(1)} %get-tuple-element.38.volume, f32[64,128]{1,0:T(8,128)S(1)} %get-tuple-element.39.weight, f32[64,128]{1,0:T(8,128)S(1)} %last_backward.1.corr, f32[64,128]{1,0:T(8,128)S(1)} %collective-permute-done.15.near, f32[64,128]{1,0:T(8,128)S(1)} %collective-permute-done.16.mid, ...), custom_call_target="tpu_custom_call" | custom-call | tf_op jit(solution)/shard_map/last_update/pallas_call | solution.py:342
  (22 shorter events, 1.0 us)
Async XLA Ops:
  4.7 1.5 %collective-permute-start.2 = (f32[256,128]{1,0:T(8,128)S(1)}, f32[256,128]{1,0:T(8,128)S(1)}, u32[]{:S(2)}, u32[]{:S(2)}) collective-permute-start(f32[256,128]{1,0:T(8,128)S(1)} %get-tuple-element.33), channel_id=1, source_target_pairs={{0,4},{4,0},{8,12},{12,8},{16,20},{20,16},{24,28},{28,24},{1,5},{5... | collective-permute-start | bytes 393224 | tf_op jit(solution)/shard_map/ppermute | solution.py:207
  6.2 7.8 %collective-permute-start.5 = (f32[256,128]{1,0:T(8,128)S(1)}, f32[256,128]{1,0:T(8,128)S(1)}, u32[]{:S(2)}, u32[]{:S(2)}) collective-permute-start(f32[256,128]{1,0:T(8,128)S(1)} %add.35), channel_id=1, source_target_pairs={{0,24},{4,28},{8,16},{12,20},{16,8},{20,12},{24,0},{28,4},{1,25},{... | collective-permute-start | bytes 393224 | tf_op jit(solution)/shard_map/ppermute | solution.py:207
  10.1 6.6 %collective-permute-start.4 = (f32[256,128]{1,0:T(8,128)S(1)}, f32[256,128]{1,0:T(8,128)S(1)}, u32[]{:S(2)}, u32[]{:S(2)}) collective-permute-start(f32[256,128]{1,0:T(8,128)S(1)} %add.35), channel_id=1, source_target_pairs={{0,16},{4,20},{8,24},{12,28},{16,0},{20,4},{24,8},{28,12},{1,17},{... | collective-permute-start | bytes 393224 | tf_op jit(solution)/shard_map/ppermute | solution.py:207
  10.6 6.4 %collective-permute-start.3 = (f32[256,128]{1,0:T(8,128)S(1)}, f32[256,128]{1,0:T(8,128)S(1)}, u32[]{:S(2)}, u32[]{:S(2)}) collective-permute-start(f32[256,128]{1,0:T(8,128)S(1)} %add.35), channel_id=1, source_target_pairs={{0,8},{4,12},{8,0},{12,4},{16,24},{20,28},{24,16},{28,20},{1,9},{5... | collective-permute-start | bytes 393224 | tf_op jit(solution)/shard_map/ppermute | solution.py:207
  10.7 6.4 %collective-permute-start = (f32[64,128]{1,0:T(8,128)S(1)}, f32[64,128]{1,0:T(8,128)S(1)}, u32[]{:S(2)}, u32[]{:S(2)}) collective-permute-start(f32[64,128]{1,0:T(8,128)S(1)} %get-tuple-element.30), channel_id=1, source_target_pairs={{0,2},{1,3},{2,0},{3,1},{4,6},{5,7},{6,4},{7,5},{8,10},{9,11},{10,... | collective-permute-start | bytes 98312 | tf_op jit(solution)/shard_map/ppermute | solution.py:207
  17.0 1.7 %collective-permute-start.6 = (bf16[128,128]{1,0:T(8,128)(2,1)S(1)}, bf16[128,128]{1,0:T(8,128)(2,1)S(1)}, u32[]{:S(2)}, u32[]{:S(2)}) collective-permute-start(bf16[128,128]{1,0:T(8,128)(2,1)S(1)} %fusion.mine), channel_id=1, source_target_pairs={{0,4},{4,0},{8,12},{12,8},{16,20},{20,16},{24,28},{28,24},{1,5},{5... | collective-permute-start | bytes 98312 | tf_op jit(solution)/shard_map/ppermute | solution.py:207
  17.1 8.2 %collective-permute-start.1 = (f32[64,128]{1,0:T(8,128)S(1)}, f32[64,128]{1,0:T(8,128)S(1)}, u32[]{:S(2)}, u32[]{:S(2)}) collective-permute-start(f32[64,128]{1,0:T(8,128)S(1)} %add.33), channel_id=1, source_target_pairs={{0,1},{1,0},{2,3},{3,2},{4,5},{5,4},{6,7},{7,6},{8,9},{9,8},{10,11... | collective-permute-start | bytes 98312 | tf_op jit(solution)/shard_map/ppermute | solution.py:207
  19.7 5.8 %collective-permute-start.9 = (f32[64,128]{1,0:T(8,128)S(1)}, f32[64,128]{1,0:T(8,128)S(1)}, u32[]{:S(2)}, u32[]{:S(2)}) collective-permute-start(f32[64,128]{1,0:T(8,128)S(1)} %first_backward.1.own), channel_id=1, source_target_pairs={{0,3},{1,2},{2,1},{3,0},{4,7},{5,6},{6,5},{7,4},{8,11},{9,10},{10,... | collective-permute-start | bytes 98312 | tf_op jit(solution)/shard_map/ppermute | solution.py:207
  22.9 4.8 %collective-permute-start.8 = (f32[64,128]{1,0:T(8,128)S(1)}, f32[64,128]{1,0:T(8,128)S(1)}, u32[]{:S(2)}, u32[]{:S(2)}) collective-permute-start(f32[64,128]{1,0:T(8,128)S(1)} %first_backward.1.own), channel_id=1, source_target_pairs={{0,2},{1,3},{2,0},{3,1},{4,6},{5,7},{6,4},{7,5},{8,10},{9,11},{10,... | collective-permute-start | bytes 98312 | tf_op jit(solution)/shard_map/ppermute | solution.py:207
  22.9 4.8 %collective-permute-start.7 = (f32[64,128]{1,0:T(8,128)S(1)}, f32[64,128]{1,0:T(8,128)S(1)}, u32[]{:S(2)}, u32[]{:S(2)}) collective-permute-start(f32[64,128]{1,0:T(8,128)S(1)} %first_backward.1.own), channel_id=1, source_target_pairs={{0,1},{1,0},{2,3},{3,2},{4,5},{5,4},{6,7},{7,6},{8,9},{9,8},{10,11... | collective-permute-start | bytes 98312 | tf_op jit(solution)/shard_map/ppermute | solution.py:207
  28.8 1.3 %collective-permute-start.10 = (f32[128,128]{1,0:T(8,128)S(1)}, f32[128,128]{1,0:T(8,128)S(1)}, u32[]{:S(2)}, u32[]{:S(2)}) collective-permute-start(f32[128,128]{1,0:T(8,128)S(1)} %get-tuple-element.41), channel_id=1, source_target_pairs={{0,4},{4,0},{8,12},{12,8},{16,20},{20,16},{24,28},{28,24},{1,5},{5... | collective-permute-start | bytes 196616 | tf_op jit(solution)/shard_map/ppermute | solution.py:207
  30.1 5.5 %collective-permute-start.13 = (f32[128,128]{1,0:T(8,128)S(1)}, f32[128,128]{1,0:T(8,128)S(1)}, u32[]{:S(2)}, u32[]{:S(2)}) collective-permute-start(f32[128,128]{1,0:T(8,128)S(1)} %add.39), channel_id=1, source_target_pairs={{0,24},{4,28},{8,16},{12,20},{16,8},{20,12},{24,0},{28,4},{1,25},{... | collective-permute-start | bytes 196616 | tf_op jit(solution)/shard_map/ppermute | solution.py:207
  31.8 4.8 %collective-permute-start.12 = (f32[128,128]{1,0:T(8,128)S(1)}, f32[128,128]{1,0:T(8,128)S(1)}, u32[]{:S(2)}, u32[]{:S(2)}) collective-permute-start(f32[128,128]{1,0:T(8,128)S(1)} %add.39), channel_id=1, source_target_pairs={{0,16},{4,20},{8,24},{12,28},{16,0},{20,4},{24,8},{28,12},{1,17},{... | collective-permute-start | bytes 196616 | tf_op jit(solution)/shard_map/ppermute | solution.py:207
  33.1 4.3 %collective-permute-start.11 = (f32[128,128]{1,0:T(8,128)S(1)}, f32[128,128]{1,0:T(8,128)S(1)}, u32[]{:S(2)}, u32[]{:S(2)}) collective-permute-start(f32[128,128]{1,0:T(8,128)S(1)} %add.39), channel_id=1, source_target_pairs={{0,8},{4,12},{8,0},{12,4},{16,24},{20,28},{24,16},{28,20},{1,9},{5... | collective-permute-start | bytes 196616 | tf_op jit(solution)/shard_map/ppermute | solution.py:207
  37.4 1.3 %collective-permute-start.14 = (bf16[128,128]{1,0:T(8,128)(2,1)S(1)}, bf16[128,128]{1,0:T(8,128)(2,1)S(1)}, u32[]{:S(2)}, u32[]{:S(2)}) collective-permute-start(bf16[128,128]{1,0:T(8,128)(2,1)S(1)} %get-tuple-element.46.mine), channel_id=1, source_target_pairs={{0,4},{4,0},{8,12},{12,8},{16,20},{20,16},{24,28},{28,24},{1,5},{5... | collective-permute-start | bytes 98312 | tf_op jit(solution)/shard_map/ppermute | solution.py:207
  39.7 5.9 %collective-permute-start.17 = (f32[64,128]{1,0:T(8,128)S(1)}, f32[64,128]{1,0:T(8,128)S(1)}, u32[]{:S(2)}, u32[]{:S(2)}) collective-permute-start(f32[64,128]{1,0:T(8,128)S(1)} %last_backward.1.corr), channel_id=1, source_target_pairs={{0,3},{1,2},{2,1},{3,0},{4,7},{5,6},{6,5},{7,4},{8,11},{9,10},{10,... | collective-permute-start | bytes 98312 | tf_op jit(solution)/shard_map/ppermute | solution.py:207
  41.4 5.3 %collective-permute-start.16 = (f32[64,128]{1,0:T(8,128)S(1)}, f32[64,128]{1,0:T(8,128)S(1)}, u32[]{:S(2)}, u32[]{:S(2)}) collective-permute-start(f32[64,128]{1,0:T(8,128)S(1)} %last_backward.1.corr), channel_id=1, source_target_pairs={{0,2},{1,3},{2,0},{3,1},{4,6},{5,7},{6,4},{7,5},{8,10},{9,11},{10,... | collective-permute-start | bytes 98312 | tf_op jit(solution)/shard_map/ppermute | solution.py:207
  41.9 4.9 %collective-permute-start.15 = (f32[64,128]{1,0:T(8,128)S(1)}, f32[64,128]{1,0:T(8,128)S(1)}, u32[]{:S(2)}, u32[]{:S(2)}) collective-permute-start(f32[64,128]{1,0:T(8,128)S(1)} %last_backward.1.corr), channel_id=1, source_target_pairs={{0,1},{1,0},{2,3},{3,2},{4,5},{5,4},{6,7},{7,6},{8,9},{9,8},{10,11... | collective-permute-start | bytes 98312 | tf_op jit(solution)/shard_map/ppermute | solution.py:207
